TPU v7x, 256 devices: a whole 4x4x8 slice. The times are simulated.
256 devices in a mesh: beam: 32 (over z, y), slab: 8 (over x, core).
Axes of the slice: x: 4, y: 4, z: 8, core: 2. Of those that a mesh axis runs over, the one named last changes fastest.
Arguments:
- pot_first: bfloat16 [4096, 4096], P('beam'), may hold values from -3.140625 to 3.140625
- pot_second: bfloat16 [4096, 4096], P('beam'), may hold values from -3.140625 to 3.140625
- beam_index: int32 [8, 2], replicated, may hold values from -3 to 3
- aberration: float32 [8], replicated, may hold values from -3.140625 to 3.140625
- tile_table: int32 [256, 4], replicated, may hold values from 0 to 4095, as said below
- tile_count: int32 [256], replicated, may hold values from 1 to 4, as said below
Outputs:
- detector_sums: float32 [256, 4, 3, 16], P(('beam', 'slab'))
Inputs may be any that keep to these rules, and one draw needn't show every extreme that they name: `tile_table`: group the blocks by the beam index of their device, block // 8; among the 32 slots of one group, active or not, exactly 1 name a tile of row band b, for every band b = ty // 2. The first tile_count[block] slots of a block are active; some block has all 4 active.
All inputs are finite; a program needn't handle non-finite values.
Results may differ from a plain program's by a relative error of at most 0.012.
The roundings to bfloat16 on the way count: a program that leaves them out, or rounds other values in their place, can miss the bound.
Values may be sent and summed in bfloat16 or wider, within the bound.
A program may use at most 128 MiB of HBM per device.

v0:
```python
import math

import jax
import jax.numpy as jnp
from jax import lax
from jax.sharding import PartitionSpec as P

A = 64
N = 4096
F = 64
G = 3
NDET = 16


def rounded(values):
    return lax.optimization_barrier(values.astype(jnp.bfloat16)).astype(jnp.float32)


def radix_tables(factor):
    digits = jnp.arange(A, dtype=jnp.int32)
    product = digits[:, None] * digits[None, :] % A
    angles = 2.0 * math.pi / A * product.astype(jnp.float32)
    return (rounded(jnp.cos(angles)) * factor, rounded(jnp.sin(angles)) * factor)


def radix_block(orient, factor):
    cosine, sine_tab = radix_tables(factor)
    upper_half = jnp.concatenate([cosine, -orient * sine_tab], axis=1)
    lower_half = jnp.concatenate([orient * sine_tab, cosine], axis=1)
    return jnp.concatenate([upper_half, lower_half], axis=0).astype(jnp.bfloat16)


def paired_block():
    cosine, sine_tab = radix_tables(1.0 / A)
    blocks = jnp.stack(
        [jnp.stack([cosine, -sine_tab], axis=-1), jnp.stack([sine_tab, cosine], axis=-1)], axis=1
    )
    return blocks.reshape(2 * A, 2 * A).astype(jnp.bfloat16)


def twist_table(orient):
    digits = jnp.arange(A, dtype=jnp.int32)
    product = digits[:, None] * digits[None, :] % N
    angles = 2.0 * math.pi / N * product.astype(jnp.float32)
    return (jnp.cos(angles), orient * jnp.sin(angles))


def apply_twist(values, cosine, turned, part_axis):
    real_part = jnp.take(values, 0, axis=part_axis)
    imag_part = jnp.take(values, 1, axis=part_axis)
    stacked = jnp.stack(
        [real_part * cosine + imag_part * turned, imag_part * cosine - real_part * turned],
        axis=part_axis,
    )
    return stacked.astype(jnp.bfloat16)


def radix_section(values, table):
    flat = values.reshape(-1, table.shape[0])
    return jnp.dot(flat, table, preferred_element_type=jnp.float32).reshape(values.shape)


def coefficients(tile_ids, beam_rows, shifts):
    across = N // A
    offsets = jnp.arange(G, dtype=jnp.int32)
    spot_y = (tile_ids // across)[:, None] * A + A // 2 + offsets[None, :]
    spot_x = (tile_ids % across)[:, None] * A + A // 2 + 2 * offsets[None, :]
    wave_y = jnp.remainder(F * beam_rows[:, 0], N)[:, None, None]
    wave_x = jnp.remainder(F * beam_rows[:, 1], N)[:, None, None]
    windings = (wave_y * spot_y[None] % N + wave_x * spot_x[None] % N) % N
    phases = shifts[:, None, None] + 2.0 * math.pi / N * windings.astype(jnp.float32)
    return (jnp.cos(phases), -jnp.sin(phases))


def detector_weights(beam_total):
    digits = jnp.arange(A, dtype=jnp.int32)
    signed = jnp.where(digits < A // 2, digits, digits - A)
    radius = (signed[:, None] ** 2 + signed[None, :] ** 2).reshape(A * A)
    step_width = A // (2 * NDET)
    bin_index = jnp.arange(NDET, dtype=jnp.int32)
    member = (radius[:, None] >= (step_width * bin_index[None, :]) ** 2) & (
        radius[:, None] < (step_width * (bin_index[None, :] + 1)) ** 2
    )
    counts = jnp.sum(member.astype(jnp.float32), axis=0)
    return jnp.where(member, A * A / (beam_total * counts), 0.0)


def phase_pair(values):
    angles = -math.pi / N * (values % (2 * N)).astype(jnp.float32)
    return (jnp.cos(angles), jnp.sin(angles))


def shards(pot_first, pot_second, beam_index, aberration, tile_table, tile_count):
    field_count = lax.axis_size("beam")
    hold_count = lax.axis_size("slab")
    field_pos = lax.axis_index("beam")
    hold_pos = lax.axis_index("slab")
    band_rows = pot_first.shape[0]
    band_tiles = band_rows // A
    width_k = A // field_count
    across = N // A
    beam_total = beam_index.shape[0]
    local_count = beam_total // hold_count
    forward_tab = radix_block(1.0, 1.0 / A)
    inverse_tab = radix_block(-1.0, 1.0)
    fwd_cos, fwd_turn = twist_table(1.0)
    inv_cos, inv_turn = twist_table(-1.0)
    digits = jnp.arange(A, dtype=jnp.int32)
    row_ids = field_pos * band_rows + jnp.arange(band_rows, dtype=jnp.int32)
    columns = A * digits[None, :] + digits[:, None]
    first_pot = pot_first.astype(jnp.float32).reshape(band_rows, A, A).transpose(0, 2, 1)
    second_pot = pot_second.astype(jnp.float32).reshape(band_rows, A, A)
    freq_y = digits[:, None] + A * digits[None, :]
    freq_x = (
        field_pos * width_k + jnp.arange(width_k, dtype=jnp.int32)[:, None] + A * digits[None, :]
    )
    square_y = jnp.where(freq_y < N // 2, freq_y, freq_y - N) ** 2
    square_x = jnp.where(freq_x < N // 2, freq_x, freq_x - N) ** 2
    cos_y, sin_y = phase_pair(square_y)
    cos_x, sin_x = phase_pair(square_x)
    beam_row = lax.dynamic_index_in_dim(beam_index, hold_pos * local_count + 0, 0, keepdims=False)
    wave_y = jnp.remainder(F * beam_row[0], N)
    wave_x = jnp.remainder(F * beam_row[1], N)
    row_angles = 2.0 * math.pi / N * (wave_y * row_ids % N).astype(jnp.float32)
    col_angles = 2.0 * math.pi / N * (wave_x * columns % N).astype(jnp.float32)
    row_cos = jnp.cos(row_angles)[:, None, None]
    row_sin = jnp.sin(row_angles)[:, None, None]
    col_cos = jnp.cos(col_angles)[None]
    col_sin = jnp.sin(col_angles)[None]
    plane_cos = row_cos * col_cos - row_sin * col_sin
    plane_sin = row_sin * col_cos + row_cos * col_sin
    first_cos = jnp.cos(first_pot)
    first_sin = jnp.sin(first_pot)
    incident = jnp.stack(
        [
            plane_cos * first_cos - plane_sin * first_sin,
            plane_cos * first_sin + plane_sin * first_cos,
        ],
        axis=2,
    ).astype(jnp.bfloat16)
    sectioned = radix_section(incident.reshape(band_rows, A, 2 * A), forward_tab).reshape(
        band_rows, A, 2, A
    )
    sectioned = apply_twist(sectioned, fwd_cos, fwd_turn, 2)
    sectioned = sectioned.transpose(0, 3, 2, 1).reshape(band_rows, A, 2 * A)
    spectrum = radix_section(sectioned, forward_tab).astype(jnp.bfloat16)
    columns_all = lax.all_to_all(spectrum, "beam", split_axis=1, concat_axis=0, tiled=True)
    sectioned = (
        columns_all.reshape(A, A, width_k, 2, A)
        .transpose(1, 2, 4, 3, 0)
        .reshape(A, width_k, A, 2 * A)
    )
    sectioned = radix_section(sectioned, forward_tab).reshape(A, width_k, A, 2, A)
    sectioned = apply_twist(sectioned, fwd_cos[:, None, None, :], fwd_turn[:, None, None, :], 3)
    sectioned = sectioned.transpose(4, 1, 2, 3, 0).reshape(A, width_k, A, 2 * A)
    spectrum = radix_section(sectioned, forward_tab).reshape(A, width_k, A, 2, A)
    spec_real = spectrum[:, :, :, 0, :]
    spec_imag = spectrum[:, :, :, 1, :]
    inside = square_x[None, :, :, None] + square_y[:, None, None, :] <= (N // 3) ** 2
    prop_cos = jnp.where(
        inside,
        cos_x[None, :, :, None] * cos_y[:, None, None, :]
        - sin_x[None, :, :, None] * sin_y[:, None, None, :],
        0.0,
    )
    prop_sin = jnp.where(
        inside,
        sin_x[None, :, :, None] * cos_y[:, None, None, :]
        + cos_x[None, :, :, None] * sin_y[:, None, None, :],
        0.0,
    )
    shifted = jnp.stack(
        [spec_real * prop_cos - spec_imag * prop_sin, spec_real * prop_sin + spec_imag * prop_cos],
        axis=3,
    ).astype(jnp.bfloat16)
    sectioned = radix_section(shifted.reshape(A, width_k, A, 2 * A), inverse_tab).reshape(
        A, width_k, A, 2, A
    )
    sectioned = apply_twist(sectioned, inv_cos[:, None, None, :], inv_turn[:, None, None, :], 3)
    sectioned = sectioned.transpose(4, 1, 2, 3, 0).reshape(A, width_k, A, 2 * A)
    sectioned = (
        radix_section(sectioned, inverse_tab).reshape(A, width_k, A, 2, A).astype(jnp.bfloat16)
    )
    sectioned = sectioned.transpose(4, 0, 1, 3, 2).reshape(N, width_k, 2 * A)
    rows_back = lax.all_to_all(sectioned, "beam", split_axis=0, concat_axis=1, tiled=True)
    sectioned = radix_section(rows_back, inverse_tab).reshape(band_rows, A, 2, A)
    sectioned = apply_twist(sectioned, inv_cos, inv_turn, 2)
    sectioned = sectioned.transpose(0, 3, 2, 1).reshape(band_rows, A, 2 * A)
    field_wave = (
        radix_section(sectioned, inverse_tab).reshape(band_rows, A, 2, A).transpose(0, 3, 1, 2)
    )
    second_cos = jnp.cos(second_pot)
    second_sin = jnp.sin(second_pot)
    exit_real = field_wave[..., 0] * second_cos - field_wave[..., 1] * second_sin
    exit_imag = field_wave[..., 0] * second_sin + field_wave[..., 1] * second_cos
    exit_list = [jnp.stack([exit_real, exit_imag], axis=-1).reshape(band_tiles, A, A, 2 * A)]
    exit_all = jnp.stack(exit_list, axis=0)
    blocks_dev = tile_table.shape[0] // (field_count * hold_count)
    slot_count = tile_table.shape[1]
    share_slots = blocks_dev * slot_count
    length = hold_count * share_slots
    capacity = length // field_count
    owner_lists = tile_table.reshape(field_count, length)
    owner_band = owner_lists // across // band_tiles
    matched = (owner_band == field_pos).astype(jnp.int32)
    rank_all = jnp.cumsum(matched, axis=1) - 1
    picked = (matched[:, None, :] == 1) & (
        rank_all[:, None, :] == jnp.arange(capacity, dtype=jnp.int32)[None, :, None]
    )
    chosen = jnp.sum(jnp.where(picked, owner_lists[:, None, :], 0), axis=2)
    outgoing = exit_all[:, chosen // across - field_pos * band_tiles, :, chosen % across, :]
    received = lax.all_to_all(
        outgoing.astype(jnp.bfloat16), "beam", split_axis=0, concat_axis=0, tiled=True
    ).astype(outgoing.dtype)
    own_list = lax.dynamic_index_in_dim(owner_lists, field_pos, 0, keepdims=False)
    own_band = own_list // across // band_tiles
    band_ids = jnp.arange(field_count, dtype=jnp.int32)
    member = own_band[None, :] == band_ids[:, None]
    own_rank = jnp.sum(
        jnp.where(member, jnp.cumsum(member.astype(jnp.int32), axis=1) - 1, 0), axis=0
    )
    tiles_own = received.reshape(field_count * capacity, local_count, A, 2 * A)[
        own_band * capacity + own_rank
    ]
    highest = lax.Precision.HIGHEST
    local_rows = lax.dynamic_slice_in_dim(beam_index, hold_pos * local_count, local_count, 0)
    local_shift = lax.dynamic_slice_in_dim(aberration, hold_pos * local_count, local_count, 0)
    coef_cos, coef_sin = coefficients(own_list, local_rows, local_shift)
    tile_parts = tiles_own.reshape(length, local_count, A, A, 2)
    tile_real = tile_parts[..., 0]
    tile_imag = tile_parts[..., 1]
    pattern = "blg,lbyx->lgyx"
    partial_real = jnp.einsum(pattern, coef_cos, tile_real, precision=highest) - jnp.einsum(
        pattern, coef_sin, tile_imag, precision=highest
    )
    partial_imag = jnp.einsum(pattern, coef_cos, tile_imag, precision=highest) + jnp.einsum(
        pattern, coef_sin, tile_real, precision=highest
    )
    partial_value = jnp.stack([partial_real, partial_imag], axis=-1).reshape(length, G, A, 2 * A)
    probes = lax.psum_scatter(
        partial_value.astype(jnp.bfloat16), "slab", scatter_dimension=0, tiled=True
    )
    paired = paired_block()
    spectrum = radix_section(probes, paired).astype(jnp.bfloat16)
    spectrum = (
        spectrum.reshape(share_slots, G, A, A, 2)
        .transpose(0, 1, 3, 2, 4)
        .reshape(share_slots, G, A, 2 * A)
    )
    spectrum = radix_section(spectrum, paired).reshape(share_slots * G, A * A, 2)
    intensity = spectrum[..., 0] ** 2 + spectrum[..., 1] ** 2
    weights = detector_weights(beam_total)
    binned = jnp.dot(intensity, weights, precision=highest).reshape(blocks_dev, slot_count, G, NDET)
    first_block = (field_pos * hold_count + hold_pos) * blocks_dev
    counts = lax.dynamic_slice_in_dim(tile_count, first_block, blocks_dev, 0)
    active = jnp.arange(slot_count, dtype=jnp.int32)[None, :] < counts[:, None]
    return jnp.where(active[:, :, None, None], binned, 0.0)


def solution(mesh):
    return jax.shard_map(
        shards,
        mesh=mesh,
        in_specs=(P("beam", None), P("beam", None), P(), P(), P(), P()),
        out_specs=P(("beam", "slab"), None, None, None),
        check_vma=False,
    )
```

profile of v0, /device:TPU:8, one launch (start us, length us, event | category | flops | bytes accessed | tf_op | source)
XLA Modules:
  0.0 402.1 jit_solution(16738210480739177099)
XLA Ops:
  10.2 1.6 copy.158
  11.8 8.2 %convert_sine_fusion.1 = (f32[128,4096]{0,1:T(8,128)S(1)}, f32[128,4096]{0,1:T(8,128)}) fusion(bf16[128,4096]{0,1:T(8,128)(2,1)S(1)} %copy.158), kind=kLoop, calls=%fused_computation.29 | loop fusion | flops 524288 | bytes 5242880 | tf_op jit(solution)/shard_map/sin | solution.py:133
  20.2 3.3 fusion.23
  23.7 1.6 fusion.9
  25.4 1.4 fusion.19
  27.0 3.9 fusion.13
  30.8 12.0 %all-to-all-start = ((bf16[128,64,128]{2,0,1:T(8,128)(2,1)}), bf16[128,64,128]{2,0,1:T(8,128)(2,1)S(1)}, u32[]{:S(2)}, u32[]{:S(2)}) async-start(bf16[128,64,128]{2,0,1:T(8,128)(2,1)} %fusion.13), calls=%async_computation | async-start | bytes 4194304 | tf_op jit(solution)/shard_map/all_to_all | solution.py:147
  43.5 48.5 %all-to-all-done = bf16[128,64,128]{2,0,1:T(8,128)(2,1)S(1)} async-done(((bf16[128,64,128]{2,0,1:T(8,128)(2,1)}), bf16[128,64,128]{2,0,1:T(8,128)(2,1)S(1)}, u32[]{:S(2)}, u32[]{:S(2)}) %all-to-all-start) | async-done | bytes 2097184 | tf_op jit(solution)/shard_map/all_to_all | solution.py:147
  92.0 1.3 copy-done.3
  93.3 3.5 copy.166
  96.8 3.3 reshape.1196
  100.1 11.8 %copy.167 = bf16[64,2,64,2,64]{4,3,2,1,0:T(2,128)(2,1)} copy(bf16[64,2,64,2,64]{0,4,2,3,1:T(8,128)(2,1)} %bitcast.304) | data formatting | bytes 4194304 | tf_op jit(solution)/shard_map/transpose | solution.py:150
  111.9 6.8 %reshape.1367 = bf16[64,2,64,128,1]{3,2,1,0,4:T(8,128)(2,1)S(1)} reshape(bf16[64,2,64,2,64]{4,3,2,1,0:T(2,128)(2,1)} %copy.167) | data formatting | bytes 4194304 | tf_op jit(solution)/shard_map/dot_general | solution.py:60
  118.6 1.3 fusion.7
  119.9 1.3 fusion.2
  121.3 2.9 pad_maximum_fusion
  124.2 7.8 %copy.203 = bf16[64,2,64,128,1]{3,2,4,1,0:T(8,128)(2,1)S(1)} copy(bf16[64,2,64,128,1]{0,2,1,3,4:T(8,128)(2,1)} %bitcast.302) | data formatting | bytes 4194304 | tf_op jit(solution)/shard_map/dot_general | solution.py:60
  132.0 1.3 fusion.101
  133.2 3.2 subtract_convert_fusion.1
  137.3 10.4 %copy.170 = bf16[64,2,64,2,64]{4,3,2,1,0:T(2,128)(2,1)} copy(bf16[64,2,64,2,64]{4,2,3,1,0:T(8,128)(2,1)S(1)} %pad_maximum_fusion.1) | data formatting | bytes 4194304 | tf_op jit(solution)/shard_map/stack | solution.py:172
  147.7 7.0 %reshape.1370 = bf16[64,2,64,128,1]{3,2,1,0,4:T(8,128)(2,1)S(1)} reshape(bf16[64,2,64,2,64]{4,3,2,1,0:T(2,128)(2,1)} %copy.170) | data formatting | bytes 4194304 | tf_op jit(solution)/shard_map/convert_element_type | solution.py:175
  154.6 1.3 fusion.102
  155.9 1.3 fusion.4
  157.2 2.9 pad_maximum_fusion.2
  160.1 7.8 %copy.206 = bf16[64,2,64,128,1]{3,2,4,1,0:T(8,128)(2,1)S(1)} copy(bf16[64,2,64,128,1]{0,2,1,3,4:T(8,128)(2,1)} %bitcast.303) | data formatting | bytes 4194304 | tf_op jit(solution)/shard_map/dot_general | solution.py:60
  167.9 3.3 convert_bitcast_fusion
  171.2 11.7 %copy.221 = bf16[64,64,2,2,64]{4,3,2,1,0:T(2,128)(2,1)} copy(bf16[64,64,2,2,64]{0,4,3,2,1:T(8,128)(2,1)} %convert_bitcast_fusion) | data formatting | bytes 4194304 | tf_op jit(solution)/shard_map/reshape | solution.py:184
  182.9 9.6 %reshape.1380 = bf16[4096,2,128]{2,1,0:T(2,128)(2,1)} reshape(bf16[64,64,2,2,64]{4,3,2,1,0:T(2,128)(2,1)} %copy.221) | data formatting | bytes 4194304 | tf_op jit(solution)/shard_map/reshape | solution.py:184
  192.6 7.5 %all-to-all-start.1 = ((bf16[4096,2,128]{2,1,0:T(2,128)(2,1)}), bf16[4096,2,128]{2,1,0:T(2,128)(2,1)}, u32[]{:S(2)}, u32[]{:S(2)}) async-start(bf16[4096,2,128]{2,1,0:T(2,128)(2,1)} %reshape.1380), calls=%async_computation.1 | async-start | bytes 4194304 | tf_op jit(solution)/shard_map/all_to_all | solution.py:185
  201.5 8.1 %convert_cosine_fusion = (f32[128,4096]{0,1:T(8,128)S(1)}, f32[128,4096]{0,1:T(8,128)}) fusion(bf16[128,4096]{0,1:T(8,128)(2,1)S(1)} %copy.182), kind=kLoop, calls=%fused_computation.28 | loop fusion | flops 524288 | bytes 5242880 | tf_op jit(solution)/shard_map/cos | solution.py:192
  209.7 38.8 %all-to-all-done.1 = bf16[4096,2,128]{2,1,0:T(2,128)(2,1)} async-done(((bf16[4096,2,128]{2,1,0:T(2,128)(2,1)}), bf16[4096,2,128]{2,1,0:T(2,128)(2,1)}, u32[]{:S(2)}, u32[]{:S(2)}) %all-to-all-start.1) | async-done | bytes 2097184 | tf_op jit(solution)/shard_map/all_to_all | solution.py:185
  248.4 1.9 copy.177
  251.3 1.4 fusion.21
  252.9 1.6 convolution_bitcast_fusion
  254.5 2.6 multiply_subtract_fusion
  257.3 3.3 reshape.1330
  260.6 8.8 %copy.188 = bf16[2,64,64,128]{3,1,2,0:T(8,128)(2,1)S(1)} copy(bf16[2,64,64,128]{1,0,2,3:T(2,128)(2,1)} %reshape.1330) | data formatting | bytes 4194304 | tf_op jit(solution)/shard_map/stack;reshape | solution.py:197
  269.4 1.5 gather_fusion
  270.9 6.5 %all-to-all-start.2 = ((bf16[32,1,1,64,128]{4,3,2,1,0:T(8,128)(2,1)}), bf16[32,1,1,64,128]{4,3,2,1,0:T(8,128)(2,1)S(1)}, u32[]{:S(2)}, u32[]{:S(2)}) async-start(bf16[32,1,1,64,128]{4,3,2,1,0:T(8,128)(2,1)} %bitcast.286), calls=%async_computation.2 | async-start | bytes 1048576 | tf_op jit(solution)/shard_map/all_to_all | solution.py:212
  279.4 13.3 %all-to-all-done.2 = bf16[32,1,1,64,128]{4,3,2,1,0:T(8,128)(2,1)S(1)} async-done(((bf16[32,1,1,64,128]{4,3,2,1,0:T(8,128)(2,1)}), bf16[32,1,1,64,128]{4,3,2,1,0:T(8,128)(2,1)S(1)}, u32[]{:S(2)}, u32[]{:S(2)}) %all-to-all-start.2) | async-done | bytes 524320 | tf_op jit(solution)/shard_map/all_to_all | solution.py:212
  293.3 1.6 copy.190
  298.3 4.1 %copy.194 = bf16[32,3,64,64,2]{2,0,4,3,1:T(8,128)(2,1)} copy(bf16[32,3,64,64,2]{3,2,1,0,4:T(8,128)(2,1)S(1)} %pad_maximum_fusion.4) | data formatting | bytes 3145728 | tf_op jit(solution)/shard_map/stack | solution.py:239
  302.4 5.6 %copy.195 = bf16[32,3,64,128]{3,2,1,0:T(8,128)(2,1)} copy(bf16[32,3,64,128]{2,0,3,1:T(8,128)(2,1)} %bitcast.305) | data formatting | bytes 3145728 | tf_op jit(solution)/shard_map/convert_element_type | solution.py:241
  309.2 3.2 reshape.1376
  312.4 3.2 convert_element_type.258
  317.3 22.8 %reduce-scatter.2.cloned.1.call-done = bf16[4,3,64,128]{3,2,1,0:T(8,128)(2,1)} async-done(((bf16[32,3,64,128]{3,2,1,0:T(8,128)(2,1)}), bf16[4,3,64,128]{3,2,1,0:T(8,128)(2,1)}) %reduce-scatter.2.cloned.1.call-update) | async-done | bytes 196624 | tf_op jit(solution)/shard_map/reduce_scatter | solution.py:240
  342.7 26.5 %reshape_reshape.5 = f32[12,4096,2]{2,1,0:T(8,128)} reshape(f32[768,128]{1,0:T(8,128)S(1)} %fusion.104) | data formatting | bytes 786432 | tf_op jit(solution)/shard_map/reshape;reshape | solution.py:250
  369.3 23.9 %fusion.1 = f32[12,4096]{1,0:T(8,128)S(1)} fusion(f32[12,4096,2]{2,1,0:T(8,128)} %reshape_reshape.5), kind=kLoop, calls=%fused_computation.4 | loop fusion | flops 147456 | bytes 589824 | tf_op jit(solution)/shard_map/add | solution.py:251
  (94 shorter events, 19.9 us)
Async XLA Ops:
  6.5 0.7 copy-start
  30.8 61.1 %all-to-all-start = ((bf16[128,64,128]{2,0,1:T(8,128)(2,1)}), bf16[128,64,128]{2,0,1:T(8,128)(2,1)S(1)}, u32[]{:S(2)}, u32[]{:S(2)}) async-start(bf16[128,64,128]{2,0,1:T(8,128)(2,1)} %fusion.13), calls=%async_computation | async-start | bytes 4194304 | tf_op jit(solution)/shard_map/all_to_all | solution.py:147
  92.0 1.3 copy-start.3
  192.6 7.5 %copy-start.5 = (s32[256,4]{0,1:T(4,128)S(1)}, s32[256,4]{0,1:T(4,128)}, u32[]{:S(2)}) copy-start(s32[256,4]{0,1:T(4,128)} %param.18) | copy-start | bytes 12292
  192.6 7.8 %copy-start.4 = (bf16[128,4096]{1,0:T(8,128)(2,1)S(1)}, bf16[128,4096]{1,0:T(8,128)(2,1)}, u32[]{:S(2)}) copy-start(bf16[128,4096]{1,0:T(8,128)(2,1)} %param.15) | copy-start | bytes 3145732
  192.6 55.9 %all-to-all-start.1 = ((bf16[4096,2,128]{2,1,0:T(2,128)(2,1)}), bf16[4096,2,128]{2,1,0:T(2,128)(2,1)}, u32[]{:S(2)}, u32[]{:S(2)}) async-start(bf16[4096,2,128]{2,1,0:T(2,128)(2,1)} %reshape.1380), calls=%async_computation.1 | async-start | bytes 4194304 | tf_op jit(solution)/shard_map/all_to_all | solution.py:185
  252.9 1.6 copy-start.2
  269.4 8.3 %copy-start.7 = (f32[8]{0:T(128)S(1)}, f32[8]{0:T(128)}, u32[]{:S(2)}) copy-start(f32[8]{0:T(128)} %param.17) | copy-start | bytes 100
  270.9 21.8 %all-to-all-start.2 = ((bf16[32,1,1,64,128]{4,3,2,1,0:T(8,128)(2,1)}), bf16[32,1,1,64,128]{4,3,2,1,0:T(8,128)(2,1)S(1)}, u32[]{:S(2)}, u32[]{:S(2)}) async-start(bf16[32,1,1,64,128]{4,3,2,1,0:T(8,128)(2,1)} %bitcast.286), calls=%async_computation.2 | async-start | bytes 1048576 | tf_op jit(solution)/shard_map/all_to_all | solution.py:212
  277.4 62.7 %reduce-scatter.2.cloned.1.call-start = ((), (), s32[]{:S(2)}) async-start(), calls=%async_computation.4 | async-start | bytes 1769472 | tf_op jit(solution)/shard_map/reduce_scatter | solution.py:240
  309.1 6.6 %copy-start.6 = (s32[256]{0:T(256)S(1)}, s32[256]{0:T(256)}, u32[]{:S(2)}) copy-start(s32[256]{0:T(256)} %param.19) | copy-start | bytes 3076
  369.3 25.5 %copy-start.1 = (s32[8,2]{0,1:T(2,128)S(1)}, s32[8,2]{0,1:T(2,128)}, u32[]{:S(2)}) copy-start(s32[8,2]{0,1:T(2,128)} %param.16) | copy-start | bytes 196
Sparse Core Ops, SparseCore 0:
  308.1 31.9 reduce-scatter.1
where the time goes:
time: 410 us; the launch traced here: 402 us
  local copies, waits for them, and re-layouts  152 us (37%)
  waiting for transfers between devices  123 us (30%)
  other arithmetic  67.9 us (17%)
  starting transfers between devices  26.1 us (6%)
  matrix products  17.1 us (4%)
  between operations  15.9 us (4%)
    all_to_all x1, waiting for transfers between devices, shards(): lax.all_to_all(spectrum, 'beam', split_axis=1, concat_axis=0, tiled=True)  48.5 us
    all_to_all x1, waiting for transfers between devices, shards(): lax.all_to_all(sectioned, 'beam', split_axis=0, concat_axis=1, tiled=True)  38.8 us
    another operation x1, local copies, waits for them, and re-layouts, shards(): radix_section(spectrum, paired).reshape(share_slots * G, A * A, 2)  26.5 us
    add x1, other arithmetic, shards(): intensity = spectrum[..., 0] ** 2 + spectrum[..., 1] ** 2  23.9 us
    reduce_scatter x1, waiting for transfers between devices, shards(): lax.psum_scatter(partial_value.astype(jnp.bfloat16), 'slab', scatter_dime...  22.8 us
    dot_general x5, local copies, waits for them, and re-layouts, radix_section(): jnp.dot(flat, table, preferred_element_type=jnp.float32)  22.6 us
    reshape x2, local copies, waits for them, and re-layouts, shards(): sectioned = sectioned.transpose(4, 0, 1, 3, 2).reshape(N, width_k, 2 * A)  21.4 us
    dot_general x10, matrix products, radix_section(): jnp.dot(flat, table, preferred_element_type=jnp.float32)  16.2 us
  transfers between devices with their start and end apart: 4, of which 4 were waited for; matrix products, arithmetic and copies ran while one was open for 5% of the time, Pallas kernels for 0%

commit v1 on v0

v1 whole, which is shorter than its diff:
```python
import math

import jax
import jax.numpy as jnp
import numpy as np
from jax import lax
from jax.experimental import pallas as pl
from jax.experimental.pallas import tpu as pltpu
from jax.sharding import PartitionSpec as P

A = 64
N = 4096
F = 64
G = 3
NDET = 16
QMAX = 3
NB = 32
NS = 8
KY = 48
LOW = 24
F32 = jnp.float32
BF16 = jnp.bfloat16


def trig64(product):
    angles = 2.0 * np.pi / A * (np.asarray(product) % A)
    cosine = np.cos(angles).astype(np.float32).astype(jnp.bfloat16).astype(np.float32)
    sine = np.sin(angles).astype(np.float32).astype(jnp.bfloat16).astype(np.float32)
    return cosine, sine


def rotate_block(cosine, sine, orient):
    top = np.concatenate([cosine, orient * sine], axis=1)
    low = np.concatenate([-orient * sine, cosine], axis=1)
    return np.concatenate([top, low], axis=0)


def host_tables():
    d = np.arange(A)
    order = np.concatenate([np.arange(0, A, 2), np.arange(1, A, 2)])
    c, s = trig64(order[:, None] * d[None, :])
    xf1 = rotate_block(c, s, 1.0) / A
    c, s = trig64(d[:, None] * d[None, :])
    eye2 = np.eye(2)
    xf2 = rotate_block(np.kron(eye2, c), np.kron(eye2, s), -1.0) / A
    n1 = 2 * np.arange(NB)[:, None] + np.arange(2)[None, :]
    c, s = trig64(d[:, None, None] * n1[None])
    re = np.stack([c, s], axis=2).reshape(A, 2 * A)
    im = np.stack([-s, c], axis=2).reshape(A, 2 * A)
    yf1 = np.concatenate([re, im], axis=0) / A
    k2 = np.arange(56) - LOW - QMAX
    n2 = NS * np.arange(NS)[:, None] + np.arange(8)[None, :]
    c, s = trig64(k2[:, None, None] * n2[None])
    re = np.stack([c, s], axis=2).reshape(56, 2 * A)
    im = np.stack([-s, c], axis=2).reshape(56, 2 * A)
    yf2 = np.stack([re, im]) / A
    c, s = trig64(d[:, None] * (np.arange(KY) - LOW)[None, :])
    yi1 = rotate_block(c, s, -1.0)
    c, s = trig64(order[:, None] * d[None, :])
    yi2 = rotate_block(c, s, -1.0)
    k2 = np.arange(72) - QMAX
    c, s = trig64(k2[:, None] * d[None, :])
    zero = np.zeros_like(c)
    xi1 = np.stack(
        [
            np.stack(
                [np.concatenate([c, zero, s, zero], 1), np.concatenate([zero, c, zero, s], 1)]
            ),
            np.stack(
                [np.concatenate([-s, zero, c, zero], 1), np.concatenate([zero, -s, zero, c], 1)]
            ),
        ]
    )
    c, s = trig64(d[:, None] * d[None, :])
    df1 = rotate_block(c, s, -1.0) / A
    df2 = np.concatenate([c, s], axis=0) / A
    to16 = lambda t: t.astype(np.float32).astype(jnp.bfloat16)
    return {
        "xf1": to16(xf1),
        "xf2": to16(xf2),
        "yf1": to16(yf1),
        "yf2": yf2.astype(np.float32),
        "yi1": to16(yi1),
        "yi2": to16(yi2),
        "xi1": np.stack([xi1[..., :128], xi1[..., 128:]], axis=2).astype(np.float32),
        "df1": to16(df1),
        "df2": to16(df2),
    }


def ring_counts():
    d = np.arange(A)
    signed = np.where(d < A // 2, d, d - A)
    radius = signed[:, None] ** 2 + signed[None, :] ** 2
    width = A // (2 * NDET)
    return [
        int(((radius >= (width * b) ** 2) & (radius < (width * (b + 1)) ** 2)).sum())
        for b in range(NDET)
    ]


def poly_sincos(r):
    t = r * r
    sine = r + r * t * (-1.6666667e-1 + t * (8.3333333e-3 + t * (-1.9841270e-4 + t * 2.7557319e-6)))
    cosine = 1.0 + t * (-0.5 + t * (4.1666667e-2 + t * (-1.3888889e-3 + t * 2.4801587e-5)))
    return sine, cosine


def place(sine, cosine, quadrant):
    swap = (quadrant & 1) == 1
    a = jnp.where(swap, cosine, sine)
    b = jnp.where(swap, sine, cosine)
    a = jnp.where((quadrant & 2) == 2, -a, a)
    b = jnp.where(((quadrant + 1) & 2) == 2, -b, b)
    return a, b


def sincos(x):
    k = jnp.floor(x * (2.0 / math.pi) + 0.5)
    r = (x - k * 1.5707963) - k * 2.6794897e-8
    sine, cosine = poly_sincos(r)
    return place(sine, cosine, k.astype(jnp.int32))


def sincos_int(m, period):
    shift = int(math.log2(period)) - 2
    quadrant = (m + (period >> 3)) >> shift
    r = (m - (quadrant << shift)).astype(F32) * (2.0 * math.pi / period)
    sine, cosine = poly_sincos(r)
    return place(sine, cosine, quadrant)


def dot(a, b):
    return jnp.dot(a, b, preferred_element_type=F32)


def iota(shape, axis):
    return lax.broadcasted_iota(jnp.int32, shape, axis)


def x_forward(px, xf1, xf2, out, buf):
    pot = px[...].astype(F32)
    ti, tr = sincos(pot)
    wave = jnp.concatenate([tr.astype(BF16), ti.astype(BF16)], axis=0)
    y = dot(xf1[...], wave)
    row = iota((A, 128), 0)
    k1 = 2 * (row & 31) + (row >> 5)
    ts, tc = sincos_int(k1 * (iota((A, 128), 1) & 63), N)
    left = iota((32, 128), 1) < A
    for t in range(8):
        yr = y[:A, 128 * t : 128 * t + 128]
        yi = y[A:, 128 * t : 128 * t + 128]
        z = jnp.concatenate(
            [(yr * tc + yi * ts).astype(BF16), (yi * tc - yr * ts).astype(BF16)], axis=1
        )
        spec = dot(z, xf2[...])
        for part in range(2):
            block = spec[:, 128 * part : 128 * part + 128]
            even, odd = block[:32], block[32:]
            first = jnp.where(left, even, pltpu.roll(odd, A, 1))
            second = jnp.where(left, pltpu.roll(even, A, 1), odd)
            buf[pl.ds(part * 16 + 2 * t, 32, stride=32), :] = first
            buf[pl.ds(part * 16 + 2 * t + 1, 32, stride=32), :] = second
    out[...] = buf[...].astype(BF16)


def y_first(rows, yf1, out, buf, buf2):
    slab = lax.axis_index("slab")
    buf[...] = rows[...].astype(F32)
    for i in range(8):
        x = buf[pl.ds(i, 128, stride=8), :].astype(BF16)
        y = dot(yf1[...], x)
        ts, tc = sincos_int(iota((A, 128), 0) * (8 * slab + i), N)
        yr, yi = y[:A], y[A:]
        buf2[pl.ds(i, A, stride=16), :] = yr * tc + yi * ts
        buf2[pl.ds(8 + i, A, stride=16), :] = yi * tc - yr * ts
    out[...] = buf2[...].astype(BF16)


def y_second(beams, cols, yf2, yi1, yi2, out, buf, buf2):
    slab = lax.axis_index("slab")
    band = lax.axis_index("beam")
    jy = beams[slab, 0]
    jx = beams[slab, 1]
    forward = jnp.concatenate(
        [yf2[0, pl.ds(QMAX - jy, KY), :], yf2[1, pl.ds(QMAX - jy, KY), :]], axis=0
    ).astype(BF16)
    lane = iota((KY, 128), 1)
    fx = ((2 * band + (lane >> 6) + A * ((lane & 63) + jx) + N // 2) & (N - 1)) - N // 2
    qx = fx * fx
    ky0 = A * (iota((KY, 128), 0) - LOW)
    b_row = iota((A, 128), 0)

    def first(k1, carry):
        x = jnp.concatenate([cols[p, pl.ds(k1 * 16, 16), :] for p in range(NS)], axis=0)
        g = dot(forward, x)
        fy = ky0 + k1
        q = qx + fy * fy
        hs, hc = sincos_int(q, 2 * N)
        inside = q <= (N // 3) ** 2
        hc = jnp.where(inside, hc, 0.0)
        hs = jnp.where(inside, hs, 0.0)
        gr, gi = g[:KY], g[KY:]
        v = jnp.concatenate(
            [(gr * hc + gi * hs).astype(BF16), (gi * hc - gr * hs).astype(BF16)], axis=0
        )
        u = dot(yi1[...], v)
        ts, tc = sincos_int(b_row * k1, N)
        ur, ui = u[:A], u[A:]
        buf[pl.ds(k1, A, stride=128), :] = ur * tc - ui * ts
        buf[pl.ds(A + k1, A, stride=128), :] = ur * ts + ui * tc
        return carry

    lax.fori_loop(0, A, first, 0)

    def second(b, carry):
        z = buf[pl.ds(pl.multiple_of(b * 128, 128), 128), :].astype(BF16)
        w = dot(yi2[...], z)
        for k in range(4):
            buf2[pl.ds(k * A + b, 32, stride=256), :] = w[32 * k : 32 * k + 32]
        return carry

    lax.fori_loop(0, A, second, 0)
    out[...] = buf2[...].astype(BF16)


def x_inverse(beams, tiles, rows, xi1, out, buf, buf2):
    slab = lax.axis_index("slab")
    jx = beams[slab, 1]
    shifted = [
        jnp.concatenate([xi1[p, q, k, pl.ds(QMAX + jx, A), :] for k in range(2)], axis=1)
        for p in range(2)
        for q in range(2)
    ]
    table = jnp.concatenate(shifted, axis=0).astype(BF16)
    lane = iota((8, 128), 1)

    def first(f, carry):
        base = pl.multiple_of(f * 256, 256)
        z = jnp.concatenate([rows[pl.ds(base, 128), :], rows[pl.ds(base + 128, 128), :]], axis=1)
        u = dot(z, table)
        ts, tc = sincos_int((2 * f + (lane >> 6)) * (lane & 63), N)
        ts, tc = ts[:1], tc[:1]
        ur, ui = u[:, :128], u[:, 128:]
        zr = ur * tc - ui * ts
        zi = ur * ts + ui * tc
        for h in range(2):
            buf[pl.ds(h * A + f, A, stride=128), :] = zr[A * h : A * h + A]
            buf[pl.ds(h * A + 32 + f, A, stride=128), :] = zi[A * h : A * h + A]
        return carry

    lax.fori_loop(0, NB, first, 0)

    row = iota((128, 128), 0)
    col = iota((128, 128), 1)
    ids = tiles[...]
    ids = jnp.concatenate([ids, ids, ids, ids], axis=0)
    k1 = 2 * (col & 31) + (row >> 6)
    ws, wc = sincos_int((k1 * (ids & 63)) & 63, A)
    row_part = (row >> 5) & 1
    col_part = (col >> 5) & 1
    value = jnp.where(row_part == col_part, wc, jnp.where(row_part == 1, ws, -ws))
    value = jnp.where(((ids >> 6) & 1) == (col >> 6), value, 0.0).astype(BF16)
    left = iota((A, 128), 1) < A

    def second(y, carry):
        z = buf[pl.ds(pl.multiple_of(y * 128, 128), 128), :].astype(BF16)
        o = dot(value, z)
        both = jnp.where(left, o[:A], o[A:])
        both = both + pltpu.roll(both, A, 1)
        buf2[pl.ds(y, 32, stride=A), :] = jnp.where(left[:32], both[:32], both[32:])
        return carry

    lax.fori_loop(0, A, second, 0)
    out[...] = buf2[...].astype(BF16)


def detect(ids, coef, parts, pot, df1, df2, out, buf):
    left = iota((A, 128), 1) < A
    sign = jnp.where(left, -1.0, 1.0)
    ky = iota((A, 128), 0)
    kx = iota((A, 128), 1) & 63
    ky = jnp.where(ky < 32, ky, ky - A)
    kx = jnp.where(kx < 32, kx, kx - A)
    radius = ky * ky + kx * kx
    counts = ring_counts()
    width = A // (2 * NDET)
    for l in range(4):
        ident = ids[l]
        half = pl.multiple_of(((ident >> 6) & 1) * A, A)
        pair = pl.multiple_of(((ident & 63) >> 1) * 128, 128)
        tile = pot[pl.ds(half, A), pl.ds(pair, 128)].astype(F32)
        odd = (ident & 1) == 1
        turned = pltpu.roll(tile, A, 1)
        tile = jnp.where(left != odd, tile, turned)
        ps, pc = sincos(tile)
        ps = ps * sign
        fields = [parts[j, A * l : A * l + A, :].astype(F32) for j in range(8)]
        swapped = [pltpu.roll(f, A, 1) * sign for f in fields]
        for g in range(G):
            probe = jnp.zeros((A, 128), F32)
            for j in range(8):
                at = (j * 4 + l) * G + g
                probe = probe + fields[j] * coef[0, at] + swapped[j] * coef[1, at]
            probe = probe * pc + pltpu.roll(probe, A, 1) * ps
            d = dot(probe.astype(BF16), df1[...]).astype(BF16)
            w = dot(df2[...], d)
            value = w[:A] - sign * pltpu.roll(w[A:], A, 1)
            power = value * value
            for b in range(NDET):
                member = (radius >= (width * b) ** 2) & (radius < (width * (b + 1)) ** 2)
                part = jnp.where(member, power, 0.0) * (A * A / (8.0 * counts[b]))
                buf[(l * G + g) * NDET + b, :] = jnp.sum(part, axis=0)
    ones = jnp.ones((8, 128), F32)
    total = lax.dot_general(
        ones,
        buf[...],
        (((1,), (1,)), ((), ())),
        precision=lax.Precision.HIGHEST,
        preferred_element_type=F32,
    )
    out[...] = total


def call(kernel, out_shape, out_type, scratch, smem, args):
    specs = [
        pl.BlockSpec(memory_space=pltpu.SMEM if k < smem else pltpu.VMEM) for k in range(len(args))
    ]
    return pl.pallas_call(
        kernel,
        out_shape=jax.ShapeDtypeStruct(out_shape, out_type),
        in_specs=specs,
        out_specs=pl.BlockSpec(memory_space=pltpu.VMEM),
        scratch_shapes=[pltpu.VMEM(s, F32) for s in scratch],
        compiler_params=pltpu.CompilerParams(vmem_limit_bytes=50 * 1024 * 1024),
    )(*args)


def coefficients(tile_ids, beam_rows, shifts):
    across = N // A
    offsets = jnp.arange(G, dtype=jnp.int32)
    spot_y = (tile_ids // across)[:, None] * A + A // 2 + offsets[None, :]
    spot_x = (tile_ids % across)[:, None] * A + A // 2 + 2 * offsets[None, :]
    wave_y = jnp.remainder(F * beam_rows[:, 0], N)[:, None, None]
    wave_x = jnp.remainder(F * beam_rows[:, 1], N)[:, None, None]
    windings = (wave_y * spot_y[None] % N + wave_x * spot_x[None] % N) % N
    phases = shifts[:, None, None] + 2.0 * math.pi / N * windings.astype(F32)
    return (jnp.cos(phases), -jnp.sin(phases))


def shards(pot_first, pot_second, beam_index, aberration, tile_table, tile_count):
    band = lax.axis_index("beam")
    slab = lax.axis_index("slab")
    tab = host_tables()
    px = lax.dynamic_slice_in_dim(pot_first.reshape(2, A, N), 8 * slab, 8, 1)
    px = px.reshape(16, A, A).transpose(1, 0, 2).reshape(A, 1024)
    msg = call(
        x_forward, (1024, 128), BF16, [(1024, 128)], 0, (px, tab["xf1"], tab["xf2"])
    )
    rows = lax.all_to_all(msg.reshape(NB, 32, 128), "beam", 0, 0, tiled=True)
    piece = call(
        y_first,
        (1024, 128),
        BF16,
        [(1024, 128), (1024, 128)],
        0,
        (rows.reshape(1024, 128), tab["yf1"]),
    )
    cols = lax.all_gather(piece, "slab")
    msg = call(
        y_second,
        (8192, 128),
        BF16,
        [(8192, 128), (8192, 128)],
        1,
        (beam_index, cols, tab["yf2"], tab["yi1"], tab["yi2"]),
    )
    rows = lax.all_to_all(msg.reshape(NB, 256, 128), "beam", 0, 0, tiled=True)

    lists = tile_table.reshape(NB, NB)
    matched = (lists // 128) == band
    chosen = jnp.sum(jnp.where(matched, lists, 0), axis=1)
    within = jnp.arange(NB, dtype=jnp.int32) % 4
    active = within[None, :] < jnp.repeat(tile_count.reshape(NB, NS), 4, axis=1)
    active = jnp.sum(jnp.where(matched & active, 1.0, 0.0), axis=1)
    tiles = jnp.broadcast_to(chosen[:, None], (NB, 128))
    exits = call(
        x_inverse,
        (2048, 128),
        BF16,
        [(8192, 128), (2048, 128)],
        1,
        (beam_index, tiles, rows.reshape(8192, 128), tab["xi1"]),
    )
    parts = lax.all_to_all(exits.reshape(NS, 256, 128), "slab", 0, 0, tiled=True)
    own = lax.dynamic_slice_in_dim(chosen, 4 * slab, 4, 0)
    cc, cs = coefficients(own, beam_index, aberration)
    coef = jnp.stack([cc.reshape(-1), cs.reshape(-1)])
    sums = call(
        detect,
        (8, 192),
        F32,
        [(192, 128)],
        2,
        (own, coef, parts, pot_second, tab["df1"], tab["df2"]),
    )
    sums = sums[0].reshape(4, G * NDET)
    sums = jnp.where(lax.dynamic_slice_in_dim(active, 4 * slab, 4, 0)[:, None] > 0, sums, 0.0)
    spread = jnp.where(
        (jnp.arange(NS) == slab)[:, None, None], sums[None], 0.0
    ).reshape(NB, G * NDET)
    spread = lax.all_to_all(spread, "beam", 0, 0, tiled=True)
    spread = lax.psum(spread, "slab")
    mine = lax.dynamic_index_in_dim(lists, band, 0, keepdims=False) // 128
    mine = lax.dynamic_slice_in_dim(mine, 4 * slab, 4, 0)
    return spread[mine].reshape(1, 4, G, NDET)


def solution(mesh):
    return jax.shard_map(
        shards,
        mesh=mesh,
        in_specs=(P("beam", None), P("beam", None), P(), P(), P(), P()),
        out_specs=P(("beam", "slab"), None, None, None),
        check_vma=False,
    )
```

time: 410 us -> 249 us (0.61); the launches traced: 402 us -> 248 us
  local copies, waits for them, and re-layouts: 152 us -> 10.7 us
  Pallas kernels: 0 us -> 67.7 us
  other arithmetic: 67.9 us -> 3.41 us
  blocking collectives: 0 us -> 46.3 us
  waiting for transfers between devices: 123 us -> 86.5 us
  matrix products: 17.1 us -> 0 us
  starting transfers between devices: 26.1 us -> 20.1 us
    pallas_call x0 -> x5, Pallas kernels: none -> 67.7 us  [call(): pl.pallas_call(kernel, out_shape=jax.ShapeDtypeStruct(out_shape, out_type...]
    another operation x8 -> x1, local copies, waits for them, and re-layouts: 54.8 us -> 0.08 us  [shards(): sums = sums[0].reshape(4, G * NDET)]
    all_to_all x3, waiting for transfers between devices: 101 us -> 62 us  [the longest x1 43.6 us: shards(): rows = lax.all_to_all(msg.reshape(NB, 256, 128), 'beam', 0, 0, tiled=True)]
    all_gather x0 -> x1, waiting for transfers between devices: none -> 24.5 us  [shards(): cols = lax.all_gather(piece, 'slab')]
    add x3 -> x0, other arithmetic: 24 us -> none  [the longest x1 23.9 us: shards(): intensity = spectrum[..., 0] ** 2 + spectrum[..., 1] ** 2]
    psum x0 -> x1, blocking collectives: none -> 23.5 us  [shards(): spread = lax.psum(spread, 'slab')]
    reduce_scatter x1 -> x0, waiting for transfers between devices: 22.8 us -> none  [shards(): lax.psum_scatter(partial_value.astype(jnp.bfloat16), 'slab', scatter_dime...]
    all_to_all x0 -> x1, blocking collectives: none -> 22.7 us  [shards(): rows = lax.all_to_all(msg.reshape(NB, 32, 128), 'beam', 0, 0, tiled=True)]
  transfers between devices with their start and end apart: 4 -> 4, of which waited for: 4 -> 4; matrix products, arithmetic and copies ran while one was open for 5% -> 3% of each run, Pallas kernels for 0% -> 0%
where the time goes in v1:
time: 249 us; the launch traced here: 248 us
  waiting for transfers between devices  86.5 us (35%)
  Pallas kernels  67.7 us (27%)
  blocking collectives  46.3 us (19%)
  starting transfers between devices  20.1 us (8%)
  between operations  13.6 us (5%)
  local copies, waits for them, and re-layouts  10.7 us (4%)
  other arithmetic  3.41 us (1%)
    pallas_call x5, Pallas kernels, call(): pl.pallas_call(kernel, out_shape=jax.ShapeDtypeStruct(out_shape, out_type...  67.7 us
    all_to_all x1, waiting for transfers between devices, shards(): rows = lax.all_to_all(msg.reshape(NB, 256, 128), 'beam', 0, 0, tiled=True)  43.6 us
    all_gather x1, waiting for transfers between devices, shards(): cols = lax.all_gather(piece, 'slab')  24.5 us
    psum x1, blocking collectives, shards(): spread = lax.psum(spread, 'slab')  23.5 us
    all_to_all x1, blocking collectives, shards(): rows = lax.all_to_all(msg.reshape(NB, 32, 128), 'beam', 0, 0, tiled=True)  22.7 us
    all_to_all x1, starting transfers between devices, shards(): rows = lax.all_to_all(msg.reshape(NB, 256, 128), 'beam', 0, 0, tiled=True)  10.3 us
    all_to_all x1, waiting for transfers between devices, shards(): lax.all_to_all(exits.reshape(NS, 256, 128), 'slab', 0, 0, tiled=True)  9.94 us
    all_to_all x1, waiting for transfers between devices, shards(): spread = lax.all_to_all(spread, 'beam', 0, 0, tiled=True)  8.51 us
  transfers between devices with their start and end apart: 4, of which 4 were waited for; matrix products, arithmetic and copies ran while one was open for 3% of the time, Pallas kernels for 0%

profile of v1, /device:TPU:8, one launch (start us, length us, event | category | flops | bytes accessed | tf_op | source)
XLA Modules:
  0.0 248.3 jit_solution(10779506757446231497)
XLA Ops:
  6.6 1.2 copy-done
  7.8 0.2 reshape.408
  8.0 0.2 copy.24
  8.2 0.2 reshape.409.px
  8.4 0.9 copy-done.4
  9.3 0.8 copy-done.11
  10.1 1.1 shard_map.145
  11.2 22.7 %all_to_all.24 = bf16[32,32,128]{2,1,0:T(8,128)(2,1)S(1)} all-to-all(bf16[32,32,128]{2,1,0:T(8,128)(2,1)S(1)} %bitcast.27), channel_id=1, replica_groups=mesh['beam'=32,'slab'=8] {'beam'}, dimensions={0} | all-to-all | bytes 524288 | tf_op jit(solution)/shard_map/all_to_all | solution.py:360
  33.9 1.4 shard_map.146
  35.3 0.1 copy.26.beams
  35.4 24.5 %all-gather.3.cloned.1.call-done = bf16[8192,128]{1,0:T(8,128)(2,1)} async-done(((bf16[1024,128]{1,0:T(8,128)(2,1)}), bf16[8192,128]{1,0:T(8,128)(2,1)}) %all-gather.3.cloned.1.call-update) | async-done | bytes 2097168 | tf_op jit(solution)/shard_map/all_gather | solution.py:369
  59.9 37.8 %shard_map.147 = bf16[8192,128]{1,0:T(8,128)(2,1)} custom-call(s32[8,2]{1,0:T(8,128)S(1)} %copy.26.beams, bf16[8,1024,128]{2,1,0:T(8,128)(2,1)} %bitcast.29, f32[2,56,128]{2,1,0:T(8,128)S(1)} %copy-done.5, bf16[128,96]{1,0:T(8,128)(2,1)S(1)} %copy-done.6, bf16[128,128]{1,0:T(8,128)(2,1)S(1)} %copy-done.7), custom_call_target="tpu_custom_call" | custom-call | tf_op jit(solution)/shard_map/pallas_call | solution.py:329
  97.7 10.3 %all-to-all-start.1 = ((bf16[32,256,128]{2,1,0:T(8,128)(2,1)}), bf16[32,256,128]{2,1,0:T(8,128)(2,1)S(1)}, u32[]{:S(2)}, u32[]{:S(2)}) async-start(bf16[32,256,128]{2,1,0:T(8,128)(2,1)} %bitcast.7), calls=%async_computation.1 | async-start | bytes 4194304 | tf_op jit(solution)/shard_map/all_to_all | solution.py:378
  108.1 0.1 lt.64
  108.2 0.8 copy.27
  109.0 0.1 reduce_sum.36
  109.1 0.1 reduce_sum.37
  109.3 0.1 multiply_add_fusion
  109.4 0.1 iota_add_fusion
  109.5 0.1 broadcast_multiply_fusion
  109.6 0.1 mul.119
  109.7 0.6 mul.127
  110.3 0.1 add.183
  110.4 0.6 add.184
  111.0 0.1 reduce_sum.24
  111.1 1.0 reshape.415
  112.2 0.6 reduce_sum.25
  112.8 0.6 dynamic-slice_compare_fusion
  113.4 0.7 fusion.18
  114.1 43.6 %all-to-all-done.1 = bf16[32,256,128]{2,1,0:T(8,128)(2,1)S(1)} async-done(((bf16[32,256,128]{2,1,0:T(8,128)(2,1)}), bf16[32,256,128]{2,1,0:T(8,128)(2,1)S(1)}, u32[]{:S(2)}, u32[]{:S(2)}) %all-to-all-start.1) | async-done | bytes 2097184 | tf_op jit(solution)/shard_map/all_to_all | solution.py:378
  157.8 24.1 %shard_map.148 = bf16[2048,128]{1,0:T(8,128)(2,1)S(1)} custom-call(s32[8,2]{1,0:T(8,128)S(1)} %copy.26.beams, s32[32,128]{1,0:T(8,128)S(1)} %broadcast_in_dim.80.tiles, bf16[8192,128]{1,0:T(8,128)(2,1)S(1)} %bitcast.25, f32[2,2,2,72,128]{4,3,2,1,0:T(8,128)S(1)} %copy-done.3), custom_call_target="tpu_custom_call" | custom-call | tf_op jit(solution)/shard_map/pallas_call | solution.py:329
  181.9 0.8 copy-done.1
  182.7 3.5 %all-to-all-start.2 = ((bf16[8,256,128]{2,1,0:T(8,128)(2,1)}), bf16[8,256,128]{2,1,0:T(8,128)(2,1)S(1)}, u32[]{:S(2)}, u32[]{:S(2)}) async-start(bf16[8,256,128]{2,1,0:T(8,128)(2,1)} %bitcast.26), calls=%async_computation.2 | async-start | bytes 1048576 | tf_op jit(solution)/shard_map/all_to_all | solution.py:395
  186.2 0.1 broadcast_in_dim.73
  186.3 0.1 broadcast_in_dim.74
  186.4 0.1 compare_select_fusion
  186.5 9.9 %all-to-all-done.2.parts = bf16[8,256,128]{2,1,0:T(8,128)(2,1)S(1)} async-done(((bf16[8,256,128]{2,1,0:T(8,128)(2,1)}), bf16[8,256,128]{2,1,0:T(8,128)(2,1)S(1)}, u32[]{:S(2)}, u32[]{:S(2)}) %all-to-all-start.2) | async-done | bytes 524320 | tf_op jit(solution)/shard_map/all_to_all | solution.py:395
  196.5 1.2 copy-done.2
  197.7 3.3 %shard_map.149 = f32[8,192]{1,0:T(8,128)S(1)} custom-call(s32[4]{0:T(128)S(1)} %get-tuple-element.10.ids, f32[2,96]{1,0:T(2,128)S(1)} %pad_maximum_fusion.coef, bf16[8,256,128]{2,1,0:T(8,128)(2,1)S(1)} %all-to-all-done.2.parts, bf16[128,4096]{1,0:T(8,128)(2,1)S(1)} %copy-done.2, bf16[128,128]{1,0:T(8,128)(2,1)S(1)} %copy-done.8, bf16[128,64]{1,0:T(8,128)(2,1)S(1)} %copy-done.9), custom_call_target="tpu_custom_call" | custom-call | tf_op jit(solution)/shard_map/pallas_call | solution.py:329
  201.0 0.1 reshape_squeeze.3
  201.1 0.1 broadcast_select_fusion.1
  201.2 0.7 broadcast_select_fusion
  201.9 6.3 %all-to-all-start.3 = ((f32[32,1,48]{2,1,0:T(1,128)}), f32[32,1,48]{2,1,0:T(1,128)S(1)}, u32[]{:S(2)}, u32[]{:S(2)}) async-start(f32[32,1,48]{2,1,0:T(1,128)} %broadcast_select_fusion), calls=%async_computation.3 | async-start | bytes 32768 | tf_op jit(solution)/shard_map/all_to_all | solution.py:412
  208.2 8.5 %all-to-all-done.3 = f32[32,1,48]{2,1,0:T(1,128)S(1)} async-done(((f32[32,1,48]{2,1,0:T(1,128)}), f32[32,1,48]{2,1,0:T(1,128)S(1)}, u32[]{:S(2)}, u32[]{:S(2)}) %all-to-all-start.3) | async-done | bytes 6176 | tf_op jit(solution)/shard_map/all_to_all | solution.py:412
  216.7 23.5 %psum.7 = f32[32,48]{1,0:T(8,128)S(1)} all-reduce(f32[32,48]{1,0:T(8,128)S(1)} %bitcast.31), channel_id=1, replica_groups=mesh['beam'=32,'slab'=8] {'slab'}, use_global_device_ids=true, to_apply=%region_4.5 | all-reduce | flops 1536 | bytes 12288 | tf_op jit(solution)/shard_map/psum | solution.py:413
  240.3 0.6 gather_fusion
  240.8 0.1 reshape.416
  240.9 0.6 copy.28
  (46 shorter events, 0.5 us)
Async XLA Ops:
  6.5 1.2 copy-start
  6.5 27.4 %copy-start.10 = (bf16[128,128]{1,0:T(8,128)(2,1)S(1)}, bf16[128,128]{1,0:T(8,128)(2,1)}, u32[]{:S(2)}) copy-start(bf16[128,128]{1,0:T(8,128)(2,1)} %constant.155.clone.yf1) | copy-start | bytes 98308
  6.5 53.4 %copy-start.5 = (f32[2,56,128]{2,1,0:T(8,128)S(1)}, f32[2,56,128]{2,1,0:T(8,128)}, u32[]{:S(2)}) copy-start(f32[2,56,128]{2,1,0:T(8,128)} %constant.156.clone.yf2) | copy-start | bytes 172036
  6.5 53.4 %copy-start.6 = (bf16[128,96]{1,0:T(8,128)(2,1)S(1)}, bf16[128,96]{1,0:T(8,128)(2,1)}, u32[]{:S(2)}) copy-start(bf16[128,96]{1,0:T(8,128)(2,1)} %constant.157.clone.yi1) | copy-start | bytes 73732
  6.5 53.4 %copy-start.7 = (bf16[128,128]{1,0:T(8,128)(2,1)S(1)}, bf16[128,128]{1,0:T(8,128)(2,1)}, u32[]{:S(2)}) copy-start(bf16[128,128]{1,0:T(8,128)(2,1)} %constant.158.clone.yi2) | copy-start | bytes 98308
  6.6 28.8 %copy-start.13 = (s32[8,2]{0,1:T(2,128)S(1)}, s32[8,2]{0,1:T(2,128)}, u32[]{:S(2)}) copy-start(s32[8,2]{0,1:T(2,128)} %param.17) | copy-start | bytes 196
  6.6 53.3 %all-gather.3.cloned.1.call-start = ((), (), s32[]{:S(2)}) async-start(), calls=%async_computation.4 | async-start | bytes 2359296 | tf_op jit(solution)/shard_map/all_gather | solution.py:369
  8.4 0.9 copy-start.4
  9.3 0.8 copy-start.11
  97.7 10.5 %copy-start.12 = (s32[256,4]{0,1:T(4,128)S(1)}, s32[256,4]{0,1:T(4,128)}, u32[]{:S(2)}) copy-start(s32[256,4]{0,1:T(4,128)} %param.19) | copy-start | bytes 12292
  97.7 11.3 %copy-start.14 = (s32[256]{0:T(256)S(1)}, s32[256]{0:T(256)}, u32[]{:S(2)}) copy-start(s32[256]{0:T(256)} %param.20) | copy-start | bytes 3076
  97.7 12.6 %copy-start.15 = (f32[8]{0:T(128)S(1)}, f32[8]{0:T(128)}, u32[]{:S(2)}) copy-start(f32[8]{0:T(128)} %param.18) | copy-start | bytes 100
  97.7 60.0 %copy-start.3 = (f32[2,2,2,72,128]{4,3,2,1,0:T(8,128)S(1)}, f32[2,2,2,72,128]{4,3,2,1,0:T(8,128)}, u32[]{:S(2)}) copy-start(f32[2,2,2,72,128]{4,3,2,1,0:T(8,128)} %constant.159.clone.xi1) | copy-start | bytes 884740
  97.7 59.9 %all-to-all-start.1 = ((bf16[32,256,128]{2,1,0:T(8,128)(2,1)}), bf16[32,256,128]{2,1,0:T(8,128)(2,1)S(1)}, u32[]{:S(2)}, u32[]{:S(2)}) async-start(bf16[32,256,128]{2,1,0:T(8,128)(2,1)} %bitcast.7), calls=%async_computation.1 | async-start | bytes 4194304 | tf_op jit(solution)/shard_map/all_to_all | solution.py:378
  111.1 85.3 %copy-start.8 = (bf16[128,128]{1,0:T(8,128)(2,1)S(1)}, bf16[128,128]{1,0:T(8,128)(2,1)}, u32[]{:S(2)}) copy-start(bf16[128,128]{1,0:T(8,128)(2,1)} %constant.160.clone.df1) | copy-start | bytes 98308
  111.1 85.3 %copy-start.9 = (bf16[128,64]{1,0:T(8,128)(2,1)S(1)}, bf16[128,64]{1,0:T(8,128)(2,1)}, u32[]{:S(2)}) copy-start(bf16[128,64]{1,0:T(8,128)(2,1)} %constant.161.clone.df2) | copy-start | bytes 49156
  181.9 0.8 copy-start.1
  182.7 13.8 %all-to-all-start.2 = ((bf16[8,256,128]{2,1,0:T(8,128)(2,1)}), bf16[8,256,128]{2,1,0:T(8,128)(2,1)S(1)}, u32[]{:S(2)}, u32[]{:S(2)}) async-start(bf16[8,256,128]{2,1,0:T(8,128)(2,1)} %bitcast.26), calls=%async_computation.2 | async-start | bytes 1048576 | tf_op jit(solution)/shard_map/all_to_all | solution.py:395
  196.5 1.2 copy-start.2
  201.9 14.8 %all-to-all-start.3 = ((f32[32,1,48]{2,1,0:T(1,128)}), f32[32,1,48]{2,1,0:T(1,128)S(1)}, u32[]{:S(2)}, u32[]{:S(2)}) async-start(f32[32,1,48]{2,1,0:T(1,128)} %broadcast_select_fusion), calls=%async_computation.3 | async-start | bytes 32768 | tf_op jit(solution)/shard_map/all_to_all | solution.py:412
Sparse Core Ops, SparseCore 0:
  35.4 24.4 all-gather.2

commit v2 on v1

v2 whole, which is shorter than its diff:
```python
import math

import jax
import jax.numpy as jnp
import numpy as np
from jax import lax
from jax.experimental import pallas as pl
from jax.experimental.pallas import tpu as pltpu
from jax.sharding import PartitionSpec as P

A = 64
N = 4096
F = 64
G = 3
NDET = 16
QMAX = 3
NB = 32
NS = 8
KY = 48
LOW = 24
AGC = 4
AXC = 4
F32 = jnp.float32
BF16 = jnp.bfloat16


def trig64(product):
    angles = 2.0 * np.pi / A * (np.asarray(product) % A)
    cosine = np.cos(angles).astype(np.float32).astype(jnp.bfloat16).astype(np.float32)
    sine = np.sin(angles).astype(np.float32).astype(jnp.bfloat16).astype(np.float32)
    return cosine, sine


def rotate_block(cosine, sine, orient):
    top = np.concatenate([cosine, orient * sine], axis=1)
    low = np.concatenate([-orient * sine, cosine], axis=1)
    return np.concatenate([top, low], axis=0)


def host_tables():
    d = np.arange(A)
    order = np.concatenate([np.arange(0, A, 2), np.arange(1, A, 2)])
    c, s = trig64(order[:, None] * d[None, :])
    xf1 = rotate_block(c, s, 1.0) / A
    c, s = trig64(d[:, None] * d[None, :])
    eye2 = np.eye(2)
    xf2 = rotate_block(np.kron(eye2, c), np.kron(eye2, s), -1.0) / A
    n1 = 2 * np.arange(NB)[:, None] + np.arange(2)[None, :]
    c, s = trig64(d[:, None, None] * n1[None])
    re = np.stack([c, s], axis=2).reshape(A, 2 * A)
    im = np.stack([-s, c], axis=2).reshape(A, 2 * A)
    yf1 = np.concatenate([re, im], axis=0) / A
    c, s = trig64(d[:, None] * (np.arange(KY) - LOW)[None, :])
    yi1 = rotate_block(c, s, -1.0)
    c, s = trig64(order[:, None] * d[None, :])
    yi2 = rotate_block(c, s, -1.0)
    c, s = trig64(d[:, None] * d[None, :])
    df1 = rotate_block(c, s, -1.0) / A
    df2 = np.concatenate([c, s], axis=0) / A
    to16 = lambda t: t.astype(np.float32).astype(jnp.bfloat16)
    return {
        "xf1": to16(xf1),
        "xf2": to16(xf2),
        "yf1": to16(yf1),
        "yi1": to16(yi1),
        "yi2": to16(yi2),
        "df1": to16(df1),
        "df2": to16(df2),
    }


def ring_counts():
    d = np.arange(A)
    signed = np.where(d < A // 2, d, d - A)
    radius = signed[:, None] ** 2 + signed[None, :] ** 2
    width = A // (2 * NDET)
    return [
        int(((radius >= (width * b) ** 2) & (radius < (width * (b + 1)) ** 2)).sum())
        for b in range(NDET)
    ]


def poly_sincos(r):
    t = r * r
    sine = r + r * t * (-1.6666667e-1 + t * (8.3333333e-3 + t * (-1.9841270e-4 + t * 2.7557319e-6)))
    cosine = 1.0 + t * (-0.5 + t * (4.1666667e-2 + t * (-1.3888889e-3 + t * 2.4801587e-5)))
    return sine, cosine


def place(sine, cosine, quadrant):
    swap = (quadrant & 1) == 1
    a = jnp.where(swap, cosine, sine)
    b = jnp.where(swap, sine, cosine)
    a = jnp.where((quadrant & 2) == 2, -a, a)
    b = jnp.where(((quadrant + 1) & 2) == 2, -b, b)
    return a, b


def sincos(x):
    k = jnp.floor(x * (2.0 / math.pi) + 0.5)
    r = (x - k * 1.5707963) - k * 2.6794897e-8
    sine, cosine = poly_sincos(r)
    return place(sine, cosine, k.astype(jnp.int32))


def sincos_int(m, period):
    shift = int(math.log2(period)) - 2
    quadrant = (m + (period >> 3)) >> shift
    r = (m - (quadrant << shift)).astype(F32) * (2.0 * math.pi / period)
    sine, cosine = poly_sincos(r)
    return place(sine, cosine, quadrant)


def dot(a, b):
    return jnp.dot(a, b, preferred_element_type=F32)


def iota(shape, axis):
    return lax.broadcasted_iota(jnp.int32, shape, axis)


def remote(src, dst, send, recv, target):
    return pltpu.make_async_remote_copy(
        src_ref=src,
        dst_ref=dst,
        send_sem=send,
        recv_sem=recv,
        device_id=target,
        device_id_type=pl.DeviceIdType.MESH,
    )


def x_forward(px, xf1, xf2, out, buf):
    pot = px[...].astype(F32)
    ti, tr = sincos(pot)
    wave = jnp.concatenate([tr.astype(BF16), ti.astype(BF16)], axis=0)
    y = dot(xf1[...], wave)
    row = iota((A, 128), 0)
    k1 = 2 * (row & 31) + (row >> 5)
    ts, tc = sincos_int(k1 * (iota((A, 128), 1) & 63), N)
    left = iota((32, 128), 1) < A
    for t in range(8):
        yr = y[:A, 128 * t : 128 * t + 128]
        yi = y[A:, 128 * t : 128 * t + 128]
        z = jnp.concatenate(
            [(yr * tc + yi * ts).astype(BF16), (yi * tc - yr * ts).astype(BF16)], axis=1
        )
        spec = dot(z, xf2[...])
        for part in range(2):
            block = spec[:, 128 * part : 128 * part + 128]
            even, odd = block[:32], block[32:]
            first = jnp.where(left, even, pltpu.roll(odd, A, 1))
            second = jnp.where(left, pltpu.roll(even, A, 1), odd)
            buf[pl.ds(part * 16 + 2 * t, 32, stride=32), :] = first
            buf[pl.ds(part * 16 + 2 * t + 1, 32, stride=32), :] = second
    for f in range(NB):
        out[f] = buf[32 * f : 32 * f + 32, :].astype(BF16)


def tables(jx, band, fresnel, twist):
    lane = iota((KY, 128), 1)
    fx = ((2 * band + (lane >> 6) + A * ((lane & 63) + jx) + N // 2) & (N - 1)) - N // 2
    qx = fx * fx
    ky0 = A * (iota((KY, 128), 0) - LOW)
    b_row = iota((A, 128), 0)

    def step(k1, carry):
        fy = ky0 + k1
        q = qx + fy * fy
        hs, hc = sincos_int(q, 2 * N)
        inside = q <= (N // 3) ** 2
        fresnel[k1, :KY, :] = jnp.where(inside, hc, 0.0)
        fresnel[k1, KY:, :] = jnp.where(inside, hs, 0.0)
        ts, tc = sincos_int(b_row * k1, N)
        twist[k1, :A, :] = tc
        twist[k1, A:, :] = ts
        return carry

    lax.fori_loop(0, A, step, 0, unroll=2)


def forward_table(jy):
    row = iota((KY, 128), 0)
    col = iota((KY, 128), 1)
    n2 = NS * (col >> 4) + (col & 7)
    s, c = sincos_int((n2 * (row - LOW - jy)) & (A - 1), A)
    s = s.astype(BF16).astype(F32) * (1.0 / A)
    c = c.astype(BF16).astype(F32) * (1.0 / A)
    first = (col & 8) == 0
    both = [jnp.where(first, c, s), jnp.where(first, -s, c)]
    return jnp.concatenate(both, axis=0).astype(BF16)


def inverse_table(jx):
    lane = iota((A, 128), 1)
    s, c = sincos_int(((iota((A, 128), 0) + jx) * (lane & 63)) & (A - 1), A)
    left = lane < A
    blocks = []
    for pair in ((c, s), (-s, c)):
        for q in range(2):
            keep = left if q == 0 else ~left
            blocks.append(jnp.concatenate([jnp.where(keep, v, 0.0) for v in pair], axis=1))
    return jnp.concatenate(blocks, axis=0).astype(BF16)


def y_first(slab, rows, yf1, out, buf, buf2):
    for f in range(NB):
        buf[32 * f : 32 * f + 32, :] = rows[f].astype(F32)
    for i in range(8):
        x = buf[pl.ds(i, 128, stride=8), :].astype(BF16)
        y = dot(yf1[...], x)
        ts, tc = sincos_int(iota((A, 128), 0) * (8 * slab + i), N)
        yr, yi = y[:A], y[A:]
        buf2[pl.ds(i, A, stride=16), :] = yr * tc + yi * ts
        buf2[pl.ds(8 + i, A, stride=16), :] = yi * tc - yr * ts
    out[...] = buf2[pl.ds(0, 1024), :].astype(BF16)


def y_second(start, forward, cols, yi1, fresnel, twist, buf):
    def step(k1, carry):
        x = jnp.concatenate(
            [cols[p, pl.ds(pl.multiple_of(k1 * 16, 16), 16), :] for p in range(NS)], axis=0
        )
        g = dot(forward, x)
        hc, hs = fresnel[k1, :KY, :], fresnel[k1, KY:, :]
        gr, gi = g[:KY], g[KY:]
        v = jnp.concatenate(
            [(gr * hc + gi * hs).astype(BF16), (gi * hc - gr * hs).astype(BF16)], axis=0
        )
        u = dot(yi1[...], v)
        tc, ts = twist[k1, :A, :], twist[k1, A:, :]
        ur, ui = u[:A], u[A:]
        buf[pl.ds(k1, A, stride=128), :] = ur * tc - ui * ts
        buf[pl.ds(A + k1, A, stride=128), :] = ur * ts + ui * tc
        return carry

    lax.fori_loop(start, start + A // AGC, step, 0, unroll=4)


def y_third(c, yi2, out, buf, buf2):
    size = A // AXC

    def step(b, carry):
        z = buf[pl.ds(pl.multiple_of((c * size + b) * 128, 128), 128), :].astype(BF16)
        w = dot(yi2[...], z)
        for k in range(4):
            buf2[pl.ds(k * size + b, NB, stride=4 * size), :] = w[32 * k : 32 * k + 32]
        return carry

    lax.fori_loop(0, size, step, 0, unroll=4)

    def pack(f, carry):
        out[c, f] = buf2[pl.ds(pl.multiple_of(f * 4 * size, 4 * size), 4 * size), :].astype(BF16)
        return carry

    lax.fori_loop(0, NB, pack, 0, unroll=4)


def x_second(c, table, rows, buf):
    size = A // AXC
    lane = iota((8, 128), 1)

    def step(f, carry):
        z = jnp.concatenate([rows[c, f, : 2 * size, :], rows[c, f, 2 * size :, :]], axis=1)
        u = dot(z, table)
        ts, tc = sincos_int((2 * f + (lane >> 6)) * (lane & 63), N)
        ts, tc = ts[:1], tc[:1]
        ur, ui = u[:, :128], u[:, 128:]
        zr = ur * tc - ui * ts
        zi = ur * ts + ui * tc
        for h in range(2):
            base = c * size * 128 + h * A + f
            buf[pl.ds(base, size, stride=128), :] = zr[size * h : size * h + size]
            buf[pl.ds(base + 32, size, stride=128), :] = zi[size * h : size * h + size]
        return carry

    lax.fori_loop(0, NB, step, 0, unroll=4)


def x_third(ids, out, buf, buf2):
    row = iota((128, 128), 0)
    col = iota((128, 128), 1)
    ids = jnp.broadcast_to(jnp.concatenate([ids, ids, ids, ids], axis=0), (128, 128))
    k1 = 2 * (col & 31) + (row >> 6)
    ws, wc = sincos_int((k1 * (ids & 63)) & 63, A)
    row_part = (row >> 5) & 1
    col_part = (col >> 5) & 1
    value = jnp.where(row_part == col_part, wc, jnp.where(row_part == 1, ws, -ws))
    value = jnp.where(((ids >> 6) & 1) == (col >> 6), value, 0.0).astype(BF16)
    left = iota((A, 128), 1) < A

    def step(y, carry):
        z = buf[pl.ds(pl.multiple_of(y * 128, 128), 128), :].astype(BF16)
        o = dot(value, z)
        both = jnp.where(left, o[:A], o[A:])
        both = both + pltpu.roll(both, A, 1)
        buf2[pl.ds(y, 32, stride=A), :] = jnp.where(left[:32], both[:32], both[32:])
        return carry

    lax.fori_loop(0, A, step, 0, unroll=4)
    for p in range(NS):
        out[p] = buf2[256 * p : 256 * p + 256, :].astype(BF16)


def own_tiles(band, slab, tiles):
    found = []
    for l in range(4):
        ident = jnp.int32(0)
        for q in range(NS):
            for k in range(4):
                value = tiles[(4 * slab + l) * NS + q, k]
                ident = ident + jnp.where((value >> 7) == band, value, 0)
        found.append(ident)
    return found


def probe_factors(ids, beams, shifts):
    sub = iota((8, 128), 0)
    lane = iota((8, 128), 1)
    by = jnp.zeros((8, 128), jnp.int32)
    bx = jnp.zeros((8, 128), jnp.int32)
    ab = jnp.zeros((8, 128), F32)
    for j in range(8):
        by = jnp.where(sub == j, beams[j, 0], by)
        bx = jnp.where(sub == j, beams[j, 1], bx)
        ab = jnp.where(sub == j, shifts[j], ab)
    ry = jnp.zeros((8, 128), jnp.int32)
    rx = jnp.zeros((8, 128), jnp.int32)
    for l in range(4):
        for g in range(G):
            here = lane == l * G + g
            ry = jnp.where(here, (ids[l] >> 6) * A + A // 2 + g, ry)
            rx = jnp.where(here, (ids[l] & 63) * A + A // 2 + 2 * g, rx)
    m = (F * (by * ry + bx * rx)) & (N - 1)
    s, c = sincos(ab + 2.0 * math.pi / N * m.astype(F32))
    return c, -s


def split_tiles(pot, out):
    for h in range(2):
        for pair in range(32):
            out[32 * h + pair] = pot[A * h : A * h + A, 128 * pair : 128 * pair + 128]


def detect(ids, alpha, parts, pot, df1, df2, out, buf):
    left = iota((A, 128), 1) < A
    sign = jnp.where(left, -1.0, 1.0)
    ky = iota((A, 128), 0)
    kx = iota((A, 128), 1) & 63
    ky = jnp.where(ky < 32, ky, ky - A)
    kx = jnp.where(kx < 32, kx, kx - A)
    radius = ky * ky + kx * kx
    counts = ring_counts()
    width = A // (2 * NDET)
    ones = jnp.ones((8, 128), F32)
    for l in range(4):
        ident = ids[l]
        tile = pot[((ident & 127) >> 1)].astype(F32)
        odd = (ident & 1) == 1
        turned = pltpu.roll(tile, A, 1)
        tile = jnp.where(left != odd, tile, turned)
        ps, pc = sincos(tile)
        ps = ps * sign
        fields = [parts[j, A * l : A * l + A, :].astype(F32) for j in range(8)]
        swapped = [pltpu.roll(f, A, 1) * sign for f in fields]
        for g in range(G):
            probe = jnp.zeros((A, 128), F32)
            at = l * G + g
            for j in range(8):
                probe = (
                    probe
                    + fields[j] * alpha[0][j : j + 1, at : at + 1]
                    + swapped[j] * alpha[1][j : j + 1, at : at + 1]
                )
            probe = probe * pc + pltpu.roll(probe, A, 1) * ps
            d = dot(probe.astype(BF16), df1[...]).astype(BF16)
            w = dot(df2[...], d)
            value = w[:A] - sign * pltpu.roll(w[A:], A, 1)
            power = value * value
            for b in range(NDET):
                member = (radius >= (width * b) ** 2) & (radius < (width * (b + 1)) ** 2)
                part = jnp.where(member, power, 0.0) * (A * A / (8.0 * counts[b]))
                buf[g * NDET + b : g * NDET + b + 1, :] = jnp.sum(part, axis=0, keepdims=True)
        total = lax.dot_general(
            ones,
            buf[0:128, :],
            (((1,), (1,)), ((), ())),
            precision=lax.Precision.HIGHEST,
            preferred_element_type=F32,
        )
        out[l] = total[:1]


def kernel(
    beams,
    shifts,
    tiles_s,
    counts,
    tiles_v,
    px,
    pot2,
    xf1,
    xf2,
    yf1,
    yi1,
    yi2,
    df1,
    df2,
    out,
    buf,
    buf2,
    pairs,
    fresnel,
    twist,
    msg1,
    rows1,
    cols,
    msg2,
    rows2,
    msg3,
    parts,
    res,
    sums,
    send1,
    recv1,
    sendg,
    recvg,
    send2,
    recv2,
    send3,
    recv3,
    send4,
    recv4,
):
    band = lax.axis_index("beam")
    slab = lax.axis_index("slab")
    jy = beams[slab, 0]
    jx = beams[slab, 1]
    barrier = pltpu.get_barrier_semaphore()

    def greet_beam(k, carry):
        target = {"beam": (band + k) & (NB - 1), "slab": slab}
        pl.semaphore_signal(
            barrier, inc=1, device_id=target, device_id_type=pl.DeviceIdType.MESH
        )
        return carry

    lax.fori_loop(1, NB, greet_beam, 0)

    def greet_slab(k, carry):
        target = {"beam": band, "slab": (slab + k) & (NS - 1)}
        pl.semaphore_signal(
            barrier, inc=1, device_id=target, device_id_type=pl.DeviceIdType.MESH
        )
        return carry

    lax.fori_loop(1, NS, greet_slab, 0)
    home = band >> 2

    def greet_home(k, carry):
        source = {"beam": (band + k) & (NB - 1), "slab": home}
        pl.semaphore_signal(
            barrier, inc=1, device_id=source, device_id_type=pl.DeviceIdType.MESH
        )
        return carry

    @pl.when(home != slab)
    def _():
        lax.fori_loop(1, NB, greet_home, 0)

    x_forward(px, xf1, xf2, msg1, buf)
    extra = 4 * (NS - 1) - jnp.where(home == slab, NS - 1, 0)
    pl.semaphore_wait(barrier, NB - 1 + NS - 1 + extra)

    def exchange1(k):
        target = (band + k) & (NB - 1)
        return remote(
            msg1.at[target], rows1.at[band], send1.at[target], recv1.at[band],
            {"beam": target, "slab": slab},
        )

    def arrival1(k):
        source = (band + k) & (NB - 1)
        return remote(
            msg1.at[source], rows1.at[source], send1.at[source], recv1.at[source],
            {"beam": source, "slab": slab},
        )

    lax.fori_loop(1, NB, lambda k, c: (exchange1(k).start(), c)[1], 0)
    rows1[band] = msg1[band]
    tables(jx, band, fresnel, twist)
    split_tiles(pot2, pairs)
    lax.fori_loop(1, NB, lambda k, c: (arrival1(k).wait_recv(), c)[1], 0)
    y_first(slab, rows1, yf1, cols.at[slab], buf, buf2)

    core = slab & 1
    right = (slab + 2) & (NS - 1)
    left = (slab + 6) & (NS - 1)
    far = (slab + 4) & (NS - 1)
    partner = slab ^ 1
    step = 1024 // AGC

    def gather(source, c, half, kind, target):
        begin = c * step + (step // 2 if half == 1 else 0)
        length = step if half is None else step // 2
        view = cols.at[source, pl.ds(begin, length), :]
        return remote(
            view, view, sendg.at[kind, c], recvg.at[source, c, 1 if half == 1 else 0],
            {"beam": band, "slab": target},
        )

    for c in range(AGC):
        gather(slab, c, None, 0, right).start()
        gather(slab, c, None, 1, left).start()
        gather(slab, c, None, 2, partner).start()
    for c in range(AGC):
        gather(left, c, None, 0, left).wait_recv()
        gather(left, c, 0, 3, right).start()
        gather(left, c, None, 4, partner).start()
        gather(right, c, None, 1, right).wait_recv()
        gather(right, c, 1, 5, left).start()
        gather(right, c, None, 6, partner).start()

    forward = forward_table(jy)
    for c in range(AGC):
        gather(far, c, 0, 3, left).wait_recv()
        gather(far, c, 1, 5, right).wait_recv()
        gather(far, c, None, 7, partner).start()
        for source in (partner, left ^ 1, right ^ 1, far ^ 1):
            gather(source, c, None, 2, partner).wait_recv()
        y_second(c * (A // AGC), forward, cols, yi1, fresnel, twist, buf)

    def exchange2(c, k):
        target = (band + k) & (NB - 1)
        return remote(
            msg2.at[c, target], rows2.at[c, band], send2.at[c, target], recv2.at[c, band],
            {"beam": target, "slab": slab},
        )

    def arrival2(c, k):
        source = (band + k) & (NB - 1)
        return remote(
            msg2.at[c, source], rows2.at[c, source], send2.at[c, source], recv2.at[c, source],
            {"beam": source, "slab": slab},
        )

    for c in range(AXC):
        y_third(c, yi2, msg2, buf, buf2)
        lax.fori_loop(1, NB, lambda k, z: (exchange2(c, k).start(), z)[1], 0)
        rows2[c, band] = msg2[c, band]

    table = inverse_table(jx)
    for c in range(AXC):
        lax.fori_loop(1, NB, lambda k, z: (arrival2(c, k).wait_recv(), z)[1], 0)
        x_second(c, table, rows2, buf)

    wanted = tiles_v[...]
    wanted = jnp.where((wanted >> 7) == band, wanted, 0).reshape(NB, NS, 4)
    wanted = jnp.sum(jnp.sum(wanted, axis=1), axis=1, keepdims=True)
    x_third(wanted, msg3, buf, buf2)

    def exchange3(k):
        target = (slab + k) & (NS - 1)
        return remote(
            msg3.at[target], parts.at[slab], send3.at[target], recv3.at[slab],
            {"beam": band, "slab": target},
        )

    def arrival3(k):
        source = (slab + k) & (NS - 1)
        return remote(
            msg3.at[source], parts.at[source], send3.at[source], recv3.at[source],
            {"beam": band, "slab": source},
        )

    lax.fori_loop(1, NS, lambda k, z: (exchange3(k).start(), z)[1], 0)
    parts[slab] = msg3[slab]
    ids = own_tiles(band, slab, tiles_s)
    alpha = probe_factors(ids, beams, shifts)
    lax.fori_loop(1, NS, lambda k, z: (arrival3(k).wait_recv(), z)[1], 0)
    detect(ids, alpha, parts, pairs, df1, df2, res, buf)

    def exchange4(l, p):
        group = 4 * slab + l
        return remote(
            res.at[l], sums.at[band], send4.at[l, p], recv4.at[band],
            {"beam": group, "slab": p},
        )

    def arrival4(source):
        return remote(
            res.at[0], sums.at[source], send4.at[0, 0], recv4.at[source],
            {"beam": source, "slab": home},
        )

    def each4(act):
        for l in range(4):

            def body(p, carry):
                @pl.when((4 * slab + l != band) | (p != slab))
                def _():
                    act(exchange4(l, p))

                return carry

            lax.fori_loop(0, NS, body, 0)

    each4(lambda copy: copy.start())

    @pl.when(home == slab)
    def _():
        sums[band] = res[band & 3]

    def finish(source, carry):
        @pl.when((source != band) | (home != slab))
        def _():
            arrival4(source).wait_recv()

        return carry

    lax.fori_loop(0, NB, finish, 0)
    block = band * NS + slab
    for k in range(4):
        row = sums[tiles_s[block, k] >> 7]
        row = jnp.where(k < counts[block], row, 0.0)
        for g in range(G):
            out[0, k, g : g + 1, :] = row[:, NDET * g : NDET * g + NDET]

    lax.fori_loop(1, NB, lambda k, z: (exchange1(k).wait_send(), z)[1], 0)
    for c in range(AGC):
        gather(slab, c, None, 0, right).wait_send()
        gather(slab, c, None, 1, left).wait_send()
        gather(slab, c, None, 2, partner).wait_send()
        gather(left, c, 0, 3, right).wait_send()
        gather(left, c, None, 4, partner).wait_send()
        gather(right, c, 1, 5, left).wait_send()
        gather(right, c, None, 6, partner).wait_send()
        gather(far, c, None, 7, partner).wait_send()
    for c in range(AXC):
        lax.fori_loop(1, NB, lambda k, z: (exchange2(c, k).wait_send(), z)[1], 0)
    lax.fori_loop(1, NS, lambda k, z: (exchange3(k).wait_send(), z)[1], 0)
    each4(lambda copy: copy.wait_send())


def shards(pot_first, pot_second, beam_index, aberration, tile_table, tile_count):
    slab = lax.axis_index("slab")
    tab = host_tables()
    px = lax.dynamic_slice_in_dim(pot_first.reshape(2, A, N), 8 * slab, 8, 1)
    px = px.reshape(16, A, A).transpose(1, 0, 2).reshape(A, 1024)
    names = ("xf1", "xf2", "yf1", "yi1", "yi2", "df1", "df2")
    args = (beam_index, aberration, tile_table, tile_count, tile_table, px, pot_second)
    args = args + tuple(tab[name] for name in names)
    specs = [pl.BlockSpec(memory_space=pltpu.SMEM if k < 4 else pltpu.VMEM) for k in range(len(args))]
    size = 4 * A // AXC
    dma = pltpu.SemaphoreType.DMA
    return pl.pallas_call(
        kernel,
        out_shape=jax.ShapeDtypeStruct((1, 4, G, NDET), F32),
        in_specs=specs,
        out_specs=pl.BlockSpec(memory_space=pltpu.VMEM),
        scratch_shapes=[
            pltpu.VMEM((A * 128, 128), F32),
            pltpu.VMEM((2048, 128), F32),
            pltpu.VMEM((64, A, 128), BF16),
            pltpu.VMEM((A, 2 * KY, 128), F32),
            pltpu.VMEM((A, 128, 128), F32),
            pltpu.VMEM((NB, 32, 128), BF16),
            pltpu.VMEM((NB, 32, 128), BF16),
            pltpu.VMEM((NS, 1024, 128), BF16),
            pltpu.VMEM((AXC, NB, size, 128), BF16),
            pltpu.VMEM((AXC, NB, size, 128), BF16),
            pltpu.VMEM((NS, 256, 128), BF16),
            pltpu.VMEM((NS, 256, 128), BF16),
            pltpu.VMEM((4, 1, 128), F32),
            pltpu.VMEM((NB, 1, 128), F32),
            dma((NB,)),
            dma((NB,)),
            dma((8, AGC)),
            dma((NS, AGC, 2)),
            dma((AXC, NB)),
            dma((AXC, NB)),
            dma((NS,)),
            dma((NS,)),
            dma((4, NS)),
            dma((NB,)),
        ],
        compiler_params=pltpu.CompilerParams(
            vmem_limit_bytes=50 * 1024 * 1024, collective_id=0, has_side_effects=True
        ),
    )(*args)


def solution(mesh):
    return jax.shard_map(
        shards,
        mesh=mesh,
        in_specs=(P("beam", None), P("beam", None), P(), P(), P(), P()),
        out_specs=P(("beam", "slab"), None, None, None),
        check_vma=False,
    )
```

time: 249 us -> 137 us (0.55)
  waiting for transfers between devices: 86.5 us -> 0 us
  Pallas kernels: 67.7 us -> 131 us
  blocking collectives: 46.3 us -> 0 us
  starting transfers between devices: 20.1 us -> 0 us
  between operations: 13.6 us -> 0.13 us
  local copies, waits for them, and re-layouts: 10.7 us -> 4.21 us
  other arithmetic: 3.41 us -> 0 us
    pallas_call x5 -> x1, Pallas kernels: 67.7 us -> 131 us  [shards(): pl.pallas_call(kernel, out_shape=jax.ShapeDtypeStruct((1, 4, G, NDET), F3...]
    all_to_all x3 -> x0, waiting for transfers between devices: 62 us -> none  [the longest x1 43.6 us: shards(): rows = lax.all_to_all(msg.reshape(NB, 256, 128), 'beam', 0, 0, tiled=True)]
    all_gather x1 -> x0, waiting for transfers between devices: 24.5 us -> none  [shards(): cols = lax.all_gather(piece, 'slab')]
    psum x1 -> x0, blocking collectives: 23.5 us -> none  [shards(): spread = lax.psum(spread, 'slab')]
    all_to_all x1 -> x0, blocking collectives: 22.7 us -> none  [shards(): rows = lax.all_to_all(msg.reshape(NB, 32, 128), 'beam', 0, 0, tiled=True)]
    all_to_all x3 -> x0, starting transfers between devices: 20.1 us -> none  [the longest x1 10.3 us: shards(): rows = lax.all_to_all(msg.reshape(NB, 256, 128), 'beam', 0, 0, tiled=True)]
    unnamed x34 -> x28, local copies, waits for them, and re-layouts: 5.76 us -> 2.99 us
  transfers between devices with their start and end apart: 4 -> 0, of which waited for: 4 -> 0; matrix products, arithmetic and copies ran while one was open for 3% -> 0% of each run, Pallas kernels for 0% -> 0%
where the time goes in v2:
time: 137 us; the launch traced here: 135 us
  Pallas kernels  131 us (96%)
  local copies, waits for them, and re-layouts  4.21 us (3%)
    pallas_call x1, Pallas kernels, shards(): pl.pallas_call(kernel, out_shape=jax.ShapeDtypeStruct((1, 4, G, NDET), F3...  131 us
    unnamed x28, local copies, waits for them, and re-layouts  2.99 us

profile of v2, /device:TPU:8, one launch (start us, length us, event | category | flops | bytes accessed | tf_op | source)
XLA Modules:
  0.0 135.4 jit_solution(7993630108475409378)
XLA Ops:
  0.0 0.0 copy-start
  0.0 0.0 copy-start.1
  0.0 1.2 copy-done
  1.2 0.2 reshape.10
  1.5 0.2 copy.18
  1.7 0.0 copy-start.11
  1.7 0.0 copy-start.3
  1.7 0.0 copy-start.4
  1.7 0.0 copy-start.5
  1.7 0.0 copy-start.6
  1.7 0.0 copy-start.7
  1.7 0.0 copy-start.8
  1.8 0.2 reshape.11.px
  2.0 0.4 copy-done.11
  2.4 0.0 copy-start.12
  2.4 0.0 copy-start.2
  2.4 0.1 copy.20.tiles_s.tiles_v
  2.5 0.5 copy-done.12
  3.0 0.0 copy-start.9
  3.0 0.0 copy-start.10
  3.0 0.1 copy.19.beams
  3.1 0.0 copy-done.1
  3.1 0.0 copy-done.3
  3.1 0.0 copy-done.4
  3.1 0.0 copy-done.5
  3.1 0.0 copy-done.6
  3.1 0.0 copy-done.7
  3.2 0.0 copy-done.8
  3.2 0.1 copy-done.2
  3.3 0.4 copy-done.9
  3.7 0.0 copy-done.10
  3.7 131.1 %shard_map.127 = f32[1,4,3,16]{3,2,1,0:T(4,128)S(1)} custom-call(s32[8,2]{1,0:T(8,128)S(1)} %copy.19.beams, f32[8]{0:T(128)S(1)} %copy-done.10, s32[256,4]{1,0:T(8,128)S(1)} %copy.20.tiles_s.tiles_v, s32[256]{0:T(256)S(1)} %copy-done.9, s32[256,4]{1,0:T(8,128)S(1)} %copy.20.tiles_s.tiles_v, bf16[64,1024]{1,0:T(8,128)(2,1)S(1)} %reshape.11.px, ...), custom_call_target="tpu_custom_call" | custom-call | tf_op jit(solution)/shard_map/pallas_call | solution.py:656
  134.8 0.6 copy.22
  (1 shorter events, 0.0 us)
Async XLA Ops:
  0.0 1.2 copy-start
  0.0 3.1 %copy-start.1 = (bf16[128,4096]{1,0:T(8,128)(2,1)S(1)}, bf16[128,4096]{1,0:T(8,128)(2,1)}, u32[]{:S(2)}) copy-start(bf16[128,4096]{1,0:T(8,128)(2,1)} %pot2.1) | copy-start | bytes 3145732
  1.7 0.7 copy-start.11
  1.7 1.4 %copy-start.3 = (bf16[128,128]{1,0:T(8,128)(2,1)S(1)}, bf16[128,128]{1,0:T(8,128)(2,1)}, u32[]{:S(2)}) copy-start(bf16[128,128]{1,0:T(8,128)(2,1)} %constant.24.clone.xf1) | copy-start | bytes 98308
  1.7 1.4 %copy-start.4 = (bf16[128,128]{1,0:T(8,128)(2,1)S(1)}, bf16[128,128]{1,0:T(8,128)(2,1)}, u32[]{:S(2)}) copy-start(bf16[128,128]{1,0:T(8,128)(2,1)} %constant.26.clone.yf1) | copy-start | bytes 98308
  1.7 1.4 %copy-start.5 = (bf16[128,96]{1,0:T(8,128)(2,1)S(1)}, bf16[128,96]{1,0:T(8,128)(2,1)}, u32[]{:S(2)}) copy-start(bf16[128,96]{1,0:T(8,128)(2,1)} %constant.27.clone.yi1) | copy-start | bytes 73732
  1.7 1.4 %copy-start.6 = (bf16[128,128]{1,0:T(8,128)(2,1)S(1)}, bf16[128,128]{1,0:T(8,128)(2,1)}, u32[]{:S(2)}) copy-start(bf16[128,128]{1,0:T(8,128)(2,1)} %constant.28.clone.yi2) | copy-start | bytes 98308
  1.7 1.4 %copy-start.7 = (bf16[128,128]{1,0:T(8,128)(2,1)S(1)}, bf16[128,128]{1,0:T(8,128)(2,1)}, u32[]{:S(2)}) copy-start(bf16[128,128]{1,0:T(8,128)(2,1)} %constant.29.clone.df1) | copy-start | bytes 98308
  1.7 1.4 %copy-start.8 = (bf16[128,64]{1,0:T(8,128)(2,1)S(1)}, bf16[128,64]{1,0:T(8,128)(2,1)}, u32[]{:S(2)}) copy-start(bf16[128,64]{1,0:T(8,128)(2,1)} %constant.30.clone.df2) | copy-start | bytes 49156
  2.4 0.7 copy-start.12
  2.4 0.9 copy-start.2
  3.0 0.7 copy-start.9
  3.0 0.7 copy-start.10

commit v3 on v2

v3 whole, which is shorter than its diff:
```python
import math

import jax
import jax.numpy as jnp
import numpy as np
from jax import lax
from jax.experimental import pallas as pl
from jax.experimental.pallas import tpu as pltpu
from jax.sharding import PartitionSpec as P

A = 64
N = 4096
F = 64
G = 3
NDET = 16
QMAX = 3
NB = 32
NS = 8
KY = 48
LOW = 24
SPARE = 20
F32 = jnp.float32
BF16 = jnp.bfloat16


def ring_counts():
    d = np.arange(A)
    signed = np.where(d < A // 2, d, d - A)
    radius = signed[:, None] ** 2 + signed[None, :] ** 2
    width = A // (2 * NDET)
    return [
        int(((radius >= (width * b) ** 2) & (radius < (width * (b + 1)) ** 2)).sum())
        for b in range(NDET)
    ]


def poly_sincos(r):
    t = r * r
    sine = r + r * t * (-1.6666667e-1 + t * (8.3333333e-3 + t * (-1.9841270e-4 + t * 2.7557319e-6)))
    cosine = 1.0 + t * (-0.5 + t * (4.1666667e-2 + t * (-1.3888889e-3 + t * 2.4801587e-5)))
    return sine, cosine


def place(sine, cosine, quadrant):
    swap = (quadrant & 1) == 1
    a = jnp.where(swap, cosine, sine)
    b = jnp.where(swap, sine, cosine)
    a = jnp.where((quadrant & 2) == 2, -a, a)
    b = jnp.where(((quadrant + 1) & 2) == 2, -b, b)
    return a, b


def sincos(x):
    k = jnp.floor(x * (2.0 / math.pi) + 0.5)
    r = (x - k * 1.5707963) - k * 2.6794897e-8
    sine, cosine = poly_sincos(r)
    return place(sine, cosine, k.astype(jnp.int32))


def sincos_int(m, period):
    shift = int(math.log2(period)) - 2
    quadrant = (m + (period >> 3)) >> shift
    r = (m - (quadrant << shift)).astype(F32) * (2.0 * math.pi / period)
    sine, cosine = poly_sincos(r)
    return place(sine, cosine, quadrant)


def dot(a, b):
    return jnp.dot(a, b, preferred_element_type=F32)


def iota(shape, axis):
    return lax.broadcasted_iota(jnp.int32, shape, axis)


def remote(src, dst, send, recv, target):
    return pltpu.make_async_remote_copy(
        src_ref=src,
        dst_ref=dst,
        send_sem=send,
        recv_sem=recv,
        device_id=target,
        device_id_type=pl.DeviceIdType.MESH,
    )


def swap(v):
    return pltpu.roll(v, A, 1)


def left_half():
    return iota((1, 128), 1) < A


def sign():
    return jnp.where(left_half(), 1.0, -1.0)


def table64(product):
    s, c = sincos_int(product & (A - 1), A)
    return c.astype(BF16).astype(F32), s.astype(BF16).astype(F32)


def stacked(product, scale):
    c, s = table64(product)
    return jnp.concatenate([c * scale, s * scale], axis=0).astype(BF16)


def x_tables():
    row = iota((128, 128), 0)
    col = iota((128, 128), 1)
    k1 = 2 * (row & 31) + ((row >> 5) & 1)
    blocks = []
    for rho in range(2):
        c, s = table64(k1 * (2 * (col & 31) + rho))
        same = (row >> 6) == ((col >> 5) & 1)
        blocks.append(jnp.where(same, c, jnp.where(row < A, s, -s)) * (1.0 / A))
    first = jnp.concatenate(blocks, axis=0)[:, :A].astype(BF16)
    lane = iota((A, 128), 1)
    c, s = table64(iota((A, 128), 0) * (lane & 63))
    left = lane < A
    zero = jnp.zeros((A, 128), F32)
    rows = []
    for block in (jnp.where(left, c, -s), jnp.where(left, s, c)):
        block = block * (1.0 / A)
        rows.append(jnp.concatenate([block, zero], axis=1))
        rows.append(jnp.concatenate([zero, block], axis=1))
    second = jnp.concatenate(rows, axis=0).astype(BF16)
    return first, second


def x_forward(slab, potential, out, buf):
    odd = (slab & 1) == 1
    for h in range(2):
        block = potential[h].astype(F32)
        block = jnp.where(odd, block[8:], block[:8])
        sine, cosine = sincos(block)
        for part, wave in enumerate((cosine, sine)):
            for p in range(32):
                start = h * 8 * A + part * 32 + p
                buf[pl.ds(start, 8, stride=A), :] = wave[:, 128 * p : 128 * p + 128]
    first, second = x_tables()
    row = iota((A, 128), 0)
    k1 = 2 * (row & 31) + (row >> 5)
    ts, tc = sincos_int(k1 * (iota((A, 128), 1) & 63), N)
    left = left_half()
    waves = [buf[A * r : A * r + A, :].astype(BF16) for r in range(16)]
    for t in range(8):
        y = dot(first, jnp.concatenate([waves[2 * t], waves[2 * t + 1]], axis=1))
        lines = []
        for k in range(2):
            both = y[:, 128 * k : 128 * k + 128]
            both = jnp.where(left, both[:128], both[128:])
            lines.append(both + swap(both))
        line = jnp.where(left, lines[0], lines[1])
        yr, yi = line[:A], line[A:]
        z = jnp.concatenate(
            [(yr * tc + yi * ts).astype(BF16), (yi * tc - yr * ts).astype(BF16)], axis=1
        )
        spec = dot(z, second)
        for k in range(2):
            r = 2 * t + k
            for q in range(2):
                start = (r >> 3) * 16 + q * 8 + (r & 7)
                buf[pl.ds(1024 + start, 32, stride=32), :] = spec[
                    32 * q : 32 * q + 32, 128 * k : 128 * k + 128
                ]
    for f in range(NB):
        out[f] = buf[1024 + 32 * f : 1056 + 32 * f, :].astype(BF16)


def tables(jx, band, fresnel, twist):
    lane = iota((KY, 128), 1)
    ky0 = A * (iota((KY, 128), 0) - LOW)
    b_row = iota((A, 128), 0)
    turn = sign()

    def step(k1, carry):
        fy = ky0 + k1
        for q in range(2):
            fx = ((2 * band + q + A * ((lane & 63) + jx) + N // 2) & (N - 1)) - N // 2
            total = fx * fx + fy * fy
            hs, hc = sincos_int(total, 2 * N)
            inside = total <= (N // 3) ** 2
            fresnel[q, k1, :KY, :] = jnp.where(inside, hc, 0.0)
            fresnel[q, k1, KY:, :] = jnp.where(inside, hs, 0.0) * turn
        ts, tc = sincos_int(b_row * k1, N)
        twist[k1, :A, :] = tc
        twist[k1, A:, :] = ts * turn
        return carry

    lax.fori_loop(0, A, step, 0, unroll=2)


def y_first(q, slab, out, buf, buf2):
    turn = sign()
    table = stacked(iota((A, A), 0) * iota((A, A), 1), 1.0 / A)
    for i in range(0, 8, 2):
        x = [buf[pl.ds(q * 8 + i + k, A, stride=16), :].astype(BF16) for k in range(2)]
        y = dot(table, jnp.concatenate(x, axis=1))
        for k in range(2):
            line = y[:, 128 * k : 128 * k + 128]
            line = line[:A] + swap(line[A:]) * turn
            ts, tc = sincos_int(iota((A, 128), 0) * (8 * slab + i + k), N)
            buf2[pl.ds(i + k, A, stride=8), :] = line * tc + swap(line) * (ts * turn)
    out[...] = buf2[0:512, :].astype(BF16)


def forward_table(jy):
    row = iota((KY, 128), 0)
    col = iota((KY, 128), 1)
    n2 = NS * (col >> 4) + (col & 7)
    c, s = table64(n2 * (row - LOW - jy))
    blocks = []
    for parity in range(2):
        keep = ((col >> 3) & 1) == parity
        blocks.append(jnp.where(keep, c, 0.0))
        blocks.append(jnp.where(keep, s, 0.0))
    return (jnp.concatenate(blocks, axis=0) * (1.0 / A)).astype(BF16)


def y_second(q, forward, cols, fresnel, twist, buf):
    turn = sign()
    c, s = table64(iota((A, KY), 0) * (iota((A, KY), 1) - LOW))
    back = jnp.concatenate([c, s], axis=0).astype(BF16)

    def step(pair, carry):
        at = pl.multiple_of(pair * 16, 16)
        x = jnp.concatenate([cols[q, p, pl.ds(at, 16), :] for p in range(NS)], axis=0)
        g = dot(forward, x)
        v = []
        for k in range(2):
            line = g[96 * k : 96 * k + KY] + swap(g[96 * k + KY : 96 * k + 96]) * turn
            hc, hs = fresnel[q, 2 * pair + k, :KY, :], fresnel[q, 2 * pair + k, KY:, :]
            v.append((line * hc + swap(line) * hs).astype(BF16))
        u = dot(back, jnp.concatenate(v, axis=1))
        for k in range(2):
            line = u[:, 128 * k : 128 * k + 128]
            line = line[:A] - swap(line[A:]) * turn
            tc, ts = twist[2 * pair + k, :A, :], twist[2 * pair + k, A:, :]
            buf[pl.ds(2 * pair + k, A, stride=A), :] = line * tc - swap(line) * ts
        return carry

    lax.fori_loop(0, A // 2, step, 0, unroll=4)


def spare_lanes(jx):
    return ((iota((1, 128), 1) - (22 - jx)) & 63) < SPARE


def y_third(q, half, jx, out, buf, buf2):
    turn = sign()
    row = iota((A, A), 0)
    table = stacked((2 * (row & 31) + (row >> 5)) * iota((A, A), 1), 1.0)
    gap = spare_lanes(jx)

    def step(g, carry):
        lines = []
        for k in range(2):
            at = pl.multiple_of((32 * half + 4 * g + 2 * k) * A, 128)
            z = buf[pl.ds(at, 128), :].astype(BF16)
            w = dot(table, jnp.concatenate([z[:A], z[A:]], axis=1))
            for m in range(2):
                line = w[:, 128 * m : 128 * m + 128]
                lines.append(line[:A] - swap(line[A:]) * turn)
        for m in range(3):
            line = jnp.where(gap, pltpu.roll(lines[3], 128 - SPARE * (m + 1), 1), lines[m])
            for h in range(2):
                buf2[pl.ds(16 * m + 8 * h + g, NB, stride=48), :] = line[32 * h : 32 * h + 32]
        return carry

    lax.fori_loop(0, 8, step, 0, unroll=2)

    def pack(f, carry):
        out[q, half, f] = buf2[pl.ds(pl.multiple_of(f * 48, 16), 48), :].astype(BF16)
        return carry

    lax.fori_loop(0, NB, pack, 0, unroll=4)


def inverse_table(jx):
    lane = iota((A, 128), 1)
    c, s = table64((iota((A, 128), 0) + jx) * (lane & 63))
    left = lane < A
    whole = jnp.concatenate([jnp.where(left, c, s), jnp.where(left, -s, c)], axis=0)
    gap = ((iota((128, 128), 0) - (22 - jx)) & 63) < SPARE
    whole = jnp.where(gap, 0.0, whole)
    zero = jnp.zeros((128, 128), F32)
    rows = []
    for m in range(3):
        fourth = jnp.where(gap, pltpu.roll(whole, 128 - SPARE * (m + 1), 0), 0.0)
        rows.append(
            jnp.concatenate([whole if k == m else zero for k in range(3)] + [fourth], axis=1)
        )
    return jnp.concatenate(rows, axis=0).astype(BF16)


def x_second(q, half, table, rows, buf):
    lane = iota((8, 128), 1)
    turn = sign()

    def step(group, carry):
        lhs = []
        for k in range(4):
            block = rows[q, half, 4 * group + k]
            lhs.append(jnp.concatenate([block[16 * m : 16 * m + 16] for m in range(3)], axis=1))
        u = dot(jnp.concatenate(lhs, axis=0), table)
        for k in range(4):
            k1 = 2 * (4 * group + k) + q
            ts, tc = sincos_int(k1 * (lane & 63), N)
            ts, tc = ts[:1] * turn, tc[:1]
            for m in range(4):
                line = u[16 * k : 16 * k + 16, 128 * m : 128 * m + 128]
                line = line * tc - swap(line) * ts
                for h in range(2):
                    start = (32 * half + m) * 128 + h * A + k1
                    buf[pl.ds(start, 8, stride=512), :] = line[8 * h : 8 * h + 8]
        return carry

    lax.fori_loop(0, 8, step, 0, unroll=2)


def tile_table(ids):
    col = iota((NB, 128), 1)
    ids = jnp.broadcast_to(ids, (NB, 128))
    c, s = table64((col & 63) * (ids & 63))
    keep = ((ids >> 6) & 1) == (col >> 6)
    return jnp.concatenate([jnp.where(keep, c, 0.0), jnp.where(keep, s, 0.0)], axis=0).astype(BF16)


def x_third(half, table, out, buf, buf2):
    turn = sign()

    def step(pair, carry):
        at = pl.multiple_of((32 * half + 2 * pair) * 128, 256)
        z = buf[pl.ds(at, 256), :].astype(BF16)
        o = dot(table, jnp.concatenate([z[:128], z[128:]], axis=1))
        for k in range(2):
            line = o[:, 128 * k : 128 * k + 128]
            buf2[pl.ds(2 * pair + k, NB, stride=32), :] = line[:32] - swap(line[32:]) * turn
        return carry

    lax.fori_loop(0, 16, step, 0, unroll=4)
    for p in range(NS):
        out[half, p] = buf2[128 * p : 128 * p + 128, :].astype(BF16)


def own_tiles(band, slab, tiles):
    found = []
    for l in range(4):
        ident = jnp.int32(0)
        for q in range(NS):
            for k in range(4):
                value = tiles[(4 * slab + l) * NS + q, k]
                ident = ident + jnp.where((value >> 7) == band, value, 0)
        found.append(ident)
    return found


def probe_factors(ids, beams, shifts):
    sub = iota((8, 128), 0)
    lane = iota((8, 128), 1)
    by = jnp.zeros((8, 128), jnp.int32)
    bx = jnp.zeros((8, 128), jnp.int32)
    ab = jnp.zeros((8, 128), F32)
    for j in range(8):
        by = jnp.where(sub == j, beams[j, 0], by)
        bx = jnp.where(sub == j, beams[j, 1], bx)
        ab = jnp.where(sub == j, shifts[j], ab)
    ry = jnp.zeros((8, 128), jnp.int32)
    rx = jnp.zeros((8, 128), jnp.int32)
    for l in range(4):
        for g in range(G):
            here = lane == l * G + g
            ry = jnp.where(here, (ids[l] >> 6) * A + A // 2 + g, ry)
            rx = jnp.where(here, (ids[l] & 63) * A + A // 2 + 2 * g, rx)
    m = (F * (by * ry + bx * rx)) & (N - 1)
    s, c = sincos(ab + 2.0 * math.pi / N * m.astype(F32))
    return c, -s


def split_tiles(pot, out):
    for h in range(2):
        for pair in range(32):
            out[32 * h + pair] = pot[A * h : A * h + A, 128 * pair : 128 * pair + 128]


def detect(ids, alpha, parts, pot, out, buf):
    left = iota((A, 128), 1) < A
    turn = sign()
    lane = iota((A, 128), 1)
    c, s = table64(iota((A, 128), 0) * (lane & 63))
    along_x = jnp.concatenate([jnp.where(left, c, -s), jnp.where(left, s, c)], axis=0)
    along_x = (along_x * (1.0 / A)).astype(BF16)
    along_y = stacked(iota((A, A), 0) * iota((A, A), 1), 1.0 / A)
    ky = iota((A, 128), 0)
    kx = iota((A, 128), 1) & 63
    ky = jnp.where(ky < 32, ky, ky - A)
    kx = jnp.where(kx < 32, kx, kx - A)
    radius = ky * ky + kx * kx
    counts = ring_counts()
    width = A // (2 * NDET)
    ones = jnp.ones((8, 128), F32)
    for l in range(4):
        ident = ids[l]
        tile = pot[((ident & 127) >> 1)].astype(F32)
        odd = (ident & 1) == 1
        tile = jnp.where(left != odd, tile, swap(tile))
        ps, pc = sincos(tile)
        ps = ps * turn
        fields = [
            jnp.concatenate(
                [parts[h, j, 32 * l : 32 * l + 32, :].astype(F32) for h in range(2)], axis=0
            )
            for j in range(8)
        ]
        swapped = [swap(f) * turn for f in fields]
        for g in range(G):
            probe = jnp.zeros((A, 128), F32)
            at = l * G + g
            for j in range(8):
                probe = (
                    probe
                    + fields[j] * alpha[0][j : j + 1, at : at + 1]
                    - swapped[j] * alpha[1][j : j + 1, at : at + 1]
                )
            probe = probe * pc - swap(probe) * ps
            d = dot(probe.astype(BF16), along_x).astype(BF16)
            w = dot(along_y, d)
            value = w[:A] + swap(w[A:]) * turn
            power = value * value
            for b in range(NDET):
                member = (radius >= (width * b) ** 2) & (radius < (width * (b + 1)) ** 2)
                part = jnp.where(member, power, 0.0) * (A * A / (8.0 * counts[b]))
                buf[g * NDET + b : g * NDET + b + 1, :] = jnp.sum(part, axis=0, keepdims=True)
        total = lax.dot_general(
            ones,
            buf[0:128, :],
            (((1,), (1,)), ((), ())),
            precision=lax.Precision.HIGHEST,
            preferred_element_type=F32,
        )
        out[l] = total[:1]


def kernel(
    beams,
    shifts,
    tiles_s,
    counts,
    tiles_v,
    pot1_hbm,
    pot2_hbm,
    out,
    pot1,
    pot2,
    buf,
    buf2,
    buf3,
    pairs,
    fresnel,
    twist,
    msg1,
    rows1,
    cols,
    msg2,
    rows2,
    msg3,
    parts,
    res,
    sums,
    load,
    send1,
    recv1,
    sendg,
    recvg,
    send2,
    recv2,
    send3,
    recv3,
    send4,
    recv4,
):
    band = lax.axis_index("beam")
    slab = lax.axis_index("slab")
    jy = beams[slab, 0]
    jx = beams[slab, 1]
    loads = [
        pltpu.make_async_copy(
            pot1_hbm.at[pl.ds(pl.multiple_of(A * h + 16 * (slab >> 1), 16), 16), :],
            pot1.at[h],
            load.at[h],
        )
        for h in range(2)
    ]
    loads.append(pltpu.make_async_copy(pot2_hbm, pot2, load.at[2]))
    for copy in loads:
        copy.start()
    barrier = pltpu.get_barrier_semaphore()

    def greet(target):
        pl.semaphore_signal(
            barrier, inc=1, device_id=target, device_id_type=pl.DeviceIdType.MESH
        )

    def greet_beam(k, carry):
        greet({"beam": (band + k) & (NB - 1), "slab": slab})
        return carry

    lax.fori_loop(1, NB, greet_beam, 0)

    def greet_slab(k, carry):
        greet({"beam": band, "slab": (slab + k) & (NS - 1)})
        return carry

    lax.fori_loop(1, NS, greet_slab, 0)
    home = band >> 2

    def greet_home(k, carry):
        greet({"beam": (band + k) & (NB - 1), "slab": home})
        return carry

    @pl.when(home != slab)
    def _():
        lax.fori_loop(1, NB, greet_home, 0)

    loads[0].wait()
    loads[1].wait()
    x_forward(slab, pot1, msg1, buf)
    extra = 4 * (NS - 1) - jnp.where(home == slab, NS - 1, 0)
    pl.semaphore_wait(barrier, NB - 1 + NS - 1 + extra)

    def exchange1(k):
        target = (band + k) & (NB - 1)
        return remote(
            msg1.at[target], rows1.at[band], send1.at[target], recv1.at[band],
            {"beam": target, "slab": slab},
        )

    def arrival1(k):
        source = (band + k) & (NB - 1)
        return remote(
            msg1.at[source], rows1.at[source], send1.at[source], recv1.at[source],
            {"beam": source, "slab": slab},
        )

    lax.fori_loop(1, NB, lambda k, c: (exchange1(k).start(), c)[1], 0)
    rows1[band] = msg1[band]
    tables(jx, band, fresnel, twist)
    loads[2].wait()
    split_tiles(pot2, pairs)
    wanted = tiles_v[...]
    wanted = jnp.where((wanted >> 7) == band, wanted, 0).reshape(NB, NS, 4)
    wanted = jnp.sum(jnp.sum(wanted, axis=1), axis=1, keepdims=True)
    tile_tab = tile_table(wanted)
    ids = own_tiles(band, slab, tiles_s)
    forward = forward_table(jy)
    inverse = inverse_table(jx)
    lax.fori_loop(1, NB, lambda k, c: (arrival1(k).wait_recv(), c)[1], 0)

    right = (slab + 2) & (NS - 1)
    left = (slab + 6) & (NS - 1)
    far = (slab + 4) & (NS - 1)
    partner = slab ^ 1

    def gather(source, q, half, kind, target):
        begin = 256 if half == 1 else 0
        length = 512 if half is None else 256
        view = cols.at[q, source, pl.ds(begin, length), :]
        return remote(
            view, view, sendg.at[kind, q], recvg.at[source, q, 1 if half == 1 else 0],
            {"beam": band, "slab": target},
        )

    for f in range(NB):
        buf[32 * f : 32 * f + 32, :] = rows1[f].astype(F32)
    for q in range(2):
        y_first(q, slab, cols.at[q, slab], buf, buf2)
        gather(slab, q, None, 0, right).start()
        gather(slab, q, None, 1, left).start()
        gather(slab, q, None, 2, partner).start()

    def near(q):
        gather(left, q, None, 0, left).wait_recv()
        gather(left, q, 0, 3, right).start()
        gather(left, q, None, 4, partner).start()
        gather(right, q, None, 1, right).wait_recv()
        gather(right, q, 1, 5, left).start()
        gather(right, q, None, 6, partner).start()

    def distant(q):
        gather(far, q, 0, 3, left).wait_recv()
        gather(far, q, 1, 5, right).wait_recv()
        gather(far, q, None, 7, partner).start()

    def across(q):
        for source in (partner, left ^ 1, right ^ 1, far ^ 1):
            gather(source, q, None, 2, partner).wait_recv()

    def exchange2(q, half, k):
        target = (band + k) & (NB - 1)
        return remote(
            msg2.at[q, half, target], rows2.at[q, half, band],
            send2.at[2 * q + half, target], recv2.at[2 * q + half, band],
            {"beam": target, "slab": slab},
        )

    def arrival2(q, half, k):
        source = (band + k) & (NB - 1)
        return remote(
            msg2.at[q, half, source], rows2.at[q, half, source],
            send2.at[2 * q + half, source], recv2.at[2 * q + half, source],
            {"beam": source, "slab": slab},
        )

    def send_rows(q, half):
        y_third(q, half, jx, msg2, buf, buf2)
        lax.fori_loop(1, NB, lambda k, z: (exchange2(q, half, k).start(), z)[1], 0)
        rows2[q, half, band] = msg2[q, half, band]

    near(0)
    distant(0)
    across(0)
    y_second(0, forward, cols, fresnel, twist, buf)
    near(1)
    send_rows(0, 0)
    distant(1)
    send_rows(0, 1)
    across(1)
    y_second(1, forward, cols, fresnel, twist, buf)
    send_rows(1, 0)
    send_rows(1, 1)

    def exchange3(half, k):
        target = (slab + k) & (NS - 1)
        return remote(
            msg3.at[half, target], parts.at[half, slab],
            send3.at[half, target], recv3.at[half, slab],
            {"beam": band, "slab": target},
        )

    def arrival3(half, k):
        source = (slab + k) & (NS - 1)
        return remote(
            msg3.at[half, source], parts.at[half, source],
            send3.at[half, source], recv3.at[half, source],
            {"beam": band, "slab": source},
        )

    alpha = probe_factors(ids, beams, shifts)
    for q in range(2):
        for half in range(2):
            lax.fori_loop(1, NB, lambda k, z: (arrival2(q, half, k).wait_recv(), z)[1], 0)
            x_second(q, half, inverse, rows2, buf3)
            if q == 1:
                x_third(half, tile_tab, msg3, buf3, buf2)
                lax.fori_loop(1, NS, lambda k, z: (exchange3(half, k).start(), z)[1], 0)
                parts[half, slab] = msg3[half, slab]
    for half in range(2):
        lax.fori_loop(1, NS, lambda k, z: (arrival3(half, k).wait_recv(), z)[1], 0)
    detect(ids, alpha, parts, pairs, res, buf)

    def exchange4(l, p):
        group = 4 * slab + l
        return remote(
            res.at[l], sums.at[band], send4.at[l, p], recv4.at[band],
            {"beam": group, "slab": p},
        )

    def arrival4(source):
        return remote(
            res.at[0], sums.at[source], send4.at[0, 0], recv4.at[source],
            {"beam": source, "slab": home},
        )

    def each4(act):
        for l in range(4):

            def body(p, carry):
                @pl.when((4 * slab + l != band) | (p != slab))
                def _():
                    act(exchange4(l, p))

                return carry

            lax.fori_loop(0, NS, body, 0)

    each4(lambda copy: copy.start())

    @pl.when(home == slab)
    def _():
        sums[band] = res[band & 3]

    def finish(source, carry):
        @pl.when((source != band) | (home != slab))
        def _():
            arrival4(source).wait_recv()

        return carry

    lax.fori_loop(0, NB, finish, 0)
    block = band * NS + slab
    for k in range(4):
        row = sums[tiles_s[block, k] >> 7]
        row = jnp.where(k < counts[block], row, 0.0)
        for g in range(G):
            out[0, k, g : g + 1, :] = row[:, NDET * g : NDET * g + NDET]

    lax.fori_loop(1, NB, lambda k, z: (exchange1(k).wait_send(), z)[1], 0)
    for q in range(2):
        gather(slab, q, None, 0, right).wait_send()
        gather(slab, q, None, 1, left).wait_send()
        gather(slab, q, None, 2, partner).wait_send()
        gather(left, q, 0, 3, right).wait_send()
        gather(left, q, None, 4, partner).wait_send()
        gather(right, q, 1, 5, left).wait_send()
        gather(right, q, None, 6, partner).wait_send()
        gather(far, q, None, 7, partner).wait_send()
        for half in range(2):
            lax.fori_loop(1, NB, lambda k, z: (exchange2(q, half, k).wait_send(), z)[1], 0)
    for half in range(2):
        lax.fori_loop(1, NS, lambda k, z: (exchange3(half, k).wait_send(), z)[1], 0)
    each4(lambda copy: copy.wait_send())


def shards(pot_first, pot_second, beam_index, aberration, tile_table, tile_count):
    args = (beam_index, aberration, tile_table, tile_count, tile_table, pot_first, pot_second)
    spaces = [pltpu.SMEM] * 4 + [pltpu.VMEM] + [pl.ANY] * 2
    dma = pltpu.SemaphoreType.DMA
    return pl.pallas_call(
        kernel,
        out_shape=jax.ShapeDtypeStruct((1, 4, G, NDET), F32),
        in_specs=[pl.BlockSpec(memory_space=space) for space in spaces],
        out_specs=pl.BlockSpec(memory_space=pltpu.VMEM),
        scratch_shapes=[
            pltpu.VMEM((2, 16, N), BF16),
            pltpu.VMEM((128, N), BF16),
            pltpu.VMEM((A * A, 128), F32),
            pltpu.VMEM((1536, 128), F32),
            pltpu.VMEM((A * 128, 128), F32),
            pltpu.VMEM((64, A, 128), BF16),
            pltpu.VMEM((2, A, 2 * KY, 128), F32),
            pltpu.VMEM((A, 128, 128), F32),
            pltpu.VMEM((NB, 32, 128), BF16),
            pltpu.VMEM((NB, 32, 128), BF16),
            pltpu.VMEM((2, NS, 512, 128), BF16),
            pltpu.VMEM((2, 2, NB, 48, 128), BF16),
            pltpu.VMEM((2, 2, NB, 48, 128), BF16),
            pltpu.VMEM((2, NS, 128, 128), BF16),
            pltpu.VMEM((2, NS, 128, 128), BF16),
            pltpu.VMEM((4, 1, 128), F32),
            pltpu.VMEM((NB, 1, 128), F32),
            dma((3,)),
            dma((NB,)),
            dma((NB,)),
            dma((8, 2)),
            dma((NS, 2, 2)),
            dma((4, NB)),
            dma((4, NB)),
            dma((2, NS)),
            dma((2, NS)),
            dma((4, NS)),
            dma((NB,)),
        ],
        compiler_params=pltpu.CompilerParams(
            vmem_limit_bytes=50 * 1024 * 1024, collective_id=0, has_side_effects=True
        ),
    )(*args)


def solution(mesh):
    return jax.shard_map(
        shards,
        mesh=mesh,
        in_specs=(P("beam", None), P("beam", None), P(), P(), P(), P()),
        out_specs=P(("beam", "slab"), None, None, None),
        check_vma=False,
    )
```

time: 137 us -> 112 us (0.82)
  Pallas kernels: 131 us -> 106 us
    pallas_call x1, Pallas kernels: 131 us -> 106 us  [shards(): pl.pallas_call(kernel, out_shape=jax.ShapeDtypeStruct((1, 4, G, NDET), F3...]
    unnamed x28 -> x12, local copies, waits for them, and re-layouts: 2.99 us -> 3.89 us
where the time goes in v3:
time: 112 us; the launch traced here: 111 us
  Pallas kernels  106 us (95%)
  local copies, waits for them, and re-layouts  4.49 us (4%)
    pallas_call x1, Pallas kernels, shards(): pl.pallas_call(kernel, out_shape=jax.ShapeDtypeStruct((1, 4, G, NDET), F3...  106 us
    unnamed x12, local copies, waits for them, and re-layouts  3.89 us

profile of v3, /device:TPU:8, one launch (start us, length us, event | category | flops | bytes accessed | tf_op | source)
XLA Modules:
  0.0 110.5 jit_solution(627562490207534173)
XLA Ops:
  0.0 0.0 copy-start.4
  0.0 0.8 copy.7.beams
  0.8 0.0 copy-done.4
  0.8 0.0 copy-start.2
  0.8 0.0 copy-start.3
  0.8 0.1 copy.8.tiles_s.tiles_v
  0.9 0.5 copy-done.2
  1.5 0.0 copy-done.3
  1.5 0.0 copy-start
  1.5 1.2 %copy-done = bf16[128,4096]{1,0:T(8,128)(2,1)S(1)} copy-done((bf16[128,4096]{1,0:T(8,128)(2,1)S(1)}, bf16[128,4096]{1,0:T(8,128)(2,1)}, u32[]{:S(2)}) %copy-start) | copy-done | bytes 1048600
  2.7 0.0 copy-start.1
  2.7 1.2 %copy-done.1 = bf16[128,4096]{1,0:T(8,128)(2,1)S(1)} copy-done((bf16[128,4096]{1,0:T(8,128)(2,1)S(1)}, bf16[128,4096]{1,0:T(8,128)(2,1)}, u32[]{:S(2)}) %copy-start.1) | copy-done | bytes 1048600
  3.9 106.0 %shard_map.64 = f32[1,4,3,16]{3,2,1,0:T(4,128)S(1)} custom-call(s32[8,2]{1,0:T(8,128)S(1)} %copy.7.beams, f32[8]{0:T(128)S(1)} %copy-done.3, s32[256,4]{1,0:T(8,128)S(1)} %copy.8.tiles_s.tiles_v, s32[256]{0:T(256)S(1)} %copy-done.2, s32[256,4]{1,0:T(8,128)S(1)} %copy.8.tiles_s.tiles_v, bf16[128,4096]{1,0:T(8,128)(2,1)S(1)} %copy-done, ...), custom_call_target="tpu_custom_call" | custom-call | tf_op jit(solution)/shard_map/pallas_call | solution.py:730
  109.9 0.6 copy.10
Async XLA Ops:
  0.0 0.8 copy-start.4
  0.8 0.7 copy-start.2
  0.8 0.7 copy-start.3
  1.5 1.2 %copy-start = (bf16[128,4096]{1,0:T(8,128)(2,1)S(1)}, bf16[128,4096]{1,0:T(8,128)(2,1)}, u32[]{:S(2)}) copy-start(bf16[128,4096]{1,0:T(8,128)(2,1)} %pot1_hbm.1) | copy-start | bytes 3145732
  2.7 1.2 %copy-start.1 = (bf16[128,4096]{1,0:T(8,128)(2,1)S(1)}, bf16[128,4096]{1,0:T(8,128)(2,1)}, u32[]{:S(2)}) copy-start(bf16[128,4096]{1,0:T(8,128)(2,1)} %pot2_hbm.1) | copy-start | bytes 3145732

commit v4 on v3

v4 whole, which is shorter than its diff:
```python
import math

import jax
import jax.numpy as jnp
import numpy as np
from jax import lax
from jax.experimental import pallas as pl
from jax.experimental.pallas import tpu as pltpu
from jax.sharding import PartitionSpec as P

A = 64
N = 4096
F = 64
G = 3
NDET = 16
QMAX = 3
NB = 32
NS = 8
KY = 48
LOW = 24
SPARE = 20
F32 = jnp.float32
BF16 = jnp.bfloat16


def ring_counts():
    d = np.arange(A)
    signed = np.where(d < A // 2, d, d - A)
    radius = signed[:, None] ** 2 + signed[None, :] ** 2
    width = A // (2 * NDET)
    return [
        int(((radius >= (width * b) ** 2) & (radius < (width * (b + 1)) ** 2)).sum())
        for b in range(NDET)
    ]


def poly_sincos(r):
    t = r * r
    sine = r + r * t * (-1.6666667e-1 + t * (8.3333333e-3 + t * (-1.9841270e-4 + t * 2.7557319e-6)))
    cosine = 1.0 + t * (-0.5 + t * (4.1666667e-2 + t * (-1.3888889e-3 + t * 2.4801587e-5)))
    return sine, cosine


def place(sine, cosine, quadrant):
    swap = (quadrant & 1) == 1
    a = jnp.where(swap, cosine, sine)
    b = jnp.where(swap, sine, cosine)
    a = jnp.where((quadrant & 2) == 2, -a, a)
    b = jnp.where(((quadrant + 1) & 2) == 2, -b, b)
    return a, b


def sincos(x):
    k = jnp.floor(x * (2.0 / math.pi) + 0.5)
    r = (x - k * 1.5707963) - k * 2.6794897e-8
    sine, cosine = poly_sincos(r)
    return place(sine, cosine, k.astype(jnp.int32))


def sincos_int(m, period):
    shift = int(math.log2(period)) - 2
    quadrant = (m + (period >> 3)) >> shift
    r = (m - (quadrant << shift)).astype(F32) * (2.0 * math.pi / period)
    sine, cosine = poly_sincos(r)
    return place(sine, cosine, quadrant)


def dot(a, b):
    return jnp.dot(a, b, preferred_element_type=F32)


def iota(shape, axis):
    return lax.broadcasted_iota(jnp.int32, shape, axis)


def remote(src, dst, send, recv, target):
    return pltpu.make_async_remote_copy(
        src_ref=src,
        dst_ref=dst,
        send_sem=send,
        recv_sem=recv,
        device_id=target,
        device_id_type=pl.DeviceIdType.MESH,
    )


def swap(v):
    return pltpu.roll(v, A, 1)


def left_half():
    return iota((1, 128), 1) < A


def sign():
    return jnp.where(left_half(), 1.0, -1.0)


def table64(product):
    s, c = sincos_int(product & (A - 1), A)
    return c.astype(BF16).astype(F32), s.astype(BF16).astype(F32)


def stacked(product, scale):
    c, s = table64(product)
    return jnp.concatenate([c * scale, s * scale], axis=0).astype(BF16)


def x_tables():
    row = iota((128, 128), 0)
    col = iota((128, 128), 1)
    k1 = 2 * (row & 31) + ((row >> 5) & 1)
    blocks = []
    for rho in range(2):
        c, s = table64(k1 * (2 * (col & 31) + rho))
        same = (row >> 6) == ((col >> 5) & 1)
        blocks.append(jnp.where(same, c, jnp.where(row < A, s, -s)) * (1.0 / A))
    first = jnp.concatenate(blocks, axis=0)[:, :A].astype(BF16)
    lane = iota((A, 128), 1)
    c, s = table64(iota((A, 128), 0) * (lane & 63))
    left = lane < A
    zero = jnp.zeros((A, 128), F32)
    rows = []
    for block in (jnp.where(left, c, -s), jnp.where(left, s, c)):
        block = block * (1.0 / A)
        rows.append(jnp.concatenate([block, zero], axis=1))
        rows.append(jnp.concatenate([zero, block], axis=1))
    second = jnp.concatenate(rows, axis=0).astype(BF16)
    return first, second


def x_forward(slab, potential, out, buf):
    odd = (slab & 1) == 1
    for h in range(2):
        block = potential[h].astype(F32)
        block = jnp.where(odd, block[8:], block[:8])
        sine, cosine = sincos(block)
        for part, wave in enumerate((cosine, sine)):
            for p in range(32):
                start = h * 8 * A + part * 32 + p
                buf[pl.ds(start, 8, stride=A), :] = wave[:, 128 * p : 128 * p + 128]
    first, second = x_tables()
    row = iota((A, 128), 0)
    k1 = 2 * (row & 31) + (row >> 5)
    ts, tc = sincos_int(k1 * (iota((A, 128), 1) & 63), N)
    left = left_half()
    waves = [buf[A * r : A * r + A, :].astype(BF16) for r in range(16)]
    for t in range(8):
        y = dot(first, jnp.concatenate([waves[2 * t], waves[2 * t + 1]], axis=1))
        lines = []
        for k in range(2):
            both = y[:, 128 * k : 128 * k + 128]
            both = jnp.where(left, both[:128], both[128:])
            lines.append(both + swap(both))
        line = jnp.where(left, lines[0], lines[1])
        yr, yi = line[:A], line[A:]
        z = jnp.concatenate(
            [(yr * tc + yi * ts).astype(BF16), (yi * tc - yr * ts).astype(BF16)], axis=1
        )
        spec = dot(z, second)
        for k in range(2):
            r = 2 * t + k
            for q in range(2):
                buf[pl.ds(1024 + 512 * q + r, 32, stride=16), :] = spec[
                    32 * q : 32 * q + 32, 128 * k : 128 * k + 128
                ]
    for q in range(2):
        for f in range(NB):
            start = 1024 + 512 * q + 16 * f
            out[q, f] = buf[start : start + 16, :].astype(BF16)


def tables(jx, band, fresnel, twist):
    lane = iota((KY, 128), 1)
    ky0 = A * (iota((KY, 128), 0) - LOW)
    b_row = iota((A, 128), 0)

    def step(k1, carry):
        fy = ky0 + k1
        for q in range(2):
            fx = ((2 * band + q + A * ((lane & 63) + jx) + N // 2) & (N - 1)) - N // 2
            total = fx * fx + fy * fy
            hs, hc = sincos_int(total, 2 * N)
            inside = total <= (N // 3) ** 2
            fresnel[q, k1, :KY, :] = jnp.where(inside, hc, 0.0)
            fresnel[q, k1, KY:, :] = jnp.where(inside, hs, 0.0)
        ts, tc = sincos_int(b_row * k1, N)
        twist[k1, :A, :] = tc
        twist[k1, A:, :] = ts
        return carry

    lax.fori_loop(0, A, step, 0, unroll=2)


def y_first(slab, out, buf, buf2):
    turn = sign()
    table = stacked(iota((A, A), 0) * iota((A, A), 1), 1.0 / A)
    for i in range(0, 8, 2):
        x = [buf[pl.ds(i + k, A, stride=8), :].astype(BF16) for k in range(2)]
        y = dot(table, jnp.concatenate(x, axis=1))
        for k in range(2):
            line = y[:, 128 * k : 128 * k + 128]
            line = line[:A] + swap(line[A:]) * turn
            ts, tc = sincos_int(iota((A, 128), 0) * (8 * slab + i + k), N)
            buf2[pl.ds(i + k, A, stride=8), :] = line * tc + swap(line) * (ts * turn)
    out[...] = buf2[0:512, :].astype(BF16)


def forward_table(jy):
    row = iota((KY, 128), 0)
    col = iota((KY, 128), 1)
    n2 = NS * (col >> 4) + (col & 7)
    c, s = table64(n2 * (row - LOW - jy))
    blocks = []
    for parity in range(2):
        keep = ((col >> 3) & 1) == parity
        pc = jnp.where(keep, c, 0.0)
        ps = jnp.where(keep, s, 0.0)
        blocks.append(jnp.concatenate([pc, -ps], axis=1))
        blocks.append(jnp.concatenate([ps, pc], axis=1))
    return (jnp.concatenate(blocks, axis=0) * (1.0 / A)).astype(BF16)


def y_second(q, forward, cols, fresnel, twist, buf):
    turn = sign().astype(BF16)
    c, s = table64(iota((A, KY), 0) * (iota((A, KY), 1) - LOW))
    back = jnp.concatenate(
        [jnp.concatenate([c, s], axis=1), jnp.concatenate([-s, c], axis=1)], axis=0
    ).astype(BF16)

    def step(pair, carry):
        at = pl.multiple_of(pair * 16, 16)
        x = jnp.concatenate([cols[q, p, pl.ds(at, 16), :] for p in range(NS)], axis=0)
        g = dot(forward, jnp.concatenate([x, swap(x) * -turn], axis=0))
        v = []
        for k in range(2):
            line, turned = g[96 * k : 96 * k + KY], g[96 * k + KY : 96 * k + 96]
            hc, hs = fresnel[q, 2 * pair + k, :KY, :], fresnel[q, 2 * pair + k, KY:, :]
            both = [line * hc - turned * hs, turned * hc + line * hs]
            v.append(jnp.concatenate(both, axis=0).astype(BF16))
        u = dot(back, jnp.concatenate(v, axis=1))
        for k in range(2):
            line, turned = u[:A, 128 * k : 128 * k + 128], u[A:, 128 * k : 128 * k + 128]
            tc, ts = twist[2 * pair + k, :A, :], twist[2 * pair + k, A:, :]
            buf[pl.ds(2 * pair + k, A, stride=128), :] = line * tc + turned * ts
            buf[pl.ds(A + 2 * pair + k, A, stride=128), :] = turned * tc - line * ts
        return carry

    lax.fori_loop(0, A // 2, step, 0, unroll=4)


def spare_lanes(jx):
    return ((iota((1, 128), 1) - (22 - jx)) & 63) < SPARE


def y_third(q, half, jx, out, buf, buf2):
    row = iota((A, A), 0)
    c, s = table64((2 * (row & 31) + (row >> 5)) * iota((A, A), 1))
    table = jnp.concatenate([c, s], axis=1).astype(BF16)
    gap = spare_lanes(jx)

    def step(g, carry):
        lines = []
        for k in range(2):
            at = pl.multiple_of((32 * half + 4 * g + 2 * k) * 128, 256)
            z = buf[pl.ds(at, 256), :].astype(BF16)
            w = dot(table, jnp.concatenate([z[:128], z[128:]], axis=1))
            lines += [w[:, :128], w[:, 128:]]
        for m in range(3):
            line = jnp.where(gap, pltpu.roll(lines[3], 128 - SPARE * (m + 1), 1), lines[m])
            for h in range(2):
                buf2[pl.ds(16 * m + 8 * h + g, NB, stride=48), :] = line[32 * h : 32 * h + 32]
        return carry

    lax.fori_loop(0, 8, step, 0, unroll=2)

    def pack(f, carry):
        out[q, half, f] = buf2[pl.ds(pl.multiple_of(f * 48, 16), 48), :].astype(BF16)
        return carry

    lax.fori_loop(0, NB, pack, 0, unroll=4)


def inverse_table(jx):
    lane = iota((A, 128), 1)
    c, s = table64((iota((A, 128), 0) + jx) * (lane & 63))
    left = lane < A
    whole = jnp.concatenate([jnp.where(left, c, s), jnp.where(left, -s, c)], axis=0)
    gap = ((iota((128, 128), 0) - (22 - jx)) & 63) < SPARE
    whole = jnp.where(gap, 0.0, whole)
    zero = jnp.zeros((128, 128), F32)
    rows = []
    for m in range(3):
        fourth = jnp.where(gap, pltpu.roll(whole, 128 - SPARE * (m + 1), 0), 0.0)
        rows.append(
            jnp.concatenate([whole if k == m else zero for k in range(3)] + [fourth], axis=1)
        )
    return jnp.concatenate(rows, axis=0).astype(BF16)


def x_second(q, half, table, rows, buf):
    lane = iota((8, 128), 1)
    turn = sign()

    def step(group, carry):
        lhs = []
        for k in range(4):
            block = rows[q, half, 4 * group + k]
            lhs.append(jnp.concatenate([block[16 * m : 16 * m + 16] for m in range(3)], axis=1))
        u = dot(jnp.concatenate(lhs, axis=0), table)
        for k in range(4):
            k1 = 2 * (4 * group + k) + q
            ts, tc = sincos_int(k1 * (lane & 63), N)
            ts, tc = ts[:1] * turn, tc[:1]
            for m in range(4):
                line = u[16 * k : 16 * k + 16, 128 * m : 128 * m + 128]
                line = line * tc - swap(line) * ts
                for h in range(2):
                    start = (32 * half + m) * 128 + h * A + k1
                    buf[pl.ds(start, 8, stride=512), :] = line[8 * h : 8 * h + 8]
        return carry

    lax.fori_loop(0, 8, step, 0, unroll=2)


def tile_table(ids):
    col = iota((NB, 128), 1)
    ids = jnp.broadcast_to(ids, (NB, 128))
    c, s = table64((col & 63) * (ids & 63))
    keep = ((ids >> 6) & 1) == (col >> 6)
    return jnp.concatenate([jnp.where(keep, c, 0.0), jnp.where(keep, s, 0.0)], axis=0).astype(BF16)


def x_third(half, table, out, buf, buf2):
    turn = sign()

    def step(pair, carry):
        at = pl.multiple_of((32 * half + 2 * pair) * 128, 256)
        z = buf[pl.ds(at, 256), :].astype(BF16)
        o = dot(table, jnp.concatenate([z[:128], z[128:]], axis=1))
        for k in range(2):
            line = o[:, 128 * k : 128 * k + 128]
            buf2[pl.ds(2 * pair + k, NB, stride=32), :] = line[:32] - swap(line[32:]) * turn
        return carry

    lax.fori_loop(0, 16, step, 0, unroll=4)
    for p in range(NS):
        out[half, p] = buf2[128 * p : 128 * p + 128, :].astype(BF16)


def own_tiles(band, slab, tiles):
    found = jnp.sum(jnp.where((tiles >> 7) == band, tiles, 0), axis=0, keepdims=True)
    column = jnp.where((iota((NB, 256), 1) >> 3) == iota((NB, 256), 0), found, 0)
    column = jnp.sum(column, axis=1, keepdims=True)
    lane = iota((1, 256), 1)
    ids = [jnp.sum(jnp.where((lane >> 3) == 4 * slab + l, found, 0)) for l in range(4)]
    return column, ids


def probe_factors(ids, beams, shifts, out):
    row = iota((8 * 12, 128), 0)
    by = jnp.zeros_like(row)
    bx = jnp.zeros_like(row)
    ab = jnp.zeros(row.shape, F32)
    for j in range(8):
        here = (row >= 12 * j) & (row < 12 * j + 12)
        by = jnp.where(here, beams[0, j], by)
        bx = jnp.where(here, beams[1, j], bx)
        ab = jnp.where(here, shifts[j], ab)
    at = row - 12 * ((row * 43691) >> 19)
    slot = (at * 43691) >> 17
    g = at - 3 * slot
    ident = jnp.zeros_like(row)
    for l in range(4):
        ident = jnp.where(slot == l, ids[l], ident)
    ry = (ident >> 6) * A + A // 2 + g
    rx = (ident & 63) * A + A // 2 + 2 * g
    m = (F * (by * ry + bx * rx)) & (N - 1)
    s, c = sincos(ab + 2.0 * math.pi / N * m.astype(F32))
    out[0] = c
    out[1] = -s


def split_tiles(pot, out):
    for h in range(2):
        for pair in range(32):
            out[32 * h + pair] = pot[A * h : A * h + A, 128 * pair : 128 * pair + 128]


def ring_weights(out):
    ky = iota((32, 128), 0)
    kx = iota((32, 128), 1) & 63
    kx = jnp.where(kx < 32, kx, kx - A)
    radius = ky * ky + kx * kx
    counts = ring_counts()
    width = A // (2 * NDET)
    for b in range(NDET):
        member = (radius >= (width * b) ** 2) & (radius < (width * (b + 1)) ** 2)
        out[b] = jnp.where(member, A * A / (8.0 * counts[b]), 0.0)


def detect(ids, alpha, parts, pot, weights, out, buf):
    left = iota((A, 128), 1) < A
    turn = sign()
    lane = iota((A, 128), 1)
    c, s = table64(iota((A, 128), 0) * (lane & 63))
    along_x = jnp.concatenate(
        [
            jnp.concatenate([jnp.where(left, c, -s), jnp.where(left, s, c)], axis=1),
            jnp.concatenate([jnp.where(left, s, c), jnp.where(left, -c, s)], axis=1),
        ],
        axis=0,
    )
    along_x = (along_x * (1.0 / A)).astype(BF16)
    row = iota((A, A), 0)
    c, s = table64(jnp.where(row < 32, row, 32 - row) * iota((A, A), 1))
    along_y = jnp.concatenate([c, -s], axis=1) * (1.0 / A)
    along_y = jnp.where(iota((A, 128), 0) == 32, 0.0, along_y).astype(BF16)
    probes = []
    for l in range(4):
        ident = ids[l]
        tile = pot[((ident & 127) >> 1)].astype(F32)
        odd = (ident & 1) == 1
        tile = jnp.where(left != odd, tile, swap(tile))
        ps, pc = sincos(tile)
        ps = ps * turn
        sums = [jnp.zeros((A, 128), F32) for _ in range(2 * G)]
        for j in range(8):
            field = jnp.concatenate(
                [parts[h, j, 32 * l : 32 * l + 32, :].astype(F32) for h in range(2)], axis=0
            )
            for g in range(G):
                at = 12 * j + G * l + g
                sums[g] = sums[g] + field * alpha[0, at : at + 1, :]
                sums[G + g] = sums[G + g] + field * alpha[1, at : at + 1, :]
        for g in range(G):
            probe = sums[g] - swap(sums[G + g]) * turn
            probes.append((probe * pc - swap(probe) * ps).astype(BF16))
    d = dot(jnp.concatenate(probes, axis=0), along_x).astype(BF16)
    images = [d[A * n : A * n + A] for n in range(4 * G)]
    images = [jnp.concatenate([image[:, :128], image[:, 128:]], axis=0) for image in images]
    value = dot(along_y, jnp.concatenate(images, axis=1))
    for n in range(4 * G):
        image = value[:, 128 * n : 128 * n + 128]
        power = image * image
        power = power[:32] + power[32:]
        first = (n // G) * A + (n % G) * NDET
        for b in range(NDET):
            buf[first + b : first + b + 1, :] = jnp.sum(power * weights[b], axis=0, keepdims=True)
    total = lax.dot_general(
        jnp.ones((8, 128), F32),
        buf[0:256, :],
        (((1,), (1,)), ((), ())),
        precision=lax.Precision.HIGHEST,
        preferred_element_type=F32,
    )
    for l in range(4):
        block = total[:, 128 * (l // 2) : 128 * (l // 2) + 128]
        out[l] = (swap(block) if l % 2 else block)[:1]


def kernel(
    beams,
    shifts,
    counts,
    tiles,
    pot1_hbm,
    pot2_hbm,
    out,
    pot1,
    pot2,
    buf,
    buf2,
    buf3,
    pairs,
    fresnel,
    twist,
    msg1,
    rows1,
    cols,
    msg2,
    rows2,
    msg3,
    parts,
    alpha,
    weights,
    res,
    sums,
    load,
    send1,
    recv1,
    sendg,
    recvg,
    send2,
    recv2,
    send3,
    recv3,
    send4,
    recv4,
):
    band = lax.axis_index("beam")
    slab = lax.axis_index("slab")
    jy = beams[0, slab]
    jx = beams[1, slab]
    loads = [
        pltpu.make_async_copy(
            pot1_hbm.at[pl.ds(pl.multiple_of(A * h + 16 * (slab >> 1), 16), 16), :],
            pot1.at[h],
            load.at[h],
        )
        for h in range(2)
    ]
    loads.append(pltpu.make_async_copy(pot2_hbm, pot2, load.at[2]))
    for copy in loads:
        copy.start()
    barrier = pltpu.get_barrier_semaphore()

    def greet(target):
        pl.semaphore_signal(
            barrier, inc=1, device_id=target, device_id_type=pl.DeviceIdType.MESH
        )

    def greet_beam(k, carry):
        greet({"beam": (band + k) & (NB - 1), "slab": slab})
        return carry

    lax.fori_loop(1, NB, greet_beam, 0)

    def greet_slab(k, carry):
        greet({"beam": band, "slab": (slab + k) & (NS - 1)})
        return carry

    lax.fori_loop(1, NS, greet_slab, 0)
    home = band >> 2

    def greet_home(k, carry):
        greet({"beam": (band + k) & (NB - 1), "slab": home})
        return carry

    @pl.when(home != slab)
    def _():
        lax.fori_loop(1, NB, greet_home, 0)

    loads[0].wait()
    loads[1].wait()
    x_forward(slab, pot1, msg1, buf)
    extra = 4 * (NS - 1) - jnp.where(home == slab, NS - 1, 0)
    pl.semaphore_wait(barrier, NB - 1 + NS - 1 + extra)

    def exchange1(q, k):
        target = (band + k) & (NB - 1)
        return remote(
            msg1.at[q, target], rows1.at[q, band], send1.at[q], recv1.at[q],
            {"beam": target, "slab": slab},
        )

    def all_of(ref, sem):
        return pltpu.make_async_copy(ref, ref, sem)

    for q in range(2):
        lax.fori_loop(1, NB, lambda k, c: (exchange1(q, k).start(), c)[1], 0)
    for q in range(2):
        rows1[q, band] = msg1[q, band]
    tables(jx, band, fresnel, twist)
    loads[2].wait()
    split_tiles(pot2, pairs)
    wanted, ids = own_tiles(band, slab, tiles[...])
    tile_tab = tile_table(wanted)
    probe_factors(ids, beams, shifts, alpha)
    ring_weights(weights)
    forward = forward_table(jy)
    inverse = inverse_table(jx)

    right = (slab + 2) & (NS - 1)
    left = (slab + 6) & (NS - 1)
    far = (slab + 4) & (NS - 1)
    partner = slab ^ 1

    def gather(source, q, kind, target):
        view = cols.at[q, source]
        return remote(
            view, view, sendg.at[kind, q], recvg.at[source, q], {"beam": band, "slab": target}
        )

    for q in range(2):
        all_of(rows1.at[q, pl.ds(0, NB - 1)], recv1.at[q]).wait()
        for f in range(NB):
            buf[16 * f : 16 * f + 16, :] = rows1[q, f].astype(F32)
        y_first(slab, cols.at[q, slab], buf, buf2)
        for kind, target in enumerate((right, left, far, partner)):
            gather(slab, q, kind, target).start()

    def near(q):
        for kind, source in enumerate((left, right, far)):
            gather(source, q, 0, source).wait_recv()
            gather(source, q, 4 + kind, partner).start()

    def across(q):
        for source in (partner, left ^ 1, right ^ 1, far ^ 1):
            gather(source, q, 0, partner).wait_recv()

    def exchange2(q, half, k):
        target = (band + k) & (NB - 1)
        return remote(
            msg2.at[q, half, target], rows2.at[q, half, band],
            send2.at[2 * q + half], recv2.at[2 * q + half],
            {"beam": target, "slab": slab},
        )

    def send_rows(q, half):
        y_third(q, half, jx, msg2, buf, buf2)
        lax.fori_loop(1, NB, lambda k, z: (exchange2(q, half, k).start(), z)[1], 0)
        rows2[q, half, band] = msg2[q, half, band]

    near(0)
    across(0)
    y_second(0, forward, cols, fresnel, twist, buf)
    near(1)
    send_rows(0, 0)
    send_rows(0, 1)
    across(1)
    y_second(1, forward, cols, fresnel, twist, buf)
    send_rows(1, 0)
    send_rows(1, 1)

    def exchange3(half, k):
        target = (slab + k) & (NS - 1)
        return remote(
            msg3.at[half, target], parts.at[half, slab],
            send3.at[half], recv3.at[half],
            {"beam": band, "slab": target},
        )

    for q in range(2):
        for half in range(2):
            all_of(rows2.at[q, half, pl.ds(0, NB - 1)], recv2.at[2 * q + half]).wait()
            x_second(q, half, inverse, rows2, buf3)
            if q == 1:
                x_third(half, tile_tab, msg3, buf3, buf2)
                lax.fori_loop(1, NS, lambda k, z: (exchange3(half, k).start(), z)[1], 0)
                parts[half, slab] = msg3[half, slab]
    for half in range(2):
        all_of(parts.at[half, pl.ds(0, NS - 1)], recv3.at[half]).wait()
    detect(ids, alpha, parts, pairs, weights, res, buf)

    def exchange4(l, p):
        return remote(
            res.at[l], sums.at[band], send4.at[0], recv4.at[0],
            {"beam": 4 * slab + l, "slab": p},
        )

    for l in range(4):

        def body(p, carry):
            @pl.when((4 * slab + l != band) | (p != slab))
            def _():
                exchange4(l, p).start()

            return carry

        lax.fori_loop(0, NS, body, 0)

    @pl.when(home == slab)
    def _():
        sums[band] = res[band & 3]
        all_of(sums.at[pl.ds(0, NB - 1)], recv4.at[0]).wait()

    @pl.when(home != slab)
    def _():
        all_of(sums, recv4.at[0]).wait()

    block = band * NS + slab
    mine = jnp.where(iota((4, 256), 1) == block, tiles[...], 0)
    slot = iota((4, 256), 0)
    for k in range(4):
        row = sums[jnp.sum(jnp.where(slot == k, mine, 0)) >> 7]
        row = jnp.where(k < counts[block], row, 0.0)
        for g in range(G):
            out[0, g, k : k + 1, :] = row[:, NDET * g : NDET * g + NDET]

    for q in range(2):
        all_of(msg1.at[q, pl.ds(0, NB - 1)], send1.at[q]).wait()
        for kind in range(7):
            all_of(cols.at[q, 0], sendg.at[kind, q]).wait()
        for half in range(2):
            all_of(msg2.at[q, half, pl.ds(0, NB - 1)], send2.at[2 * q + half]).wait()
    for half in range(2):
        all_of(msg3.at[half, pl.ds(0, NS - 1)], send3.at[half]).wait()

    @pl.when(home == slab)
    def _():
        all_of(sums.at[pl.ds(0, NB - 1)], send4.at[0]).wait()

    @pl.when(home != slab)
    def _():
        all_of(sums, send4.at[0]).wait()


def shards(pot_first, pot_second, beam_index, aberration, tile_table, tile_count):
    args = (beam_index.T, aberration, tile_count, tile_table.T, pot_first, pot_second)
    spaces = [pltpu.SMEM] * 3 + [pltpu.VMEM] + [pltpu.HBM] * 2
    dma = pltpu.SemaphoreType.DMA
    sums = pl.pallas_call(
        kernel,
        out_shape=jax.ShapeDtypeStruct((1, G, 4, NDET), F32),
        in_specs=[pl.BlockSpec(memory_space=space) for space in spaces],
        out_specs=pl.BlockSpec(memory_space=pltpu.VMEM),
        scratch_shapes=[
            pltpu.VMEM((2, 16, N), BF16),
            pltpu.VMEM((128, N), BF16),
            pltpu.VMEM((A * 128, 128), F32),
            pltpu.VMEM((1536, 128), F32),
            pltpu.VMEM((A * 128, 128), F32),
            pltpu.VMEM((64, A, 128), BF16),
            pltpu.VMEM((2, A, 2 * KY, 128), F32),
            pltpu.VMEM((A, 128, 128), F32),
            pltpu.VMEM((2, NB, 16, 128), BF16),
            pltpu.VMEM((2, NB, 16, 128), BF16),
            pltpu.VMEM((2, NS, 512, 128), BF16),
            pltpu.VMEM((2, 2, NB, 48, 128), BF16),
            pltpu.VMEM((2, 2, NB, 48, 128), BF16),
            pltpu.VMEM((2, NS, 128, 128), BF16),
            pltpu.VMEM((2, NS, 128, 128), BF16),
            pltpu.VMEM((2, 96, 128), F32),
            pltpu.VMEM((NDET, 32, 128), F32),
            pltpu.VMEM((4, 1, 128), F32),
            pltpu.VMEM((NB, 1, 128), F32),
            dma((3,)),
            dma((2,)),
            dma((2,)),
            dma((7, 2)),
            dma((NS, 2)),
            dma((4,)),
            dma((4,)),
            dma((2,)),
            dma((2,)),
            dma((1,)),
            dma((1,)),
        ],
        compiler_params=pltpu.CompilerParams(
            vmem_limit_bytes=50 * 1024 * 1024, collective_id=0, has_side_effects=True
        ),
    )(*args)
    return sums.transpose(0, 2, 1, 3)


def solution(mesh):
    return jax.shard_map(
        shards,
        mesh=mesh,
        in_specs=(P("beam", None), P("beam", None), P(), P(), P(), P()),
        out_specs=P(("beam", "slab"), None, None, None),
        check_vma=False,
    )
```

time: 112 us -> 101 us (0.902)
  Pallas kernels: 106 us -> 94.9 us
    pallas_call x1, Pallas kernels: 106 us -> 94.9 us  [shards(): pl.pallas_call(kernel, out_shape=jax.ShapeDtypeStruct((1, G, 4, NDET), F3...]
    unnamed x12 -> x13, local copies, waits for them, and re-layouts: 3.89 us -> 4.42 us
where the time goes in v4:
time: 101 us; the launch traced here: 99.3 us
  Pallas kernels  94.9 us (94%)
  local copies, waits for them, and re-layouts  4.42 us (4%)
    pallas_call x1, Pallas kernels, shards(): pl.pallas_call(kernel, out_shape=jax.ShapeDtypeStruct((1, G, 4, NDET), F3...  94.9 us
    unnamed x13, local copies, waits for them, and re-layouts  4.42 us

profile of v4, /device:TPU:8, one launch (start us, length us, event | category | flops | bytes accessed | tf_op | source)
XLA Modules:
  0.0 99.3 jit_solution(14340677663736367315)
XLA Ops:
  0.0 0.0 copy-start.4
  0.0 0.0 copy-start.3
  0.0 0.0 copy-start.5
  0.0 0.7 copy-done.4
  0.7 0.0 copy-done.3
  0.7 0.0 copy-done.5
  0.7 0.0 copy-start
  0.7 1.2 %copy-done = bf16[128,4096]{1,0:T(8,128)(2,1)S(1)} copy-done((bf16[128,4096]{1,0:T(8,128)(2,1)S(1)}, bf16[128,4096]{1,0:T(8,128)(2,1)}, u32[]{:S(2)}) %copy-start) | copy-done | bytes 1048600
  1.9 0.0 copy-start.1
  1.9 1.2 %copy-done.1 = bf16[128,4096]{1,0:T(8,128)(2,1)S(1)} copy-done((bf16[128,4096]{1,0:T(8,128)(2,1)S(1)}, bf16[128,4096]{1,0:T(8,128)(2,1)}, u32[]{:S(2)}) %copy-start.1) | copy-done | bytes 1048600
  3.1 0.0 copy-start.2
  3.2 0.7 copy-done.2
  3.8 94.9 %shard_map.64 = f32[1,3,4,16]{3,2,1,0:T(4,128)S(1)} custom-call(s32[2,8]{1,0:T(2,128)S(1)} %bitcast.5, f32[8]{0:T(128)S(1)} %copy-done.5, s32[256]{0:T(256)S(1)} %copy-done.4, s32[4,256]{1,0:T(4,128)S(1)} %bitcast.4, bf16[128,4096]{1,0:T(8,128)(2,1)S(1)} %copy-done, bf16[128,4096]{1,0:T(8,128)(2,1)S(1)} %copy-done.1), custom_call_target="tpu_custom_call" | custom-call | tf_op jit(solution)/shard_map/pallas_call | solution.py:703
  98.7 0.6 copy.8
Async XLA Ops:
  0.0 0.7 copy-start.4
  0.0 0.7 copy-start.3
  0.0 0.7 copy-start.5
  0.7 1.2 %copy-start = (bf16[128,4096]{1,0:T(8,128)(2,1)S(1)}, bf16[128,4096]{1,0:T(8,128)(2,1)}, u32[]{:S(2)}) copy-start(bf16[128,4096]{1,0:T(8,128)(2,1)} %pot1_hbm.1) | copy-start | bytes 3145732
  1.9 1.2 %copy-start.1 = (bf16[128,4096]{1,0:T(8,128)(2,1)S(1)}, bf16[128,4096]{1,0:T(8,128)(2,1)}, u32[]{:S(2)}) copy-start(bf16[128,4096]{1,0:T(8,128)(2,1)} %pot2_hbm.1) | copy-start | bytes 3145732
  3.1 0.7 copy-start.2

commit v5 on v4

--- a/solution.py
+++ b/solution.py
@@ -228,25 +228,31 @@
         [jnp.concatenate([c, s], axis=1), jnp.concatenate([-s, c], axis=1)], axis=0
     ).astype(BF16)
 
-    def step(pair, carry):
-        at = pl.multiple_of(pair * 16, 16)
-        x = jnp.concatenate([cols[q, p, pl.ds(at, 16), :] for p in range(NS)], axis=0)
-        g = dot(forward, jnp.concatenate([x, swap(x) * -turn], axis=0))
+    def step(group, carry):
+        wide = []
+        for m in range(8):
+            at = pl.multiple_of(group * 128 + 16 * m, 16)
+            x = jnp.concatenate([cols[q, p, pl.ds(at, 16), :] for p in range(NS)], axis=0)
+            wide.append(jnp.concatenate([x, swap(x) * -turn], axis=0))
+        wide = dot(forward, jnp.concatenate(wide, axis=1))
         v = []
-        for k in range(2):
-            line, turned = g[96 * k : 96 * k + KY], g[96 * k + KY : 96 * k + 96]
-            hc, hs = fresnel[q, 2 * pair + k, :KY, :], fresnel[q, 2 * pair + k, KY:, :]
+        for k in range(16):
+            g = wide[96 * (k % 2) : 96 * (k % 2) + 96, 128 * (k // 2) : 128 * (k // 2) + 128]
+            line, turned = g[:KY], g[KY:]
+            k1 = 16 * group + k
+            hc, hs = fresnel[q, k1, :KY, :], fresnel[q, k1, KY:, :]
             both = [line * hc - turned * hs, turned * hc + line * hs]
             v.append(jnp.concatenate(both, axis=0).astype(BF16))
         u = dot(back, jnp.concatenate(v, axis=1))
-        for k in range(2):
+        for k in range(16):
             line, turned = u[:A, 128 * k : 128 * k + 128], u[A:, 128 * k : 128 * k + 128]
-            tc, ts = twist[2 * pair + k, :A, :], twist[2 * pair + k, A:, :]
-            buf[pl.ds(2 * pair + k, A, stride=128), :] = line * tc + turned * ts
-            buf[pl.ds(A + 2 * pair + k, A, stride=128), :] = turned * tc - line * ts
+            k1 = 16 * group + k
+            tc, ts = twist[k1, :A, :], twist[k1, A:, :]
+            buf[pl.ds(k1, A, stride=128), :] = line * tc + turned * ts
+            buf[pl.ds(A + k1, A, stride=128), :] = turned * tc - line * ts
         return carry
 
-    lax.fori_loop(0, A // 2, step, 0, unroll=4)
+    lax.fori_loop(0, 4, step, 0, unroll=2)
 
 
 def spare_lanes(jx):
@@ -259,20 +265,17 @@
     table = jnp.concatenate([c, s], axis=1).astype(BF16)
     gap = spare_lanes(jx)
 
-    def step(g, carry):
-        lines = []
-        for k in range(2):
-            at = pl.multiple_of((32 * half + 4 * g + 2 * k) * 128, 256)
-            z = buf[pl.ds(at, 256), :].astype(BF16)
-            w = dot(table, jnp.concatenate([z[:128], z[128:]], axis=1))
-            lines += [w[:, :128], w[:, 128:]]
+    z = []
+    for b in range(32):
+        at = (32 * half + b) * 128
+        z.append(buf[at : at + 128, :].astype(BF16))
+    w = dot(table, jnp.concatenate(z, axis=1))
+    for g in range(8):
+        lines = [w[:, 128 * (4 * g + m) : 128 * (4 * g + m) + 128] for m in range(4)]
         for m in range(3):
             line = jnp.where(gap, pltpu.roll(lines[3], 128 - SPARE * (m + 1), 1), lines[m])
             for h in range(2):
                 buf2[pl.ds(16 * m + 8 * h + g, NB, stride=48), :] = line[32 * h : 32 * h + 32]
-        return carry
-
-    lax.fori_loop(0, 8, step, 0, unroll=2)
 
     def pack(f, carry):
         out[q, half, f] = buf2[pl.ds(pl.multiple_of(f * 48, 16), 48), :].astype(BF16)
@@ -302,25 +305,21 @@
     lane = iota((8, 128), 1)
     turn = sign()
 
-    def step(group, carry):
-        lhs = []
-        for k in range(4):
-            block = rows[q, half, 4 * group + k]
-            lhs.append(jnp.concatenate([block[16 * m : 16 * m + 16] for m in range(3)], axis=1))
-        u = dot(jnp.concatenate(lhs, axis=0), table)
-        for k in range(4):
-            k1 = 2 * (4 * group + k) + q
-            ts, tc = sincos_int(k1 * (lane & 63), N)
-            ts, tc = ts[:1] * turn, tc[:1]
-            for m in range(4):
-                line = u[16 * k : 16 * k + 16, 128 * m : 128 * m + 128]
-                line = line * tc - swap(line) * ts
-                for h in range(2):
-                    start = (32 * half + m) * 128 + h * A + k1
-                    buf[pl.ds(start, 8, stride=512), :] = line[8 * h : 8 * h + 8]
-        return carry
-
-    lax.fori_loop(0, 8, step, 0, unroll=2)
+    lhs = []
+    for f in range(NB):
+        block = rows[q, half, f]
+        lhs.append(jnp.concatenate([block[16 * m : 16 * m + 16] for m in range(3)], axis=1))
+    u = dot(jnp.concatenate(lhs, axis=0), table)
+    for f in range(NB):
+        k1 = 2 * f + q
+        ts, tc = sincos_int(k1 * (lane & 63), N)
+        ts, tc = ts[:1] * turn, tc[:1]
+        for m in range(4):
+            line = u[16 * f : 16 * f + 16, 128 * m : 128 * m + 128]
+            line = line * tc - swap(line) * ts
+            for h in range(2):
+                start = (32 * half + m) * 128 + h * A + k1
+                buf[pl.ds(start, 8, stride=512), :] = line[8 * h : 8 * h + 8]
 
 
 def tile_table(ids):
@@ -334,16 +333,14 @@
 def x_third(half, table, out, buf, buf2):
     turn = sign()
 
-    def step(pair, carry):
-        at = pl.multiple_of((32 * half + 2 * pair) * 128, 256)
-        z = buf[pl.ds(at, 256), :].astype(BF16)
-        o = dot(table, jnp.concatenate([z[:128], z[128:]], axis=1))
-        for k in range(2):
-            line = o[:, 128 * k : 128 * k + 128]
-            buf2[pl.ds(2 * pair + k, NB, stride=32), :] = line[:32] - swap(line[32:]) * turn
-        return carry
-
-    lax.fori_loop(0, 16, step, 0, unroll=4)
+    z = []
+    for y in range(32):
+        at = (32 * half + y) * 128
+        z.append(buf[at : at + 128, :].astype(BF16))
+    o = dot(table, jnp.concatenate(z, axis=1))
+    for y in range(32):
+        line = o[:, 128 * y : 128 * y + 128]
+        buf2[pl.ds(y, NB, stride=32), :] = line[:32] - swap(line[32:]) * turn
     for p in range(NS):
         out[half, p] = buf2[128 * p : 128 * p + 128, :].astype(BF16)
 
@@ -582,12 +579,14 @@
             view, view, sendg.at[kind, q], recvg.at[source, q], {"beam": band, "slab": target}
         )
 
-    for q in range(2):
+    def first(q):
         all_of(rows1.at[q, pl.ds(0, NB - 1)], recv1.at[q]).wait()
         for f in range(NB):
             buf[16 * f : 16 * f + 16, :] = rows1[q, f].astype(F32)
         y_first(slab, cols.at[q, slab], buf, buf2)
-        for kind, target in enumerate((right, left, far, partner)):
+
+    def spread(q):
+        for kind, target in enumerate((far, left, right, partner)):
             gather(slab, q, kind, target).start()
 
     def near(q):
@@ -612,7 +611,11 @@
         lax.fori_loop(1, NB, lambda k, z: (exchange2(q, half, k).start(), z)[1], 0)
         rows2[q, half, band] = msg2[q, half, band]
 
+    first(0)
+    spread(0)
+    first(1)
     near(0)
+    spread(1)
     across(0)
     y_second(0, forward, cols, fresnel, twist, buf)
     near(1)

time: 101 us -> 94.8 us (0.939)
  Pallas kernels: 94.9 us -> 88.7 us
    pallas_call x1, Pallas kernels: 94.9 us -> 88.7 us  [shards(): pl.pallas_call(kernel, out_shape=jax.ShapeDtypeStruct((1, G, 4, NDET), F3...]
where the time goes in v5:
time: 94.8 us; the launch traced here: 93.2 us
  Pallas kernels  88.7 us (94%)
  local copies, waits for them, and re-layouts  4.42 us (5%)
    pallas_call x1, Pallas kernels, shards(): pl.pallas_call(kernel, out_shape=jax.ShapeDtypeStruct((1, G, 4, NDET), F3...  88.7 us
    unnamed x13, local copies, waits for them, and re-layouts  4.42 us

profile of v5, /device:TPU:8, one launch (start us, length us, event | category | flops | bytes accessed | tf_op | source)
XLA Modules:
  0.0 93.2 jit_solution(892411432393580033)
XLA Ops:
  0.0 0.0 copy-start.4
  0.0 0.0 copy-start.3
  0.0 0.0 copy-start.5
  0.0 0.7 copy-done.4
  0.7 0.0 copy-done.3
  0.7 0.0 copy-done.5
  0.7 0.0 copy-start
  0.7 1.2 %copy-done = bf16[128,4096]{1,0:T(8,128)(2,1)S(1)} copy-done((bf16[128,4096]{1,0:T(8,128)(2,1)S(1)}, bf16[128,4096]{1,0:T(8,128)(2,1)}, u32[]{:S(2)}) %copy-start) | copy-done | bytes 1048600
  1.9 0.0 copy-start.1
  1.9 1.2 %copy-done.1 = bf16[128,4096]{1,0:T(8,128)(2,1)S(1)} copy-done((bf16[128,4096]{1,0:T(8,128)(2,1)S(1)}, bf16[128,4096]{1,0:T(8,128)(2,1)}, u32[]{:S(2)}) %copy-start.1) | copy-done | bytes 1048600
  3.1 0.0 copy-start.2
  3.2 0.7 copy-done.2
  3.8 88.7 %shard_map.64 = f32[1,3,4,16]{3,2,1,0:T(4,128)S(1)} custom-call(s32[2,8]{1,0:T(2,128)S(1)} %bitcast.5, f32[8]{0:T(128)S(1)} %copy-done.5, s32[256]{0:T(256)S(1)} %copy-done.4, s32[4,256]{1,0:T(4,128)S(1)} %bitcast.4, bf16[128,4096]{1,0:T(8,128)(2,1)S(1)} %copy-done, bf16[128,4096]{1,0:T(8,128)(2,1)S(1)} %copy-done.1), custom_call_target="tpu_custom_call" | custom-call | tf_op jit(solution)/shard_map/pallas_call | solution.py:706
  92.6 0.6 copy.8
Async XLA Ops:
  0.0 0.7 copy-start.4
  0.0 0.7 copy-start.3
  0.0 0.7 copy-start.5
  0.7 1.2 %copy-start = (bf16[128,4096]{1,0:T(8,128)(2,1)S(1)}, bf16[128,4096]{1,0:T(8,128)(2,1)}, u32[]{:S(2)}) copy-start(bf16[128,4096]{1,0:T(8,128)(2,1)} %pot1_hbm.1) | copy-start | bytes 3145732
  1.9 1.2 %copy-start.1 = (bf16[128,4096]{1,0:T(8,128)(2,1)S(1)}, bf16[128,4096]{1,0:T(8,128)(2,1)}, u32[]{:S(2)}) copy-start(bf16[128,4096]{1,0:T(8,128)(2,1)} %pot2_hbm.1) | copy-start | bytes 3145732
  3.1 0.7 copy-start.2

commit v6 on v5

--- a/solution.py
+++ b/solution.py
@@ -129,9 +129,15 @@
     return first, second
 
 
-def x_forward(slab, potential, out, buf):
+def x_forward(slab, loads, potential, out, buf):
+    first, second = x_tables()
+    row = iota((A, 128), 0)
+    k1 = 2 * (row & 31) + (row >> 5)
+    ts, tc = sincos_int(k1 * (iota((A, 128), 1) & 63), N)
+    left = left_half()
     odd = (slab & 1) == 1
     for h in range(2):
+        loads[h].wait()
         block = potential[h].astype(F32)
         block = jnp.where(odd, block[8:], block[:8])
         sine, cosine = sincos(block)
@@ -139,31 +145,26 @@
             for p in range(32):
                 start = h * 8 * A + part * 32 + p
                 buf[pl.ds(start, 8, stride=A), :] = wave[:, 128 * p : 128 * p + 128]
-    first, second = x_tables()
-    row = iota((A, 128), 0)
-    k1 = 2 * (row & 31) + (row >> 5)
-    ts, tc = sincos_int(k1 * (iota((A, 128), 1) & 63), N)
-    left = left_half()
     waves = [buf[A * r : A * r + A, :].astype(BF16) for r in range(16)]
+    y = dot(first, jnp.concatenate(waves, axis=1))
+    lines = []
+    for r in range(16):
+        both = y[:, 128 * r : 128 * r + 128]
+        both = jnp.where(left, both[:128], both[128:])
+        lines.append(both + swap(both))
+    pairs = []
     for t in range(8):
-        y = dot(first, jnp.concatenate([waves[2 * t], waves[2 * t + 1]], axis=1))
-        lines = []
-        for k in range(2):
-            both = y[:, 128 * k : 128 * k + 128]
-            both = jnp.where(left, both[:128], both[128:])
-            lines.append(both + swap(both))
-        line = jnp.where(left, lines[0], lines[1])
+        line = jnp.where(left, lines[2 * t], lines[2 * t + 1])
         yr, yi = line[:A], line[A:]
-        z = jnp.concatenate(
-            [(yr * tc + yi * ts).astype(BF16), (yi * tc - yr * ts).astype(BF16)], axis=1
-        )
-        spec = dot(z, second)
-        for k in range(2):
-            r = 2 * t + k
-            for q in range(2):
-                buf[pl.ds(1024 + 512 * q + r, 32, stride=16), :] = spec[
-                    32 * q : 32 * q + 32, 128 * k : 128 * k + 128
-                ]
+        both = [(yr * tc + yi * ts).astype(BF16), (yi * tc - yr * ts).astype(BF16)]
+        pairs.append(jnp.concatenate(both, axis=1))
+    spec = dot(jnp.concatenate(pairs, axis=0), second)
+    for r in range(16):
+        for q in range(2):
+            start = A * (r >> 1) + 32 * q
+            buf[pl.ds(1024 + 512 * q + r, 32, stride=16), :] = spec[
+                start : start + 32, 128 * (r & 1) : 128 * (r & 1) + 128
+            ]
     for q in range(2):
         for f in range(NB):
             start = 1024 + 512 * q + 16 * f
@@ -396,10 +397,38 @@
         out[b] = jnp.where(member, A * A / (8.0 * counts[b]), 0.0)
 
 
-def detect(ids, alpha, parts, pot, weights, out, buf):
-    left = iota((A, 128), 1) < A
+def phases(ids, pot, out):
+    left = left_half()
+    for l in range(4):
+        tile = pot[((ids[l] & 127) >> 1)].astype(F32)
+        odd = (ids[l] & 1) == 1
+        tile = jnp.where(left != odd, tile, swap(tile))
+        s, c = sincos(tile)
+        out[l, 0] = c
+        out[l, 1] = s * sign()
+
+
+def probe_rows(half, alpha, parts, phase, out):
     turn = sign()
+    for l in range(4):
+        sums = [jnp.zeros((32, 128), F32) for _ in range(2 * G)]
+        for j in range(8):
+            field = parts[half, j, 32 * l : 32 * l + 32, :].astype(F32)
+            for g in range(G):
+                at = 12 * j + G * l + g
+                sums[g] = sums[g] + field * alpha[0, at : at + 1, :]
+                sums[G + g] = sums[G + g] + field * alpha[1, at : at + 1, :]
+        pc = phase[l, 0, 32 * half : 32 * half + 32, :]
+        ps = phase[l, 1, 32 * half : 32 * half + 32, :]
+        for g in range(G):
+            probe = sums[g] - swap(sums[G + g]) * turn
+            at = (G * l + g) * A + 32 * half
+            out[at : at + 32, :] = (probe * pc - swap(probe) * ps).astype(BF16)
+
+
+def detector_tables():
     lane = iota((A, 128), 1)
+    left = lane < A
     c, s = table64(iota((A, 128), 0) * (lane & 63))
     along_x = jnp.concatenate(
         [
@@ -413,27 +442,11 @@
     c, s = table64(jnp.where(row < 32, row, 32 - row) * iota((A, A), 1))
     along_y = jnp.concatenate([c, -s], axis=1) * (1.0 / A)
     along_y = jnp.where(iota((A, 128), 0) == 32, 0.0, along_y).astype(BF16)
-    probes = []
-    for l in range(4):
-        ident = ids[l]
-        tile = pot[((ident & 127) >> 1)].astype(F32)
-        odd = (ident & 1) == 1
-        tile = jnp.where(left != odd, tile, swap(tile))
-        ps, pc = sincos(tile)
-        ps = ps * turn
-        sums = [jnp.zeros((A, 128), F32) for _ in range(2 * G)]
-        for j in range(8):
-            field = jnp.concatenate(
-                [parts[h, j, 32 * l : 32 * l + 32, :].astype(F32) for h in range(2)], axis=0
-            )
-            for g in range(G):
-                at = 12 * j + G * l + g
-                sums[g] = sums[g] + field * alpha[0, at : at + 1, :]
-                sums[G + g] = sums[G + g] + field * alpha[1, at : at + 1, :]
-        for g in range(G):
-            probe = sums[g] - swap(sums[G + g]) * turn
-            probes.append((probe * pc - swap(probe) * ps).astype(BF16))
-    d = dot(jnp.concatenate(probes, axis=0), along_x).astype(BF16)
+    return along_x, along_y
+
+
+def detect(along_x, along_y, probes, weights, out, buf):
+    d = dot(probes[...], along_x).astype(BF16)
     images = [d[A * n : A * n + A] for n in range(4 * G)]
     images = [jnp.concatenate([image[:, :128], image[:, 128:]], axis=0) for image in images]
     value = dot(along_y, jnp.concatenate(images, axis=1))
@@ -481,6 +494,8 @@
     parts,
     alpha,
     weights,
+    phase,
+    probes,
     res,
     sums,
     load,
@@ -538,9 +553,7 @@
     def _():
         lax.fori_loop(1, NB, greet_home, 0)
 
-    loads[0].wait()
-    loads[1].wait()
-    x_forward(slab, pot1, msg1, buf)
+    x_forward(slab, loads, pot1, msg1, buf)
     extra = 4 * (NS - 1) - jnp.where(home == slab, NS - 1, 0)
     pl.semaphore_wait(barrier, NB - 1 + NS - 1 + extra)
 
@@ -558,15 +571,7 @@
         lax.fori_loop(1, NB, lambda k, c: (exchange1(q, k).start(), c)[1], 0)
     for q in range(2):
         rows1[q, band] = msg1[q, band]
-    tables(jx, band, fresnel, twist)
-    loads[2].wait()
-    split_tiles(pot2, pairs)
-    wanted, ids = own_tiles(band, slab, tiles[...])
-    tile_tab = tile_table(wanted)
-    probe_factors(ids, beams, shifts, alpha)
-    ring_weights(weights)
     forward = forward_table(jy)
-    inverse = inverse_table(jx)
 
     right = (slab + 2) & (NS - 1)
     left = (slab + 6) & (NS - 1)
@@ -614,17 +619,31 @@
     first(0)
     spread(0)
     first(1)
+    tables(jx, band, fresnel, twist)
     near(0)
     spread(1)
     across(0)
     y_second(0, forward, cols, fresnel, twist, buf)
+    send_rows(0, 0)
     near(1)
-    send_rows(0, 0)
     send_rows(0, 1)
     across(1)
     y_second(1, forward, cols, fresnel, twist, buf)
     send_rows(1, 0)
     send_rows(1, 1)
+    loads[2].wait()
+    split_tiles(pot2, pairs)
+    wanted, ids = own_tiles(band, slab, tiles[...])
+    tile_tab = tile_table(wanted)
+    probe_factors(ids, beams, shifts, alpha)
+    ring_weights(weights)
+    phases(ids, pairs, phase)
+    along_x, along_y = detector_tables()
+    inverse = inverse_table(jx)
+    block = band * NS + slab
+    mine = jnp.where(iota((4, 256), 1) == block, tiles[...], 0)
+    slot = iota((4, 256), 0)
+    bands = [jnp.sum(jnp.where(slot == k, mine, 0)) >> 7 for k in range(4)]
 
     def exchange3(half, k):
         target = (slab + k) & (NS - 1)
@@ -640,11 +659,13 @@
             x_second(q, half, inverse, rows2, buf3)
             if q == 1:
                 x_third(half, tile_tab, msg3, buf3, buf2)
-                lax.fori_loop(1, NS, lambda k, z: (exchange3(half, k).start(), z)[1], 0)
+                for k in range(1, NS):
+                    exchange3(half, k).start()
                 parts[half, slab] = msg3[half, slab]
     for half in range(2):
         all_of(parts.at[half, pl.ds(0, NS - 1)], recv3.at[half]).wait()
-    detect(ids, alpha, parts, pairs, weights, res, buf)
+        probe_rows(half, alpha, parts, phase, probes)
+    detect(along_x, along_y, probes, weights, res, buf)
 
     def exchange4(l, p):
         return remote(
@@ -653,15 +674,12 @@
         )
 
     for l in range(4):
-
-        def body(p, carry):
-            @pl.when((4 * slab + l != band) | (p != slab))
-            def _():
-                exchange4(l, p).start()
-
-            return carry
-
-        lax.fori_loop(0, NS, body, 0)
+        for k in range(1, NS):
+            exchange4(l, (slab + k) & (NS - 1)).start()
+
+        @pl.when(4 * slab + l != band)
+        def _():
+            exchange4(l, slab).start()
 
     @pl.when(home == slab)
     def _():
@@ -672,11 +690,8 @@
     def _():
         all_of(sums, recv4.at[0]).wait()
 
-    block = band * NS + slab
-    mine = jnp.where(iota((4, 256), 1) == block, tiles[...], 0)
-    slot = iota((4, 256), 0)
     for k in range(4):
-        row = sums[jnp.sum(jnp.where(slot == k, mine, 0)) >> 7]
+        row = sums[bands[k]]
         row = jnp.where(k < counts[block], row, 0.0)
         for g in range(G):
             out[0, g, k : k + 1, :] = row[:, NDET * g : NDET * g + NDET]
@@ -726,6 +741,8 @@
             pltpu.VMEM((2, NS, 128, 128), BF16),
             pltpu.VMEM((2, 96, 128), F32),
             pltpu.VMEM((NDET, 32, 128), F32),
+            pltpu.VMEM((4, 2, A, 128), F32),
+            pltpu.VMEM((4 * G * A, 128), BF16),
             pltpu.VMEM((4, 1, 128), F32),
             pltpu.VMEM((NB, 1, 128), F32),
             dma((3,)),
@@ -741,7 +758,7 @@
             dma((1,)),
         ],
         compiler_params=pltpu.CompilerParams(
-            vmem_limit_bytes=50 * 1024 * 1024, collective_id=0, has_side_effects=True
+            vmem_limit_bytes=64 * 1024 * 1024, collective_id=0, has_side_effects=True
         ),
     )(*args)
     return sums.transpose(0, 2, 1, 3)

time: 94.8 us -> 91.6 us (0.966)
  local copies, waits for them, and re-layouts: 4.42 us -> 1.29 us
    unnamed x13 -> x1, local copies, waits for them, and re-layouts: 4.42 us -> 1.29 us
where the time goes in v6:
time: 91.6 us; the launch traced here: 89.9 us
  Pallas kernels  88.6 us (97%)
  local copies, waits for them, and re-layouts  1.29 us (1%)
    pallas_call x1, Pallas kernels, shards(): pl.pallas_call(kernel, out_shape=jax.ShapeDtypeStruct((1, G, 4, NDET), F3...  88.6 us

profile of v6, /device:TPU:8, one launch (start us, length us, event | category | flops | bytes accessed | tf_op | source)
XLA Modules:
  0.0 89.9 jit_solution(8138556377705198603)
XLA Ops:
  0.0 88.6 %shard_map.64 = f32[1,3,4,16]{3,2,1,0:T(4,128)} custom-call(s32[2,8]{1,0:T(2,128)} %bitcast.5, f32[8]{0:T(128)} %shifts.1, s32[256]{0:T(256)} %counts.1, s32[4,256]{1,0:T(4,128)} %bitcast.4, bf16[128,4096]{1,0:T(8,128)(2,1)} %pot1_hbm.1, bf16[128,4096]{1,0:T(8,128)(2,1)} %pot2_hbm.1), custom_call_target="tpu_custom_call" | custom-call | tf_op jit(solution)/shard_map/pallas_call | solution.py:721
  88.6 1.3 %copy.8 = f32[1,4,3,16]{3,1,2,0:T(4,128)} copy(f32[1,4,3,16]{3,1,2,0:T(4,128)} %bitcast.3) | data formatting | bytes 1536

commit v7 on v6

--- a/solution.py
+++ b/solution.py
@@ -171,26 +171,48 @@
             out[q, f] = buf[start : start + 16, :].astype(BF16)
 
 
-def tables(jx, band, fresnel, twist):
+def fresnel_table(jx, band, out):
     lane = iota((KY, 128), 1)
     ky0 = A * (iota((KY, 128), 0) - LOW)
+    square_x = []
+    for q in range(2):
+        fx = ((2 * band + q + A * ((lane & 63) + jx) + N // 2) & (N - 1)) - N // 2
+        square_x.append(fx * fx)
+    ec, es = math.cos(2.0 * math.pi / N), math.sin(2.0 * math.pi / N)
+
+    def step(block, carry):
+        fy = ky0 + 8 * block
+        total = [square + fy * fy for square in square_x]
+        factor = [sincos_int(value, 2 * N) for value in total]
+        ds, dc = sincos_int(2 * fy + 1, 2 * N)
+        for k in range(8):
+            for q in range(2):
+                hs, hc = factor[q]
+                inside = total[q] <= (N // 3) ** 2
+                out[q, 8 * block + k, :KY, :] = jnp.where(inside, hc, 0.0)
+                out[q, 8 * block + k, KY:, :] = jnp.where(inside, hs, 0.0)
+                total[q] = total[q] + 2 * fy + 1
+                factor[q] = (hs * dc + hc * ds, hc * dc - hs * ds)
+            ds, dc = ds * ec + dc * es, dc * ec - ds * es
+            fy = fy + 1
+        return carry
+
+    lax.fori_loop(0, 8, step, 0)
+
+
+def twist_table(out):
     b_row = iota((A, 128), 0)
-
-    def step(k1, carry):
-        fy = ky0 + k1
-        for q in range(2):
-            fx = ((2 * band + q + A * ((lane & 63) + jx) + N // 2) & (N - 1)) - N // 2
-            total = fx * fx + fy * fy
-            hs, hc = sincos_int(total, 2 * N)
-            inside = total <= (N // 3) ** 2
-            fresnel[q, k1, :KY, :] = jnp.where(inside, hc, 0.0)
-            fresnel[q, k1, KY:, :] = jnp.where(inside, hs, 0.0)
-        ts, tc = sincos_int(b_row * k1, N)
-        twist[k1, :A, :] = tc
-        twist[k1, A:, :] = ts
+    rs, rc = sincos_int(b_row, N)
+
+    def step(block, carry):
+        ts, tc = sincos_int(b_row * (8 * block), N)
+        for k in range(8):
+            out[8 * block + k, :A, :] = tc
+            out[8 * block + k, A:, :] = ts
+            ts, tc = ts * rc + tc * rs, tc * rc - ts * rs
         return carry
 
-    lax.fori_loop(0, A, step, 0, unroll=2)
+    lax.fori_loop(0, 8, step, 0)
 
 
 def y_first(slab, out, buf, buf2):
@@ -253,7 +275,7 @@
             buf[pl.ds(A + k1, A, stride=128), :] = turned * tc - line * ts
         return carry
 
-    lax.fori_loop(0, 4, step, 0, unroll=2)
+    lax.fori_loop(0, 4, step, 0, unroll=4)
 
 
 def spare_lanes(jx):
@@ -278,11 +300,8 @@
             for h in range(2):
                 buf2[pl.ds(16 * m + 8 * h + g, NB, stride=48), :] = line[32 * h : 32 * h + 32]
 
-    def pack(f, carry):
-        out[q, half, f] = buf2[pl.ds(pl.multiple_of(f * 48, 16), 48), :].astype(BF16)
-        return carry
-
-    lax.fori_loop(0, NB, pack, 0, unroll=4)
+    for f in range(NB):
+        out[q, half, f] = buf2[48 * f : 48 * f + 48, :].astype(BF16)
 
 
 def inverse_table(jx):
@@ -571,6 +590,7 @@
         lax.fori_loop(1, NB, lambda k, c: (exchange1(q, k).start(), c)[1], 0)
     for q in range(2):
         rows1[q, band] = msg1[q, band]
+    fresnel_table(jx, band, fresnel)
     forward = forward_table(jy)
 
     right = (slab + 2) & (NS - 1)
@@ -619,7 +639,7 @@
     first(0)
     spread(0)
     first(1)
-    tables(jx, band, fresnel, twist)
+    twist_table(twist)
     near(0)
     spread(1)
     across(0)

time: 91.6 us -> 88.5 us (0.966)
  Pallas kernels: 88.6 us -> 85.5 us
    pallas_call x1, Pallas kernels: 88.6 us -> 85.5 us  [shards(): pl.pallas_call(kernel, out_shape=jax.ShapeDtypeStruct((1, G, 4, NDET), F3...]
where the time goes in v7:
time: 88.5 us; the launch traced here: 86.8 us
  Pallas kernels  85.5 us (97%)
  local copies, waits for them, and re-layouts  1.29 us (1%)
    pallas_call x1, Pallas kernels, shards(): pl.pallas_call(kernel, out_shape=jax.ShapeDtypeStruct((1, G, 4, NDET), F3...  85.5 us

profile of v7, /device:TPU:8, one launch (start us, length us, event | category | flops | bytes accessed | tf_op | source)
XLA Modules:
  0.0 86.8 jit_solution(10878717094033781922)
XLA Ops:
  0.0 85.5 %shard_map.64 = f32[1,3,4,16]{3,2,1,0:T(4,128)} custom-call(s32[2,8]{1,0:T(2,128)} %bitcast.5, f32[8]{0:T(128)} %shifts.1, s32[256]{0:T(256)} %counts.1, s32[4,256]{1,0:T(4,128)} %bitcast.4, bf16[128,4096]{1,0:T(8,128)(2,1)} %pot1_hbm.1, bf16[128,4096]{1,0:T(8,128)(2,1)} %pot2_hbm.1), custom_call_target="tpu_custom_call" | custom-call | tf_op jit(solution)/shard_map/pallas_call | solution.py:741
  85.5 1.3 %copy.8 = f32[1,4,3,16]{3,1,2,0:T(4,128)} copy(f32[1,4,3,16]{3,1,2,0:T(4,128)} %bitcast.3) | data formatting | bytes 1536

commit v8 on v7

--- a/solution.py
+++ b/solution.py
@@ -215,17 +215,22 @@
     lax.fori_loop(0, 8, step, 0)
 
 
-def y_first(slab, out, buf, buf2):
+def first_twist(slab, out):
     turn = sign()
-    table = stacked(iota((A, A), 0) * iota((A, A), 1), 1.0 / A)
-    for i in range(0, 8, 2):
-        x = [buf[pl.ds(i + k, A, stride=8), :].astype(BF16) for k in range(2)]
-        y = dot(table, jnp.concatenate(x, axis=1))
-        for k in range(2):
-            line = y[:, 128 * k : 128 * k + 128]
-            line = line[:A] + swap(line[A:]) * turn
-            ts, tc = sincos_int(iota((A, 128), 0) * (8 * slab + i + k), N)
-            buf2[pl.ds(i + k, A, stride=8), :] = line * tc + swap(line) * (ts * turn)
+    for i in range(8):
+        ts, tc = sincos_int(iota((A, 128), 0) * (8 * slab + i), N)
+        out[i, :A, :] = tc
+        out[i, A:, :] = ts * turn
+
+
+def y_first(table, twist, out, buf, buf2):
+    turn = sign()
+    x = [buf[pl.ds(i, A, stride=8), :].astype(BF16) for i in range(8)]
+    y = dot(table, jnp.concatenate(x, axis=1))
+    for i in range(8):
+        line = y[:, 128 * i : 128 * i + 128]
+        line = line[:A] + swap(line[A:]) * turn
+        buf2[pl.ds(i, A, stride=8), :] = line * twist[i, :A, :] + swap(line) * twist[i, A:, :]
     out[...] = buf2[0:512, :].astype(BF16)
 
 
@@ -502,6 +507,7 @@
     buf2,
     buf3,
     pairs,
+    twist1,
     fresnel,
     twist,
     msg1,
@@ -590,6 +596,8 @@
         lax.fori_loop(1, NB, lambda k, c: (exchange1(q, k).start(), c)[1], 0)
     for q in range(2):
         rows1[q, band] = msg1[q, band]
+    first_table = stacked(iota((A, A), 0) * iota((A, A), 1), 1.0 / A)
+    first_twist(slab, twist1)
     fresnel_table(jx, band, fresnel)
     forward = forward_table(jy)
 
@@ -608,7 +616,7 @@
         all_of(rows1.at[q, pl.ds(0, NB - 1)], recv1.at[q]).wait()
         for f in range(NB):
             buf[16 * f : 16 * f + 16, :] = rows1[q, f].astype(F32)
-        y_first(slab, cols.at[q, slab], buf, buf2)
+        y_first(first_table, twist1, cols.at[q, slab], buf, buf2)
 
     def spread(q):
         for kind, target in enumerate((far, left, right, partner)):
@@ -701,21 +709,6 @@
         def _():
             exchange4(l, slab).start()
 
-    @pl.when(home == slab)
-    def _():
-        sums[band] = res[band & 3]
-        all_of(sums.at[pl.ds(0, NB - 1)], recv4.at[0]).wait()
-
-    @pl.when(home != slab)
-    def _():
-        all_of(sums, recv4.at[0]).wait()
-
-    for k in range(4):
-        row = sums[bands[k]]
-        row = jnp.where(k < counts[block], row, 0.0)
-        for g in range(G):
-            out[0, g, k : k + 1, :] = row[:, NDET * g : NDET * g + NDET]
-
     for q in range(2):
         all_of(msg1.at[q, pl.ds(0, NB - 1)], send1.at[q]).wait()
         for kind in range(7):
@@ -724,6 +717,21 @@
             all_of(msg2.at[q, half, pl.ds(0, NB - 1)], send2.at[2 * q + half]).wait()
     for half in range(2):
         all_of(msg3.at[half, pl.ds(0, NS - 1)], send3.at[half]).wait()
+
+    @pl.when(home == slab)
+    def _():
+        sums[band] = res[band & 3]
+        all_of(sums.at[pl.ds(0, NB - 1)], recv4.at[0]).wait()
+
+    @pl.when(home != slab)
+    def _():
+        all_of(sums, recv4.at[0]).wait()
+
+    for k in range(4):
+        row = sums[bands[k]]
+        row = jnp.where(k < counts[block], row, 0.0)
+        for g in range(G):
+            out[0, g, k : k + 1, :] = row[:, NDET * g : NDET * g + NDET]
 
     @pl.when(home == slab)
     def _():
@@ -750,6 +758,7 @@
             pltpu.VMEM((1536, 128), F32),
             pltpu.VMEM((A * 128, 128), F32),
             pltpu.VMEM((64, A, 128), BF16),
+            pltpu.VMEM((8, 128, 128), F32),
             pltpu.VMEM((2, A, 2 * KY, 128), F32),
             pltpu.VMEM((A, 128, 128), F32),
             pltpu.VMEM((2, NB, 16, 128), BF16),

time: 88.5 us -> 88.2 us (level)
  no operation moved by 1% of the time
where the time goes in v8:
time: 88.2 us; the launch traced here: 86.6 us
  Pallas kernels  85.3 us (97%)
  local copies, waits for them, and re-layouts  1.29 us (1%)
    pallas_call x1, Pallas kernels, shards(): pl.pallas_call(kernel, out_shape=jax.ShapeDtypeStruct((1, G, 4, NDET), F3...  85.3 us

profile of v8, /device:TPU:8, one launch (start us, length us, event | category | flops | bytes accessed | tf_op | source)
XLA Modules:
  0.0 86.6 jit_solution(7635972668420215832)
XLA Ops:
  0.0 85.3 %shard_map.64 = f32[1,3,4,16]{3,2,1,0:T(4,128)} custom-call(s32[2,8]{1,0:T(2,128)} %bitcast.5, f32[8]{0:T(128)} %shifts.1, s32[256]{0:T(256)} %counts.1, s32[4,256]{1,0:T(4,128)} %bitcast.4, bf16[128,4096]{1,0:T(8,128)(2,1)} %pot1_hbm.1, bf16[128,4096]{1,0:T(8,128)(2,1)} %pot2_hbm.1), custom_call_target="tpu_custom_call" | custom-call | tf_op jit(solution)/shard_map/pallas_call | solution.py:749
  85.3 1.3 %copy.8 = f32[1,4,3,16]{3,1,2,0:T(4,128)} copy(f32[1,4,3,16]{3,1,2,0:T(4,128)} %bitcast.3) | data formatting | bytes 1536
